TPU v7x, 256 devices: a whole 4x4x8 slice. The times are simulated.
256 devices in a mesh: seq: 8 (over x, core), head: 32 (over y, z).
Axes of the slice: x: 4, y: 4, z: 8, core: 2. Of those that a mesh axis runs over, the one named last changes fastest.
Arguments:
- queries: bfloat16 [32768, 4096], P(('seq', 'head')), may hold values from -4 to 4
- keys: bfloat16 [32768, 1024], P(('seq', 'head')), may hold values from -4 to 4
- values: bfloat16 [32768, 1024], P(('seq', 'head')), may hold values from -6 to 6
- modality: int32 [32768], P(('seq', 'head')), may hold values 0 or 1
- clip_lengths: int32 [128], replicated, may hold values from 1 to 512, 32768 in all
- query_gains: float32 [2, 4096], replicated, may hold values from 0.5 to 5.2
- key_gains: float32 [2, 1024], replicated, may hold values from 0.5 to 5.2
- out_grad: bfloat16 [32768, 4096], P(('seq', 'head')), may hold values from -6 to 6
Outputs:
- attended: bfloat16 [32768, 4096], P(('seq', 'head'))
- query_grad: bfloat16 [32768, 4096], P(('seq', 'head'))
- key_grad: bfloat16 [32768, 1024], P(('seq', 'head'))
- value_grad: bfloat16 [32768, 1024], P(('seq', 'head'))
- query_gain_grad: float32 [2, 4096], replicated
- key_gain_grad: float32 [2, 1024], replicated
Inputs may be any that keep to these rules, and one draw needn't show every extreme that they name: `clip_lengths`: the clips cover the 32768 positions end to end; some clip has exactly 512 positions.
All inputs are finite; a program needn't handle non-finite values. No bound on the sum of `modality` on one device may be relied on, other than what follows from the above.
Results may differ from a plain program's by a relative error of at most 0.025.
The roundings to bfloat16 on the way count: a program that leaves them out, or rounds other values in their place, can miss the bound.
Values may be sent and summed in bfloat16 or wider, within the bound.
No kernel may reach another device: no remote copies, remote signals or barrier semaphores. Data moves between devices by JAX's collectives and lax.ppermute only.
A program may use at most 128 MiB of HBM per device.

v0:
```python
import math

import jax
import jax.numpy as jnp
from jax import lax
from jax.sharding import PartitionSpec as P

HD = 128
MOST = 512


row_block = 512


def from_behind(value, axis, steps):
    count = lax.axis_size(axis)
    first, last = (max(0, -steps), min(count, count - steps))
    return lax.ppermute(value, axis, [(source, source + steps) for source in range(first, last)])


def clip_start(clip_lengths, positions):
    ends = jnp.cumsum(clip_lengths, dtype=jnp.int32)
    begins = ends - clip_lengths
    chosen = jnp.where(
        begins[None, :] <= positions[:, None], begins[None, :], jnp.zeros((), jnp.int32)
    )
    return jnp.max(chosen, axis=1)


def normalize(rows, modality, gains):
    count, width = rows.shape
    shaped = rows.astype(jnp.float32).reshape(count, width // HD, HD)
    factor = lax.rsqrt(jnp.mean(shaped * shaped, axis=2, keepdims=True) + 1e-06)
    unit = shaped * factor
    gain_rows = jnp.where(modality[:, None] == 1, gains[1][None, :], gains[0][None, :]).reshape(
        count, width // HD, HD
    )
    normed = (unit * gain_rows).astype(jnp.bfloat16).reshape(count, width)
    return (normed, unit, factor, gain_rows)


def unnormalize(grad_low, unit, factor, gain_rows, modality):
    count = unit.shape[0]
    shaped = grad_low.astype(jnp.float32).reshape(unit.shape)
    along = shaped * gain_rows
    back = factor * (along - unit * jnp.mean(along * unit, axis=2, keepdims=True))
    term = (shaped * unit).reshape(count, -1)
    choose = (modality[:, None] == jnp.arange(2, dtype=jnp.int32)[None, :]).astype(jnp.float32)
    gain_part = jnp.einsum("rm,rc->mc", choose, term, precision=lax.Precision.HIGHEST)
    return (back.reshape(count, -1).astype(jnp.bfloat16), gain_part)


def spread_heads(rows, kv_heads, repeat):
    count = rows.shape[0]
    return jnp.broadcast_to(
        rows.reshape(count, kv_heads, 1, HD), (count, kv_heads, repeat, HD)
    ).reshape(count, kv_heads * repeat, HD)


def fold_heads(rows, kv_heads, repeat):
    count = rows.shape[0]
    return jnp.sum(rows.reshape(count, kv_heads, repeat, HD), axis=2)


def attend(query_norm, key_ext, value_ext, grad_rows, first, starts, block):
    rows = query_norm.shape[0]
    reach = key_ext.shape[0] - rows
    span = block + reach
    scale = 1.0 / math.sqrt(query_norm.shape[2])
    offsets = jnp.arange(span, dtype=jnp.int32)
    inside = jnp.arange(block, dtype=jnp.int32)

    def visit(carry, index):
        key_acc, value_acc = carry
        begin = index * block
        query_pos = first + begin + inside
        key_pos = first + begin - reach + offsets
        allowed = (key_pos[None, :] >= starts[:, None]) & (key_pos[None, :] <= query_pos[:, None])
        scores = (
            jnp.einsum("qnd,knd->qnk", query_norm, key_ext, preferred_element_type=jnp.float32)
            * scale
        )
        scores = jnp.where(allowed[:, None, :], scores, jnp.float32(-1e30))
        top = jnp.max(scores, axis=2, keepdims=True)
        expo = jnp.exp(scores - top)
        probs = expo / jnp.sum(expo, axis=2, keepdims=True)
        probs_low = probs.astype(jnp.bfloat16)
        attended = jnp.einsum(
            "qnk,knd->qnd", probs_low, value_ext, preferred_element_type=jnp.float32
        ).astype(jnp.bfloat16)
        delta = jnp.sum(
            grad_rows.astype(jnp.float32) * attended.astype(jnp.float32), axis=2, keepdims=True
        )
        prob_grad = jnp.einsum(
            "qnd,knd->qnk", grad_rows, value_ext, preferred_element_type=jnp.float32
        )
        score_grad = (probs * (prob_grad - delta) * scale).astype(jnp.bfloat16)
        query_grad = jnp.einsum(
            "qnk,knd->qnd", score_grad, key_ext, preferred_element_type=jnp.float32
        ).astype(jnp.bfloat16)
        key_step = jnp.einsum(
            "qnk,qnd->knd", score_grad, query_norm, preferred_element_type=jnp.float32
        )
        value_step = jnp.einsum(
            "qnk,qnd->knd", probs_low, grad_rows, preferred_element_type=jnp.float32
        )
        key_acc = key_acc + key_step
        value_acc = value_acc + value_step
        return ((key_acc, value_acc), (attended, query_grad))

    zeros = jnp.zeros(key_ext.shape, jnp.float32)
    (key_acc, value_acc), (attended, query_grad) = lax.scan(
        visit, (zeros, zeros), jnp.arange(rows // block, dtype=jnp.int32)
    )
    heads, depth = (query_norm.shape[1], query_norm.shape[2])
    return (
        attended.reshape(rows, heads, depth),
        query_grad.reshape(rows, heads, depth),
        key_acc,
        value_acc,
    )


def on_device(queries, keys, values, modality, clip_lengths, query_gains, key_gains, out_grad):
    count, width = queries.shape
    heads = width // HD
    kv_heads = keys.shape[1] // HD
    repeat = heads // kv_heads
    query_norm, query_unit, query_factor, query_gain_rows = normalize(
        queries, modality, query_gains
    )
    key_norm, key_unit, key_factor, key_gain_rows = normalize(keys, modality, key_gains)
    first = lax.axis_index(("seq", "head")) * count
    depth = (MOST + count - 1) // count
    far_keys = []
    far_values = []
    for step in range(depth, 0, -1):
        moved_key, moved_value = from_behind((key_norm, values), ("seq", "head"), step)
        far_keys.append(moved_key)
        far_values.append(moved_value)
    key_ext = jnp.concatenate(far_keys + [key_norm], 0)
    value_ext = jnp.concatenate(far_values + [values], 0)
    starts = clip_start(clip_lengths, first + jnp.arange(count, dtype=jnp.int32))
    attended, query_low, key_acc, value_acc = attend(
        query_norm.reshape(count, heads, HD),
        spread_heads(key_ext, kv_heads, repeat),
        spread_heads(value_ext, kv_heads, repeat),
        out_grad.reshape(count, heads, HD),
        first,
        starts,
        min(row_block, count),
    )
    key_acc = fold_heads(key_acc, kv_heads, repeat)
    value_acc = fold_heads(value_acc, kv_heads, repeat)
    front_key = key_acc[:MOST]
    front_value = value_acc[:MOST]
    key_total = key_acc[MOST:]
    value_total = value_acc[MOST:]
    for step in range(depth, 0, -1):
        begin = (depth - step) * count
        back_key, back_value = (
            from_behind(
                front_key[begin : begin + count].astype(jnp.bfloat16), ("seq", "head"), -step
            ).astype(jnp.float32),
            from_behind(
                front_value[begin : begin + count].astype(jnp.bfloat16), ("seq", "head"), -step
            ).astype(jnp.float32),
        )
        key_total = key_total + back_key
        value_total = value_total + back_value
    attended = attended.reshape(count, width)
    query_low = query_low.reshape(count, width)
    key_low = key_total.reshape(count, kv_heads * HD).astype(jnp.bfloat16)
    value_grad = value_total.reshape(count, kv_heads * HD).astype(jnp.bfloat16)
    query_grad, query_gain = unnormalize(
        query_low, query_unit, query_factor, query_gain_rows, modality
    )
    key_grad, key_gain = unnormalize(key_low, key_unit, key_factor, key_gain_rows, modality)
    query_gain_grad, key_gain_grad = lax.psum((query_gain, key_gain), ("seq", "head"))
    return (attended, query_grad, key_grad, value_grad, query_gain_grad, key_gain_grad)


def solution(mesh):
    return jax.shard_map(
        on_device,
        mesh=mesh,
        in_specs=(
            P(("seq", "head"), None),
            P(("seq", "head"), None),
            P(("seq", "head"), None),
            P(("seq", "head")),
            P(),
            P(),
            P(),
            P(("seq", "head"), None),
        ),
        out_specs=(
            P(("seq", "head"), None),
            P(("seq", "head"), None),
            P(("seq", "head"), None),
            P(("seq", "head"), None),
            P(),
            P(),
        ),
        check_vma=False,
    )
```

profile of v0, /device:TPU:2, one launch (start us, length us, event | category | flops | bytes accessed | tf_op | source)
XLA Modules:
  0.0 336.1 jit_solution(18384643706049174742)
XLA Ops:
  0.7 5.3 %collective-permute-start.2 = (bf16[128,1024]{1,0:T(8,128)(2,1)}, bf16[128,1024]{1,0:T(8,128)(2,1)}, u32[]{:S(2)}, u32[]{:S(2)}) collective-permute-start(bf16[128,1024]{1,0:T(8,128)(2,1)} %param.10), channel_id=1, source_target_pairs={{0,2},{1,3},{2,4},{3,5},{4,6},{5,7},{6,8},{7,9},{8,10},{9,11},{10,... | collective-permute-start | bytes 786440 | tf_op jit(solution)/shard_map/ppermute | solution.py:18
  6.0 6.8 %collective-permute-start.1 = (bf16[128,1024]{1,0:T(8,128)(2,1)}, bf16[128,1024]{1,0:T(8,128)(2,1)}, u32[]{:S(2)}, u32[]{:S(2)}) collective-permute-start(bf16[128,1024]{1,0:T(8,128)(2,1)} %param.10), channel_id=1, source_target_pairs={{0,3},{1,4},{2,5},{3,6},{4,7},{5,8},{6,9},{7,10},{8,11},{9,12},{10... | collective-permute-start | bytes 786440 | tf_op jit(solution)/shard_map/ppermute | solution.py:18
  15.8 3.4 %collective-permute-start.6 = (bf16[128,1024]{1,0:T(8,128)(2,1)S(1)}, bf16[128,1024]{1,0:T(8,128)(2,1)}, u32[]{:S(2)}, u32[]{:S(2)}) collective-permute-start(bf16[128,1024]{1,0:T(8,128)(2,1)S(1)} %multiply_convert_fusion.1), channel_id=1, source_target_pairs={{0,2},{1,3},{2,4},{3,5},{4,6},{5,7},{6,8},{7,9},{8,10},{9,11},{10,... | collective-permute-start | bytes 786440 | tf_op jit(solution)/shard_map/ppermute | solution.py:18
  22.2 7.3 %collective-permute-start.4 = (bf16[128,1024]{1,0:T(8,128)(2,1)S(1)}, bf16[128,1024]{1,0:T(8,128)(2,1)}, u32[]{:S(2)}, u32[]{:S(2)}) collective-permute-start(bf16[128,1024]{1,0:T(8,128)(2,1)S(1)} %multiply_convert_fusion.1), channel_id=1, source_target_pairs={{0,4},{1,5},{2,6},{3,7},{4,8},{5,9},{6,10},{7,11},{8,12},{9,13},{1... | collective-permute-start | bytes 786440 | tf_op jit(solution)/shard_map/ppermute | solution.py:18
  35.7 39.3 %collective-permute-done.4 = bf16[128,1024]{1,0:T(8,128)(2,1)} collective-permute-done((bf16[128,1024]{1,0:T(8,128)(2,1)S(1)}, bf16[128,1024]{1,0:T(8,128)(2,1)}, u32[]{:S(2)}, u32[]{:S(2)}) %collective-permute-start.4) | collective-permute-done | bytes 262176 | tf_op jit(solution)/shard_map/ppermute | solution.py:18
  78.7 3.1 collective-permute-start
  82.7 11.1 %collective-permute-start.3 = (bf16[128,1024]{1,0:T(8,128)(2,1)S(1)}, bf16[128,1024]{1,0:T(8,128)(2,1)}, u32[]{:S(2)}, u32[]{:S(2)}) collective-permute-start(bf16[128,1024]{1,0:T(8,128)(2,1)S(1)} %copy-done.9), channel_id=1, source_target_pairs={{0,1},{1,2},{2,3},{3,4},{4,5},{5,6},{6,7},{7,8},{8,9},{9,10},{10,1... | collective-permute-start | bytes 786440 | tf_op jit(solution)/shard_map/ppermute | solution.py:18
  112.6 3.1 broadcast_in_dim.150
  115.6 9.4 %fusion.39 = (f32[128,32]{0,1:T(8,128)S(1)}, f32[128,32,640]{0,2,1:T(8,128)}) fusion(pred[128,640]{0,1:T(8,128)(4,1)S(1)} %compare_and_fusion, bf16[640,32,128]{0,2,1:T(8,128)(2,1)} %bitcast.118, f32[128,4096]{0,1:T(8,128)S(1)} %copy.87, f32[32,128]{1,0:T(8,128)S(1)} %bitcast.141, f32[32,128]{1,0:T(8,128)S(1)} %bitcast.137, ...), kind=kOutput, calls=%fused_computation.77 | convolution fusion | flops 683672192 | bytes 17973376 | tf_op jit(solution)/shard_map/while/body/eval_jaxpr/sub | solution.py:85
  125.0 5.4 %fusion.8 = bf16[128,32,640]{0,2,1:T(8,128)(2,1)S(1)} fusion(f32[128,32,640]{0,2,1:T(8,128)} %get-tuple-element.94, f32[128,32]{0,1:T(8,128)S(1)} %get-tuple-element.93), kind=kLoop, calls=%fused_computation.14 | loop fusion | flops 5242880 | bytes 15745024 | tf_op jit(solution)/shard_map/while/body/eval_jaxpr/convert_element_type | solution.py:87
  131.7 3.1 multiply_reduce_fusion
  134.7 3.4 %bitcast_reduce_fusion = f32[640,8,128]{2,0,1:T(8,128)} fusion(bf16[128,32,640]{0,2,1:T(8,128)(2,1)S(1)} %fusion.8, bf16[128,32,128]{0,2,1:T(8,128)(2,1)S(1)} %bitcast.122), kind=kOutput, calls=%fused_computation.1 | convolution fusion | flops 673054720 | bytes 8912896 | tf_op jit(solution)/shard_map/while/body/eval_jaxpr/qnk,qnd->knd/dot_general | solution.py:104
  138.2 6.8 %fusion.3 = bf16[128,32,640]{0,2,1:T(8,128)(2,1)} fusion(f32[128,32]{0,1:T(8,128)S(1)} %get-tuple-element.95, f32[128,32,640]{0,2,1:T(8,128)} %get-tuple-element.94, f32[128,32]{0,1:T(8,128)S(1)} %get-tuple-element.93, bf16[640,32,128]{2,0,1:T(8,128)(2,1)S(1)} %bitcast.116, bf16[128,32,128]{0,2,1:T(8,128)(2,1)S(1)} %bitcast.123), kind=kOutput, calls=%fused_computation.6 | convolution fusion | flops 684195840 | bytes 22052864 | tf_op jit(solution)/shard_map/while/body/eval_jaxpr/qnd,knd->qnk/dot_general | solution.py:94
  144.9 4.0 %fusion.12 = (f32[128,32]{0,1:T(8,128)S(1)}, bf16[32,128,128]{2,1,0:T(8,128)(2,1)S(1)}) fusion(f32[128,4096]{0,1:T(8,128)S(1)} %copy.87, f32[32,128]{1,0:T(8,128)S(1)} %bitcast.142, f32[32,128]{1,0:T(8,128)S(1)} %bitcast.138, f32[128,32]{0,1:T(8,128)S(1)} %add_rsqrt_fusion, pred[128]{0:T(512)(128)(4,1)S(1)} %broadcast_compare_fusion, ...), kind=kOutput, calls=%fused_computation.21 | convolution fusion | flops 674754560 | bytes 13697152 | tf_op jit(solution)/shard_map/while/body/eval_jaxpr/qnk,knd->qnd/dot_general | solution.py:98
  149.0 4.0 %bitcast_reduce_fusion.1 = f32[640,8,128]{0,2,1:T(8,128)} fusion(bf16[128,32,640]{0,2,1:T(8,128)(2,1)S(1)} %copy-done.2, f32[128,4096]{0,1:T(8,128)S(1)} %copy.87, f32[32,128]{1,0:T(8,128)S(1)} %bitcast.143, f32[32,128]{1,0:T(8,128)S(1)} %bitcast.139, f32[128,32]{0,1:T(8,128)S(1)} %add_rsqrt_fusion, pred[128]{0:T(512)(128)(4,1)S(1)} %broadcast_compare_fusion), kind=kOutput, calls=%fused_computation.2 | convolution fusion | flops 675151872 | bytes 10010752 | tf_op jit(solution)/shard_map/while/body/eval_jaxpr/qnk,qnd->knd/dot_general | solution.py:101
  160.6 4.5 %collective-permute-start.8 = (bf16[128,8,128]{0,2,1:T(8,128)(2,1)S(1)}, bf16[128,8,128]{0,2,1:T(8,128)(2,1)S(1)}, u32[]{:S(2)}, u32[]{:S(2)}) collective-permute-start(bf16[128,8,128]{0,2,1:T(8,128)(2,1)S(1)} %get-tuple-element.85), channel_id=1, source_target_pairs={{4,0},{5,1},{6,2},{7,3},{8,4},{9,5},{10,6},{11,7},{12,8},{13,9},{1... | collective-permute-start | bytes 786440 | tf_op jit(solution)/shard_map/ppermute | solution.py:18
  167.1 6.9 %collective-permute-start.10 = (bf16[128,8,128]{0,2,1:T(8,128)(2,1)S(1)}, bf16[128,8,128]{0,2,1:T(8,128)(2,1)S(1)}, u32[]{:S(2)}, u32[]{:S(2)}) collective-permute-start(bf16[128,8,128]{0,2,1:T(8,128)(2,1)S(1)} %get-tuple-element.87), channel_id=1, source_target_pairs={{2,0},{3,1},{4,2},{5,3},{6,4},{7,5},{8,6},{9,7},{10,8},{11,9},{12,... | collective-permute-start | bytes 786440 | tf_op jit(solution)/shard_map/ppermute | solution.py:18
  177.8 6.9 %collective-permute-start.12 = (bf16[128,8,128]{2,0,1:T(8,128)(2,1)}, bf16[128,8,128]{2,0,1:T(8,128)(2,1)S(1)}, u32[]{:S(2)}, u32[]{:S(2)}) collective-permute-start(bf16[128,8,128]{2,0,1:T(8,128)(2,1)} %get-tuple-element.81), channel_id=1, source_target_pairs={{4,0},{5,1},{6,2},{7,3},{8,4},{9,5},{10,6},{11,7},{12,8},{13,9},{1... | collective-permute-start | bytes 786440 | tf_op jit(solution)/shard_map/ppermute | solution.py:18
  190.7 7.5 %collective-permute-done.10 = bf16[128,8,128]{0,2,1:T(8,128)(2,1)S(1)} collective-permute-done((bf16[128,8,128]{0,2,1:T(8,128)(2,1)S(1)}, bf16[128,8,128]{0,2,1:T(8,128)(2,1)S(1)}, u32[]{:S(2)}, u32[]{:S(2)}) %collective-permute-start.10) | collective-permute-done | bytes 262176 | tf_op jit(solution)/shard_map/ppermute | solution.py:18
  200.1 12.4 %collective-permute-done.9 = bf16[128,8,128]{0,2,1:T(8,128)(2,1)S(1)} collective-permute-done((bf16[128,8,128]{0,2,1:T(8,128)(2,1)S(1)}, bf16[128,8,128]{0,2,1:T(8,128)(2,1)S(1)}, u32[]{:S(2)}, u32[]{:S(2)}) %collective-permute-start.9) | collective-permute-done | bytes 262176 | tf_op jit(solution)/shard_map/ppermute | solution.py:18
  215.5 14.8 %collective-permute-done.15 = bf16[128,8,128]{2,0,1:T(8,128)(2,1)} collective-permute-done((bf16[128,8,128]{2,0,1:T(8,128)(2,1)}, bf16[128,8,128]{2,0,1:T(8,128)(2,1)}, u32[]{:S(2)}, u32[]{:S(2)}) %collective-permute-start.15) | collective-permute-done | bytes 262176 | tf_op jit(solution)/shard_map/ppermute | solution.py:18
  230.3 12.9 %collective-permute-done.14 = bf16[128,8,128]{2,0,1:T(8,128)(2,1)} collective-permute-done((bf16[128,8,128]{2,0,1:T(8,128)(2,1)}, bf16[128,8,128]{2,0,1:T(8,128)(2,1)}, u32[]{:S(2)}, u32[]{:S(2)}) %collective-permute-start.14) | collective-permute-done | bytes 262176 | tf_op jit(solution)/shard_map/ppermute | solution.py:18
  243.2 6.5 %collective-permute-done.13 = bf16[128,8,128]{2,0,1:T(8,128)(2,1)} collective-permute-done((bf16[128,8,128]{2,0,1:T(8,128)(2,1)}, bf16[128,8,128]{2,0,1:T(8,128)(2,1)}, u32[]{:S(2)}, u32[]{:S(2)}) %collective-permute-start.13) | collective-permute-done | bytes 262176 | tf_op jit(solution)/shard_map/ppermute | solution.py:18
  252.2 84.0 %all-reduce = (f32[2,4096]{1,0:T(2,128)}, f32[2,1024]{1,0:T(2,128)}) all-reduce(f32[2,4096]{1,0:T(2,128)S(1)} %fusion.28, f32[2,1024]{1,0:T(2,128)S(1)} %fusion.26), channel_id=1, replica_groups=mesh['seq'=8,'head'=32] {'seq','head'}, use_global_device_ids=true, to_apply=%region_11.12 | all-reduce | flops 10240 | bytes 81920 | tf_op jit(solution)/shard_map/psum | solution.py:179
  (105 shorter events, 63.3 us)
Async XLA Ops:
  0.6 15.1 %copy-start.8 = (bf16[128,1024]{1,0:T(8,128)(2,1)S(1)}, bf16[128,1024]{1,0:T(8,128)(2,1)}, u32[]{:S(2)}) copy-start(bf16[128,1024]{1,0:T(8,128)(2,1)} %param.9) | copy-start | bytes 786436
  0.6 28.9 %copy-start.10 = (f32[2,4096]{1,0:T(2,128)S(1)}, f32[2,4096]{1,0:T(2,128)}, u32[]{:S(2)}) copy-start(f32[2,4096]{1,0:T(2,128)} %param.13) | copy-start | bytes 98308
  0.7 29.0 %copy-start.12 = (s32[128]{0:T(128)S(1)}, s32[128]{0:T(128)}, u32[]{:S(2)}) copy-start(s32[128]{0:T(128)} %param.12) | copy-start | bytes 1540
  0.7 102.4 %collective-permute-start.2 = (bf16[128,1024]{1,0:T(8,128)(2,1)}, bf16[128,1024]{1,0:T(8,128)(2,1)}, u32[]{:S(2)}, u32[]{:S(2)}) collective-permute-start(bf16[128,1024]{1,0:T(8,128)(2,1)} %param.10), channel_id=1, source_target_pairs={{0,2},{1,3},{2,4},{3,5},{4,6},{5,7},{6,8},{7,9},{8,10},{9,11},{10,... | collective-permute-start | bytes 786440 | tf_op jit(solution)/shard_map/ppermute | solution.py:18
  6.0 95.4 %collective-permute-start.1 = (bf16[128,1024]{1,0:T(8,128)(2,1)}, bf16[128,1024]{1,0:T(8,128)(2,1)}, u32[]{:S(2)}, u32[]{:S(2)}) collective-permute-start(bf16[128,1024]{1,0:T(8,128)(2,1)} %param.10), channel_id=1, source_target_pairs={{0,3},{1,4},{2,5},{3,6},{4,7},{5,8},{6,9},{7,10},{8,11},{9,12},{10... | collective-permute-start | bytes 786440 | tf_op jit(solution)/shard_map/ppermute | solution.py:18
  15.8 62.8 %collective-permute-start.6 = (bf16[128,1024]{1,0:T(8,128)(2,1)S(1)}, bf16[128,1024]{1,0:T(8,128)(2,1)}, u32[]{:S(2)}, u32[]{:S(2)}) collective-permute-start(bf16[128,1024]{1,0:T(8,128)(2,1)S(1)} %multiply_convert_fusion.1), channel_id=1, source_target_pairs={{0,2},{1,3},{2,4},{3,5},{4,6},{5,7},{6,8},{7,9},{8,10},{9,11},{10,... | collective-permute-start | bytes 786440 | tf_op jit(solution)/shard_map/ppermute | solution.py:18
  19.2 63.5 %collective-permute-start.5 = (bf16[128,1024]{1,0:T(8,128)(2,1)S(1)}, bf16[128,1024]{1,0:T(8,128)(2,1)}, u32[]{:S(2)}, u32[]{:S(2)}) collective-permute-start(bf16[128,1024]{1,0:T(8,128)(2,1)S(1)} %multiply_convert_fusion.1), channel_id=1, source_target_pairs={{0,3},{1,4},{2,5},{3,6},{4,7},{5,8},{6,9},{7,10},{8,11},{9,12},{10... | collective-permute-start | bytes 786440 | tf_op jit(solution)/shard_map/ppermute | solution.py:18
  22.2 52.8 %collective-permute-start.4 = (bf16[128,1024]{1,0:T(8,128)(2,1)S(1)}, bf16[128,1024]{1,0:T(8,128)(2,1)}, u32[]{:S(2)}, u32[]{:S(2)}) collective-permute-start(bf16[128,1024]{1,0:T(8,128)(2,1)S(1)} %multiply_convert_fusion.1), channel_id=1, source_target_pairs={{0,4},{1,5},{2,6},{3,7},{4,8},{5,9},{6,10},{7,11},{8,12},{9,13},{1... | collective-permute-start | bytes 786440 | tf_op jit(solution)/shard_map/ppermute | solution.py:18
  32.6 46.0 %copy-start.9 = (bf16[128,1024]{1,0:T(8,128)(2,1)S(1)}, bf16[128,1024]{1,0:T(8,128)(2,1)}, u32[]{:S(2)}) copy-start(bf16[128,1024]{1,0:T(8,128)(2,1)} %param.10) | copy-start | bytes 786436
  75.0 21.3 %collective-permute-start.7 = (bf16[128,1024]{1,0:T(8,128)(2,1)S(1)}, bf16[128,1024]{1,0:T(8,128)(2,1)S(1)}, u32[]{:S(2)}, u32[]{:S(2)}) collective-permute-start(bf16[128,1024]{1,0:T(8,128)(2,1)S(1)} %multiply_convert_fusion.1), channel_id=1, source_target_pairs={{0,1},{1,2},{2,3},{3,4},{4,5},{5,6},{6,7},{7,8},{8,9},{9,10},{10,1... | collective-permute-start | bytes 786440 | tf_op jit(solution)/shard_map/ppermute | solution.py:18
  78.7 19.1 %collective-permute-start = (bf16[128,1024]{1,0:T(8,128)(2,1)S(1)}, bf16[128,1024]{1,0:T(8,128)(2,1)S(1)}, u32[]{:S(2)}, u32[]{:S(2)}) collective-permute-start(bf16[128,1024]{1,0:T(8,128)(2,1)S(1)} %copy-done.9), channel_id=1, source_target_pairs={{0,4},{1,5},{2,6},{3,7},{4,8},{5,9},{6,10},{7,11},{8,12},{9,13},{1... | collective-permute-start | bytes 786440 | tf_op jit(solution)/shard_map/ppermute | solution.py:18
  82.7 24.8 %collective-permute-start.3 = (bf16[128,1024]{1,0:T(8,128)(2,1)S(1)}, bf16[128,1024]{1,0:T(8,128)(2,1)}, u32[]{:S(2)}, u32[]{:S(2)}) collective-permute-start(bf16[128,1024]{1,0:T(8,128)(2,1)S(1)} %copy-done.9), channel_id=1, source_target_pairs={{0,1},{1,2},{2,3},{3,4},{4,5},{5,6},{6,7},{7,8},{8,9},{9,10},{10,1... | collective-permute-start | bytes 786440 | tf_op jit(solution)/shard_map/ppermute | solution.py:18
  134.7 10.2 %slice-start = ((s8[5242880]{0:T(1024)(128)(4,1)}), s8[1048576]{0:T(1024)(128)(4,1)S(1)}, s32[]{:S(2)}) async-start(s8[5242880]{0:T(1024)(128)(4,1)} %bitcast.119), calls=%async_computation | async-start | bytes 2097152
  160.2 16.4 %copy-start.6 = (f32[640,8,128]{2,0,1:T(8,128)S(1)}, f32[640,8,128]{2,0,1:T(8,128)}, u32[]{:S(2)}) copy-start(f32[640,8,128]{2,0,1:T(8,128)} %bitcast_reduce_fusion) | copy-start | bytes 7864324
  160.6 25.2 %collective-permute-start.8 = (bf16[128,8,128]{0,2,1:T(8,128)(2,1)S(1)}, bf16[128,8,128]{0,2,1:T(8,128)(2,1)S(1)}, u32[]{:S(2)}, u32[]{:S(2)}) collective-permute-start(bf16[128,8,128]{0,2,1:T(8,128)(2,1)S(1)} %get-tuple-element.85), channel_id=1, source_target_pairs={{4,0},{5,1},{6,2},{7,3},{8,4},{9,5},{10,6},{11,7},{12,8},{13,9},{1... | collective-permute-start | bytes 786440 | tf_op jit(solution)/shard_map/ppermute | solution.py:18
  165.1 22.6 %collective-permute-start.11 = (bf16[128,8,128]{0,2,1:T(8,128)(2,1)S(1)}, bf16[128,8,128]{0,2,1:T(8,128)(2,1)S(1)}, u32[]{:S(2)}, u32[]{:S(2)}) collective-permute-start(bf16[128,8,128]{0,2,1:T(8,128)(2,1)S(1)} %get-tuple-element.86), channel_id=1, source_target_pairs={{1,0},{2,1},{3,2},{4,3},{5,4},{6,5},{7,6},{8,7},{9,8},{10,9},{11,1... | collective-permute-start | bytes 786440 | tf_op jit(solution)/shard_map/ppermute | solution.py:18
  167.1 31.1 %collective-permute-start.10 = (bf16[128,8,128]{0,2,1:T(8,128)(2,1)S(1)}, bf16[128,8,128]{0,2,1:T(8,128)(2,1)S(1)}, u32[]{:S(2)}, u32[]{:S(2)}) collective-permute-start(bf16[128,8,128]{0,2,1:T(8,128)(2,1)S(1)} %get-tuple-element.87), channel_id=1, source_target_pairs={{2,0},{3,1},{4,2},{5,3},{6,4},{7,5},{8,6},{9,7},{10,8},{11,9},{12,... | collective-permute-start | bytes 786440 | tf_op jit(solution)/shard_map/ppermute | solution.py:18
  174.0 10.7 %copy-start.1 = (f32[128,32,128]{0,2,1:T(8,128)S(1)}, f32[128,32,128]{0,2,1:T(8,128)}, u32[]{:S(2)}) copy-start(f32[128,32,128]{0,2,1:T(8,128)} %get-tuple-element.79) | copy-start | bytes 6291460
  174.0 10.7 %copy-start.11 = (s32[128]{0:T(128)S(1)}, s32[128]{0:T(128)}, u32[]{:S(2)}) copy-start(s32[128]{0:T(128)} %param.11) | copy-start | bytes 1540
  174.0 38.5 %collective-permute-start.9 = (bf16[128,8,128]{0,2,1:T(8,128)(2,1)S(1)}, bf16[128,8,128]{0,2,1:T(8,128)(2,1)S(1)}, u32[]{:S(2)}, u32[]{:S(2)}) collective-permute-start(bf16[128,8,128]{0,2,1:T(8,128)(2,1)S(1)} %get-tuple-element.88), channel_id=1, source_target_pairs={{3,0},{4,1},{5,2},{6,3},{7,4},{8,5},{9,6},{10,7},{11,8},{12,9},{13... | collective-permute-start | bytes 786440 | tf_op jit(solution)/shard_map/ppermute | solution.py:18
  177.8 37.7 %collective-permute-start.12 = (bf16[128,8,128]{2,0,1:T(8,128)(2,1)}, bf16[128,8,128]{2,0,1:T(8,128)(2,1)S(1)}, u32[]{:S(2)}, u32[]{:S(2)}) collective-permute-start(bf16[128,8,128]{2,0,1:T(8,128)(2,1)} %get-tuple-element.81), channel_id=1, source_target_pairs={{4,0},{5,1},{6,2},{7,3},{8,4},{9,5},{10,6},{11,7},{12,8},{13,9},{1... | collective-permute-start | bytes 786440 | tf_op jit(solution)/shard_map/ppermute | solution.py:18
  185.8 44.4 %collective-permute-start.15 = (bf16[128,8,128]{2,0,1:T(8,128)(2,1)}, bf16[128,8,128]{2,0,1:T(8,128)(2,1)}, u32[]{:S(2)}, u32[]{:S(2)}) collective-permute-start(bf16[128,8,128]{2,0,1:T(8,128)(2,1)} %get-tuple-element.82), channel_id=1, source_target_pairs={{1,0},{2,1},{3,2},{4,3},{5,4},{6,5},{7,6},{8,7},{9,8},{10,9},{11,1... | collective-permute-start | bytes 786440 | tf_op jit(solution)/shard_map/ppermute | solution.py:18
  187.8 55.4 %collective-permute-start.14 = (bf16[128,8,128]{2,0,1:T(8,128)(2,1)}, bf16[128,8,128]{2,0,1:T(8,128)(2,1)}, u32[]{:S(2)}, u32[]{:S(2)}) collective-permute-start(bf16[128,8,128]{2,0,1:T(8,128)(2,1)} %get-tuple-element.83), channel_id=1, source_target_pairs={{2,0},{3,1},{4,2},{5,3},{6,4},{7,5},{8,6},{9,7},{10,8},{11,9},{12,... | collective-permute-start | bytes 786440 | tf_op jit(solution)/shard_map/ppermute | solution.py:18
  198.2 51.5 %collective-permute-start.13 = (bf16[128,8,128]{2,0,1:T(8,128)(2,1)}, bf16[128,8,128]{2,0,1:T(8,128)(2,1)}, u32[]{:S(2)}, u32[]{:S(2)}) collective-permute-start(bf16[128,8,128]{2,0,1:T(8,128)(2,1)} %get-tuple-element.84), channel_id=1, source_target_pairs={{3,0},{4,1},{5,2},{6,3},{7,4},{8,5},{9,6},{10,7},{11,8},{12,9},{13... | collective-permute-start | bytes 786440 | tf_op jit(solution)/shard_map/ppermute | solution.py:18
  (7 other events, 33.2 us)
where the time goes:
time: 339 us; the launch traced here: 336 us
  waiting for transfers between devices  96.1 us (28%)
  blocking collectives  84 us (25%)
  starting transfers between devices  71.5 us (21%)
  local copies, waits for them, and re-layouts  37 us (11%)
  matrix products  32.1 us (9%)
  other arithmetic  14.4 us (4%)
    ppermute x16, waiting for transfers between devices, from_behind(): lax.ppermute(value, axis, [(source, source + steps) for source in range(f...  96.1 us
    psum x1, blocking collectives, on_device(): lax.psum((query_gain, key_gain), ('seq', 'head'))  84 us
    ppermute x16, starting transfers between devices, from_behind(): lax.ppermute(value, axis, [(source, source + steps) for source in range(f...  71.5 us
    unnamed x48, local copies, waits for them, and re-layouts  20.7 us
    broadcast_in_dim x4, local copies, waits for them, and re-layouts, spread_heads(): jnp.broadcast_to(rows.reshape(count, kv_heads, 1, HD), (count, kv_heads,...  9.72 us
    sub x1, matrix products, visit(): expo = jnp.exp(scores - top)  9.41 us
  transfers between devices with their start and end apart: 16, of which 7 were waited for; matrix products, arithmetic and copies ran while one was open for 8% of the time, Pallas kernels for 0%

commit v1 on v0

--- a/solution.py
+++ b/solution.py
@@ -19,8 +19,8 @@
 
 
 def clip_start(clip_lengths, positions):
-    ends = jnp.cumsum(clip_lengths, dtype=jnp.int32)
-    begins = ends - clip_lengths
+    order = jnp.arange(clip_lengths.shape[0], dtype=jnp.int32)
+    begins = jnp.sum(jnp.where(order[None, :] < order[:, None], clip_lengths[None, :], 0), axis=1)
     chosen = jnp.where(
         begins[None, :] <= positions[:, None], begins[None, :], jnp.zeros((), jnp.int32)
     )

time: 339 us -> 339 us (level)
  no operation moved by 1% of the time
where the time goes in v1:
time: 339 us; the launch traced here: 336 us
  waiting for transfers between devices  96.5 us (28%)
  blocking collectives  84 us (25%)
  starting transfers between devices  71.3 us (21%)
  local copies, waits for them, and re-layouts  36.7 us (11%)
  matrix products  32.2 us (9%)
  other arithmetic  14.2 us (4%)
    ppermute x16, waiting for transfers between devices, from_behind(): lax.ppermute(value, axis, [(source, source + steps) for source in range(f...  96.5 us
    psum x1, blocking collectives, on_device(): lax.psum((query_gain, key_gain), ('seq', 'head'))  84 us
    ppermute x16, starting transfers between devices, from_behind(): lax.ppermute(value, axis, [(source, source + steps) for source in range(f...  71.3 us
    unnamed x48, local copies, waits for them, and re-layouts  20.5 us
    broadcast_in_dim x4, local copies, waits for them, and re-layouts, spread_heads(): jnp.broadcast_to(rows.reshape(count, kv_heads, 1, HD), (count, kv_heads,...  9.7 us
    sub x1, matrix products, visit(): expo = jnp.exp(scores - top)  9.41 us
  transfers between devices with their start and end apart: 16, of which 7 were waited for; matrix products, arithmetic and copies ran while one was open for 8% of the time, Pallas kernels for 0%

profile of v1, /device:TPU:2, one launch (start us, length us, event | category | flops | bytes accessed | tf_op | source)
XLA Modules:
  0.0 336.1 jit_solution(9499922176696073550)
XLA Ops:
  0.7 5.3 %collective-permute-start.2 = (bf16[128,1024]{1,0:T(8,128)(2,1)}, bf16[128,1024]{1,0:T(8,128)(2,1)}, u32[]{:S(2)}, u32[]{:S(2)}) collective-permute-start(bf16[128,1024]{1,0:T(8,128)(2,1)} %param.10), channel_id=1, source_target_pairs={{0,2},{1,3},{2,4},{3,5},{4,6},{5,7},{6,8},{7,9},{8,10},{9,11},{10,... | collective-permute-start | bytes 786440 | tf_op jit(solution)/shard_map/ppermute | solution.py:18
  6.0 6.8 %collective-permute-start.1 = (bf16[128,1024]{1,0:T(8,128)(2,1)}, bf16[128,1024]{1,0:T(8,128)(2,1)}, u32[]{:S(2)}, u32[]{:S(2)}) collective-permute-start(bf16[128,1024]{1,0:T(8,128)(2,1)} %param.10), channel_id=1, source_target_pairs={{0,3},{1,4},{2,5},{3,6},{4,7},{5,8},{6,9},{7,10},{8,11},{9,12},{10... | collective-permute-start | bytes 786440 | tf_op jit(solution)/shard_map/ppermute | solution.py:18
  15.8 3.4 %collective-permute-start.6 = (bf16[128,1024]{1,0:T(8,128)(2,1)S(1)}, bf16[128,1024]{1,0:T(8,128)(2,1)}, u32[]{:S(2)}, u32[]{:S(2)}) collective-permute-start(bf16[128,1024]{1,0:T(8,128)(2,1)S(1)} %multiply_convert_fusion.1), channel_id=1, source_target_pairs={{0,2},{1,3},{2,4},{3,5},{4,6},{5,7},{6,8},{7,9},{8,10},{9,11},{10,... | collective-permute-start | bytes 786440 | tf_op jit(solution)/shard_map/ppermute | solution.py:18
  22.2 7.3 %collective-permute-start.4 = (bf16[128,1024]{1,0:T(8,128)(2,1)S(1)}, bf16[128,1024]{1,0:T(8,128)(2,1)}, u32[]{:S(2)}, u32[]{:S(2)}) collective-permute-start(bf16[128,1024]{1,0:T(8,128)(2,1)S(1)} %multiply_convert_fusion.1), channel_id=1, source_target_pairs={{0,4},{1,5},{2,6},{3,7},{4,8},{5,9},{6,10},{7,11},{8,12},{9,13},{1... | collective-permute-start | bytes 786440 | tf_op jit(solution)/shard_map/ppermute | solution.py:18
  35.4 39.6 %collective-permute-done.4 = bf16[128,1024]{1,0:T(8,128)(2,1)} collective-permute-done((bf16[128,1024]{1,0:T(8,128)(2,1)S(1)}, bf16[128,1024]{1,0:T(8,128)(2,1)}, u32[]{:S(2)}, u32[]{:S(2)}) %collective-permute-start.4) | collective-permute-done | bytes 262176 | tf_op jit(solution)/shard_map/ppermute | solution.py:18
  78.7 3.1 collective-permute-start
  82.7 10.9 %collective-permute-start.3 = (bf16[128,1024]{1,0:T(8,128)(2,1)S(1)}, bf16[128,1024]{1,0:T(8,128)(2,1)}, u32[]{:S(2)}, u32[]{:S(2)}) collective-permute-start(bf16[128,1024]{1,0:T(8,128)(2,1)S(1)} %copy-done.9), channel_id=1, source_target_pairs={{0,1},{1,2},{2,3},{3,4},{4,5},{5,6},{6,7},{7,8},{8,9},{9,10},{10,1... | collective-permute-start | bytes 786440 | tf_op jit(solution)/shard_map/ppermute | solution.py:18
  112.6 3.1 broadcast_in_dim.164
  115.7 9.4 %fusion.39 = (f32[128,32]{0,1:T(8,128)S(1)}, f32[128,32,640]{0,2,1:T(8,128)}) fusion(pred[128,640]{0,1:T(8,128)(4,1)S(1)} %compare_and_fusion, bf16[640,32,128]{0,2,1:T(8,128)(2,1)} %bitcast.117, f32[128,4096]{0,1:T(8,128)S(1)} %copy.68, f32[32,128]{1,0:T(8,128)S(1)} %bitcast.140, f32[32,128]{1,0:T(8,128)S(1)} %bitcast.136, ...), kind=kOutput, calls=%fused_computation.79 | convolution fusion | flops 683672192 | bytes 17973376 | tf_op jit(solution)/shard_map/while/body/eval_jaxpr/sub | solution.py:85
  125.1 5.4 %fusion.8 = bf16[128,32,640]{0,2,1:T(8,128)(2,1)S(1)} fusion(f32[128,32,640]{0,2,1:T(8,128)} %get-tuple-element.88, f32[128,32]{0,1:T(8,128)S(1)} %get-tuple-element.87), kind=kLoop, calls=%fused_computation.14 | loop fusion | flops 5242880 | bytes 15745024 | tf_op jit(solution)/shard_map/while/body/eval_jaxpr/convert_element_type | solution.py:87
  131.7 3.1 multiply_reduce_fusion
  134.8 3.4 %bitcast_reduce_fusion = f32[640,8,128]{2,0,1:T(8,128)} fusion(bf16[128,32,640]{0,2,1:T(8,128)(2,1)S(1)} %fusion.8, bf16[128,32,128]{0,2,1:T(8,128)(2,1)S(1)} %bitcast.121), kind=kOutput, calls=%fused_computation.1 | convolution fusion | flops 673054720 | bytes 8912896 | tf_op jit(solution)/shard_map/while/body/eval_jaxpr/qnk,qnd->knd/dot_general | solution.py:104
  138.2 6.8 %fusion.3 = bf16[128,32,640]{0,2,1:T(8,128)(2,1)} fusion(f32[128,32]{0,1:T(8,128)S(1)} %get-tuple-element.89, f32[128,32,640]{0,2,1:T(8,128)} %get-tuple-element.88, f32[128,32]{0,1:T(8,128)S(1)} %get-tuple-element.87, bf16[640,32,128]{2,0,1:T(8,128)(2,1)S(1)} %bitcast.115, bf16[128,32,128]{0,2,1:T(8,128)(2,1)S(1)} %bitcast.122), kind=kOutput, calls=%fused_computation.6 | convolution fusion | flops 684195840 | bytes 22052864 | tf_op jit(solution)/shard_map/while/body/eval_jaxpr/qnd,knd->qnk/dot_general | solution.py:94
  145.0 4.0 %fusion.12 = (f32[128,32]{0,1:T(8,128)S(1)}, bf16[32,128,128]{2,1,0:T(8,128)(2,1)S(1)}) fusion(f32[128,4096]{0,1:T(8,128)S(1)} %copy.68, f32[32,128]{1,0:T(8,128)S(1)} %bitcast.141, f32[32,128]{1,0:T(8,128)S(1)} %bitcast.137, f32[128,32]{0,1:T(8,128)S(1)} %add_rsqrt_fusion, pred[128]{0:T(512)(128)(4,1)S(1)} %broadcast_compare_fusion, ...), kind=kOutput, calls=%fused_computation.21 | convolution fusion | flops 674754560 | bytes 13697152 | tf_op jit(solution)/shard_map/while/body/eval_jaxpr/qnk,knd->qnd/dot_general | solution.py:98
  149.0 4.0 %bitcast_reduce_fusion.1 = f32[640,8,128]{0,2,1:T(8,128)} fusion(bf16[128,32,640]{0,2,1:T(8,128)(2,1)S(1)} %copy-done.2, f32[128,4096]{0,1:T(8,128)S(1)} %copy.68, f32[32,128]{1,0:T(8,128)S(1)} %bitcast.142, f32[32,128]{1,0:T(8,128)S(1)} %bitcast.138, f32[128,32]{0,1:T(8,128)S(1)} %add_rsqrt_fusion, pred[128]{0:T(512)(128)(4,1)S(1)} %broadcast_compare_fusion), kind=kOutput, calls=%fused_computation.2 | convolution fusion | flops 675151872 | bytes 10010752 | tf_op jit(solution)/shard_map/while/body/eval_jaxpr/qnk,qnd->knd/dot_general | solution.py:101
  160.7 4.2 %collective-permute-start.8 = (bf16[128,8,128]{0,2,1:T(8,128)(2,1)S(1)}, bf16[128,8,128]{0,2,1:T(8,128)(2,1)S(1)}, u32[]{:S(2)}, u32[]{:S(2)}) collective-permute-start(bf16[128,8,128]{0,2,1:T(8,128)(2,1)S(1)} %get-tuple-element.79), channel_id=1, source_target_pairs={{4,0},{5,1},{6,2},{7,3},{8,4},{9,5},{10,6},{11,7},{12,8},{13,9},{1... | collective-permute-start | bytes 786440 | tf_op jit(solution)/shard_map/ppermute | solution.py:18
  166.8 7.2 %collective-permute-start.10 = (bf16[128,8,128]{0,2,1:T(8,128)(2,1)S(1)}, bf16[128,8,128]{0,2,1:T(8,128)(2,1)S(1)}, u32[]{:S(2)}, u32[]{:S(2)}) collective-permute-start(bf16[128,8,128]{0,2,1:T(8,128)(2,1)S(1)} %get-tuple-element.81), channel_id=1, source_target_pairs={{2,0},{3,1},{4,2},{5,3},{6,4},{7,5},{8,6},{9,7},{10,8},{11,9},{12,... | collective-permute-start | bytes 786440 | tf_op jit(solution)/shard_map/ppermute | solution.py:18
  177.8 6.9 %collective-permute-start.12 = (bf16[128,8,128]{2,0,1:T(8,128)(2,1)}, bf16[128,8,128]{2,0,1:T(8,128)(2,1)S(1)}, u32[]{:S(2)}, u32[]{:S(2)}) collective-permute-start(bf16[128,8,128]{2,0,1:T(8,128)(2,1)} %get-tuple-element.75), channel_id=1, source_target_pairs={{4,0},{5,1},{6,2},{7,3},{8,4},{9,5},{10,6},{11,7},{12,8},{13,9},{1... | collective-permute-start | bytes 786440 | tf_op jit(solution)/shard_map/ppermute | solution.py:18
  190.8 7.6 %collective-permute-done.10 = bf16[128,8,128]{0,2,1:T(8,128)(2,1)S(1)} collective-permute-done((bf16[128,8,128]{0,2,1:T(8,128)(2,1)S(1)}, bf16[128,8,128]{0,2,1:T(8,128)(2,1)S(1)}, u32[]{:S(2)}, u32[]{:S(2)}) %collective-permute-start.10) | collective-permute-done | bytes 262176 | tf_op jit(solution)/shard_map/ppermute | solution.py:18
  200.3 12.0 %collective-permute-done.9 = bf16[128,8,128]{0,2,1:T(8,128)(2,1)S(1)} collective-permute-done((bf16[128,8,128]{0,2,1:T(8,128)(2,1)S(1)}, bf16[128,8,128]{0,2,1:T(8,128)(2,1)S(1)}, u32[]{:S(2)}, u32[]{:S(2)}) %collective-permute-start.9) | collective-permute-done | bytes 262176 | tf_op jit(solution)/shard_map/ppermute | solution.py:18
  215.3 15.0 %collective-permute-done.15 = bf16[128,8,128]{2,0,1:T(8,128)(2,1)} collective-permute-done((bf16[128,8,128]{2,0,1:T(8,128)(2,1)}, bf16[128,8,128]{2,0,1:T(8,128)(2,1)}, u32[]{:S(2)}, u32[]{:S(2)}) %collective-permute-start.15) | collective-permute-done | bytes 262176 | tf_op jit(solution)/shard_map/ppermute | solution.py:18
  230.3 13.0 %collective-permute-done.14 = bf16[128,8,128]{2,0,1:T(8,128)(2,1)} collective-permute-done((bf16[128,8,128]{2,0,1:T(8,128)(2,1)}, bf16[128,8,128]{2,0,1:T(8,128)(2,1)}, u32[]{:S(2)}, u32[]{:S(2)}) %collective-permute-start.14) | collective-permute-done | bytes 262176 | tf_op jit(solution)/shard_map/ppermute | solution.py:18
  243.4 6.2 %collective-permute-done.13 = bf16[128,8,128]{2,0,1:T(8,128)(2,1)} collective-permute-done((bf16[128,8,128]{2,0,1:T(8,128)(2,1)}, bf16[128,8,128]{2,0,1:T(8,128)(2,1)}, u32[]{:S(2)}, u32[]{:S(2)}) %collective-permute-start.13) | collective-permute-done | bytes 262176 | tf_op jit(solution)/shard_map/ppermute | solution.py:18
  252.1 84.0 %all-reduce = (f32[2,4096]{1,0:T(2,128)}, f32[2,1024]{1,0:T(2,128)}) all-reduce(f32[2,4096]{1,0:T(2,128)S(1)} %fusion.28, f32[2,1024]{1,0:T(2,128)S(1)} %fusion.26), channel_id=1, replica_groups=mesh['seq'=8,'head'=32] {'seq','head'}, use_global_device_ids=true, to_apply=%region_11.12 | all-reduce | flops 10240 | bytes 81920 | tf_op jit(solution)/shard_map/psum | solution.py:179
  (102 shorter events, 63.3 us)
Async XLA Ops:
  0.6 15.1 %copy-start.8 = (bf16[128,1024]{1,0:T(8,128)(2,1)S(1)}, bf16[128,1024]{1,0:T(8,128)(2,1)}, u32[]{:S(2)}) copy-start(bf16[128,1024]{1,0:T(8,128)(2,1)} %param.9) | copy-start | bytes 786436
  0.6 28.9 %copy-start.12 = (s32[128]{0:T(128)S(1)}, s32[128]{0:T(128)}, u32[]{:S(2)}) copy-start(s32[128]{0:T(128)} %param.12) | copy-start | bytes 1540
  0.7 29.0 %copy-start.10 = (f32[2,4096]{1,0:T(2,128)S(1)}, f32[2,4096]{1,0:T(2,128)}, u32[]{:S(2)}) copy-start(f32[2,4096]{1,0:T(2,128)} %param.13) | copy-start | bytes 98308
  0.7 102.1 %collective-permute-start.2 = (bf16[128,1024]{1,0:T(8,128)(2,1)}, bf16[128,1024]{1,0:T(8,128)(2,1)}, u32[]{:S(2)}, u32[]{:S(2)}) collective-permute-start(bf16[128,1024]{1,0:T(8,128)(2,1)} %param.10), channel_id=1, source_target_pairs={{0,2},{1,3},{2,4},{3,5},{4,6},{5,7},{6,8},{7,9},{8,10},{9,11},{10,... | collective-permute-start | bytes 786440 | tf_op jit(solution)/shard_map/ppermute | solution.py:18
  6.0 95.1 %collective-permute-start.1 = (bf16[128,1024]{1,0:T(8,128)(2,1)}, bf16[128,1024]{1,0:T(8,128)(2,1)}, u32[]{:S(2)}, u32[]{:S(2)}) collective-permute-start(bf16[128,1024]{1,0:T(8,128)(2,1)} %param.10), channel_id=1, source_target_pairs={{0,3},{1,4},{2,5},{3,6},{4,7},{5,8},{6,9},{7,10},{8,11},{9,12},{10... | collective-permute-start | bytes 786440 | tf_op jit(solution)/shard_map/ppermute | solution.py:18
  15.8 62.8 %collective-permute-start.6 = (bf16[128,1024]{1,0:T(8,128)(2,1)S(1)}, bf16[128,1024]{1,0:T(8,128)(2,1)}, u32[]{:S(2)}, u32[]{:S(2)}) collective-permute-start(bf16[128,1024]{1,0:T(8,128)(2,1)S(1)} %multiply_convert_fusion.1), channel_id=1, source_target_pairs={{0,2},{1,3},{2,4},{3,5},{4,6},{5,7},{6,8},{7,9},{8,10},{9,11},{10,... | collective-permute-start | bytes 786440 | tf_op jit(solution)/shard_map/ppermute | solution.py:18
  19.2 63.5 %collective-permute-start.5 = (bf16[128,1024]{1,0:T(8,128)(2,1)S(1)}, bf16[128,1024]{1,0:T(8,128)(2,1)}, u32[]{:S(2)}, u32[]{:S(2)}) collective-permute-start(bf16[128,1024]{1,0:T(8,128)(2,1)S(1)} %multiply_convert_fusion.1), channel_id=1, source_target_pairs={{0,3},{1,4},{2,5},{3,6},{4,7},{5,8},{6,9},{7,10},{8,11},{9,12},{10... | collective-permute-start | bytes 786440 | tf_op jit(solution)/shard_map/ppermute | solution.py:18
  22.2 52.8 %collective-permute-start.4 = (bf16[128,1024]{1,0:T(8,128)(2,1)S(1)}, bf16[128,1024]{1,0:T(8,128)(2,1)}, u32[]{:S(2)}, u32[]{:S(2)}) collective-permute-start(bf16[128,1024]{1,0:T(8,128)(2,1)S(1)} %multiply_convert_fusion.1), channel_id=1, source_target_pairs={{0,4},{1,5},{2,6},{3,7},{4,8},{5,9},{6,10},{7,11},{8,12},{9,13},{1... | collective-permute-start | bytes 786440 | tf_op jit(solution)/shard_map/ppermute | solution.py:18
  32.3 46.3 %copy-start.9 = (bf16[128,1024]{1,0:T(8,128)(2,1)S(1)}, bf16[128,1024]{1,0:T(8,128)(2,1)}, u32[]{:S(2)}) copy-start(bf16[128,1024]{1,0:T(8,128)(2,1)} %param.10) | copy-start | bytes 786436
  75.0 21.1 %collective-permute-start.7 = (bf16[128,1024]{1,0:T(8,128)(2,1)S(1)}, bf16[128,1024]{1,0:T(8,128)(2,1)S(1)}, u32[]{:S(2)}, u32[]{:S(2)}) collective-permute-start(bf16[128,1024]{1,0:T(8,128)(2,1)S(1)} %multiply_convert_fusion.1), channel_id=1, source_target_pairs={{0,1},{1,2},{2,3},{3,4},{4,5},{5,6},{6,7},{7,8},{8,9},{9,10},{10,1... | collective-permute-start | bytes 786440 | tf_op jit(solution)/shard_map/ppermute | solution.py:18
  78.7 18.9 %collective-permute-start = (bf16[128,1024]{1,0:T(8,128)(2,1)S(1)}, bf16[128,1024]{1,0:T(8,128)(2,1)S(1)}, u32[]{:S(2)}, u32[]{:S(2)}) collective-permute-start(bf16[128,1024]{1,0:T(8,128)(2,1)S(1)} %copy-done.9), channel_id=1, source_target_pairs={{0,4},{1,5},{2,6},{3,7},{4,8},{5,9},{6,10},{7,11},{8,12},{9,13},{1... | collective-permute-start | bytes 786440 | tf_op jit(solution)/shard_map/ppermute | solution.py:18
  82.7 24.8 %collective-permute-start.3 = (bf16[128,1024]{1,0:T(8,128)(2,1)S(1)}, bf16[128,1024]{1,0:T(8,128)(2,1)}, u32[]{:S(2)}, u32[]{:S(2)}) collective-permute-start(bf16[128,1024]{1,0:T(8,128)(2,1)S(1)} %copy-done.9), channel_id=1, source_target_pairs={{0,1},{1,2},{2,3},{3,4},{4,5},{5,6},{6,7},{7,8},{8,9},{9,10},{10,1... | collective-permute-start | bytes 786440 | tf_op jit(solution)/shard_map/ppermute | solution.py:18
  134.8 10.2 %slice-start = ((s8[5242880]{0:T(1024)(128)(4,1)}), s8[1048576]{0:T(1024)(128)(4,1)S(1)}, s32[]{:S(2)}) async-start(s8[5242880]{0:T(1024)(128)(4,1)} %bitcast.118), calls=%async_computation | async-start | bytes 2097152
  160.2 16.3 %copy-start.6 = (f32[640,8,128]{2,0,1:T(8,128)S(1)}, f32[640,8,128]{2,0,1:T(8,128)}, u32[]{:S(2)}) copy-start(f32[640,8,128]{2,0,1:T(8,128)} %bitcast_reduce_fusion) | copy-start | bytes 7864324
  160.7 25.1 %collective-permute-start.8 = (bf16[128,8,128]{0,2,1:T(8,128)(2,1)S(1)}, bf16[128,8,128]{0,2,1:T(8,128)(2,1)S(1)}, u32[]{:S(2)}, u32[]{:S(2)}) collective-permute-start(bf16[128,8,128]{0,2,1:T(8,128)(2,1)S(1)} %get-tuple-element.79), channel_id=1, source_target_pairs={{4,0},{5,1},{6,2},{7,3},{8,4},{9,5},{10,6},{11,7},{12,8},{13,9},{1... | collective-permute-start | bytes 786440 | tf_op jit(solution)/shard_map/ppermute | solution.py:18
  164.9 22.9 %collective-permute-start.11 = (bf16[128,8,128]{0,2,1:T(8,128)(2,1)S(1)}, bf16[128,8,128]{0,2,1:T(8,128)(2,1)S(1)}, u32[]{:S(2)}, u32[]{:S(2)}) collective-permute-start(bf16[128,8,128]{0,2,1:T(8,128)(2,1)S(1)} %get-tuple-element.80), channel_id=1, source_target_pairs={{1,0},{2,1},{3,2},{4,3},{5,4},{6,5},{7,6},{8,7},{9,8},{10,9},{11,1... | collective-permute-start | bytes 786440 | tf_op jit(solution)/shard_map/ppermute | solution.py:18
  166.8 31.6 %collective-permute-start.10 = (bf16[128,8,128]{0,2,1:T(8,128)(2,1)S(1)}, bf16[128,8,128]{0,2,1:T(8,128)(2,1)S(1)}, u32[]{:S(2)}, u32[]{:S(2)}) collective-permute-start(bf16[128,8,128]{0,2,1:T(8,128)(2,1)S(1)} %get-tuple-element.81), channel_id=1, source_target_pairs={{2,0},{3,1},{4,2},{5,3},{6,4},{7,5},{8,6},{9,7},{10,8},{11,9},{12,... | collective-permute-start | bytes 786440 | tf_op jit(solution)/shard_map/ppermute | solution.py:18
  174.0 10.7 %copy-start.1 = (f32[128,32,128]{0,2,1:T(8,128)S(1)}, f32[128,32,128]{0,2,1:T(8,128)}, u32[]{:S(2)}) copy-start(f32[128,32,128]{0,2,1:T(8,128)} %get-tuple-element.73) | copy-start | bytes 6291460
  174.0 10.7 %copy-start.11 = (s32[128]{0:T(128)S(1)}, s32[128]{0:T(128)}, u32[]{:S(2)}) copy-start(s32[128]{0:T(128)} %param.11) | copy-start | bytes 1540
  174.0 38.3 %collective-permute-start.9 = (bf16[128,8,128]{0,2,1:T(8,128)(2,1)S(1)}, bf16[128,8,128]{0,2,1:T(8,128)(2,1)S(1)}, u32[]{:S(2)}, u32[]{:S(2)}) collective-permute-start(bf16[128,8,128]{0,2,1:T(8,128)(2,1)S(1)} %get-tuple-element.82), channel_id=1, source_target_pairs={{3,0},{4,1},{5,2},{6,3},{7,4},{8,5},{9,6},{10,7},{11,8},{12,9},{13... | collective-permute-start | bytes 786440 | tf_op jit(solution)/shard_map/ppermute | solution.py:18
  177.8 37.5 %collective-permute-start.12 = (bf16[128,8,128]{2,0,1:T(8,128)(2,1)}, bf16[128,8,128]{2,0,1:T(8,128)(2,1)S(1)}, u32[]{:S(2)}, u32[]{:S(2)}) collective-permute-start(bf16[128,8,128]{2,0,1:T(8,128)(2,1)} %get-tuple-element.75), channel_id=1, source_target_pairs={{4,0},{5,1},{6,2},{7,3},{8,4},{9,5},{10,6},{11,7},{12,8},{13,9},{1... | collective-permute-start | bytes 786440 | tf_op jit(solution)/shard_map/ppermute | solution.py:18
  185.8 44.5 %collective-permute-start.15 = (bf16[128,8,128]{2,0,1:T(8,128)(2,1)}, bf16[128,8,128]{2,0,1:T(8,128)(2,1)}, u32[]{:S(2)}, u32[]{:S(2)}) collective-permute-start(bf16[128,8,128]{2,0,1:T(8,128)(2,1)} %get-tuple-element.76), channel_id=1, source_target_pairs={{1,0},{2,1},{3,2},{4,3},{5,4},{6,5},{7,6},{8,7},{9,8},{10,9},{11,1... | collective-permute-start | bytes 786440 | tf_op jit(solution)/shard_map/ppermute | solution.py:18
  187.8 55.6 %collective-permute-start.14 = (bf16[128,8,128]{2,0,1:T(8,128)(2,1)}, bf16[128,8,128]{2,0,1:T(8,128)(2,1)}, u32[]{:S(2)}, u32[]{:S(2)}) collective-permute-start(bf16[128,8,128]{2,0,1:T(8,128)(2,1)} %get-tuple-element.77), channel_id=1, source_target_pairs={{2,0},{3,1},{4,2},{5,3},{6,4},{7,5},{8,6},{9,7},{10,8},{11,9},{12,... | collective-permute-start | bytes 786440 | tf_op jit(solution)/shard_map/ppermute | solution.py:18
  198.4 51.2 %collective-permute-start.13 = (bf16[128,8,128]{2,0,1:T(8,128)(2,1)}, bf16[128,8,128]{2,0,1:T(8,128)(2,1)}, u32[]{:S(2)}, u32[]{:S(2)}) collective-permute-start(bf16[128,8,128]{2,0,1:T(8,128)(2,1)} %get-tuple-element.78), channel_id=1, source_target_pairs={{3,0},{4,1},{5,2},{6,3},{7,4},{8,5},{9,6},{10,7},{11,8},{12,9},{13... | collective-permute-start | bytes 786440 | tf_op jit(solution)/shard_map/ppermute | solution.py:18
  (7 other events, 33.5 us)

commit v2 on v1

v2 whole, which is shorter than its diff:
```python
import functools
import math

import jax
import jax.numpy as jnp
from jax import lax
from jax.experimental import pallas as pl
from jax.experimental.pallas import tpu as pltpu
from jax.sharding import PartitionSpec as P

HD = 128
MOST = 512
EPS = 1e-06
AXES = ("seq", "head")
CHUNKS = 2
SLAB = 2
FAR = -1e30


def shifted(value, steps):
    count = lax.axis_size(AXES)
    first, last = (max(0, -steps), min(count, count - steps))
    return lax.ppermute(value, AXES, [(source, source + steps) for source in range(first, last)])


def clip_start(clip_lengths, positions):
    order = jnp.arange(clip_lengths.shape[0], dtype=jnp.int32)
    begins = jnp.sum(jnp.where(order[None, :] < order[:, None], clip_lengths[None, :], 0), axis=1)
    chosen = jnp.where(
        begins[None, :] <= positions[:, None], begins[None, :], jnp.zeros((), jnp.int32)
    )
    return jnp.max(chosen, axis=1)


def nn(a, b):
    return lax.dot_general(a, b, (((1,), (0,)), ((), ())), preferred_element_type=jnp.float32)


def nt(a, b):
    return lax.dot_general(a, b, (((1,), (1,)), ((), ())), preferred_element_type=jnp.float32)


def modality_sums(picks, terms):
    return lax.dot_general(
        picks,
        terms,
        (((1,), (1,)), ((), ())),
        precision=lax.Precision.HIGHEST,
        preferred_element_type=jnp.float32,
    )


def attend_kernel(depth, repeat, aliased, *refs):
    blocks = depth + 1
    starts, mod_row, queries, grads, query_gain, key_gain = refs[:6]
    key_refs = refs[6 : 6 + blocks]
    value_refs = refs[6 + blocks : 6 + 2 * blocks]
    mod_refs = refs[6 + 2 * blocks : 6 + 3 * blocks]
    rest = refs[6 + 3 * blocks + (2 if aliased else 0) :]
    attended, query_back = rest[:2]
    back_refs = rest[2 : 2 + blocks]
    query_sums, key_sums, bias = rest[2 + blocks :]
    rows = queries.shape[0]
    span = blocks * rows
    scale = 1.0 / math.sqrt(HD)
    width = SLAB * HD

    @pl.when(pl.program_id(0) == 0)
    def _():
        key_at = lax.broadcasted_iota(jnp.int32, (span, rows), 0)
        query_at = lax.broadcasted_iota(jnp.int32, (span, rows), 1) + depth * rows
        allowed = (key_at >= starts[...]) & (key_at <= query_at)
        bias[...] = jnp.where(allowed, 0.0, FAR)

    key_raw = jnp.concatenate([r[...] for r in key_refs], 0).astype(jnp.float32)
    key_factor = lax.rsqrt(jnp.mean(key_raw * key_raw, axis=1, keepdims=True) + EPS)
    key_unit = key_raw * key_factor
    key_mod = jnp.concatenate([r[...] for r in mod_refs], 0).astype(jnp.float32) > 0.5
    key_norm = (key_unit * jnp.where(key_mod, key_gain[1:2, :], key_gain[0:1, :])).astype(
        jnp.bfloat16
    )
    value = jnp.concatenate([r[...] for r in value_refs], 0)
    key_turned = key_norm.T
    value_turned = value.T
    motion = mod_row[...] == 1
    kinds = lax.broadcasted_iota(jnp.int32, (8, rows), 0)
    picks = (kinds == mod_row[...]).astype(jnp.float32)

    key_acc = None
    value_acc = None
    for slab in range(repeat // SLAB):
        heads = [slab * SLAB + n for n in range(SLAB)]

        def turned(ref):
            return jnp.concatenate(
                [ref[:, h * HD : (h + 1) * HD].astype(jnp.float32).T for h in heads], 1
            )

        raw = turned(queries)
        grad = turned(grads)
        grad_low = grad.astype(jnp.bfloat16)
        factor = lax.rsqrt(jnp.mean(raw * raw, axis=0, keepdims=True) + EPS)
        unit = raw * factor
        gain = jnp.concatenate(
            [
                jnp.where(
                    motion,
                    query_gain[h * HD : (h + 1) * HD, 1:2],
                    query_gain[h * HD : (h + 1) * HD, 0:1],
                )
                for h in heads
            ],
            1,
        )
        query_norm = (unit * gain).astype(jnp.bfloat16)
        shield = jnp.concatenate([bias[...]] * SLAB, 1)
        scores = nn(key_norm, query_norm) * (scale * math.log2(math.e)) + shield
        expo = jnp.exp2(scores - jnp.max(scores, axis=0, keepdims=True))
        probs = expo * (1.0 / jnp.sum(expo, axis=0, keepdims=True))
        probs_low = probs.astype(jnp.bfloat16)
        seen = nn(value_turned, probs_low).astype(jnp.bfloat16)
        seen_wide = seen.astype(jnp.float32)
        delta = jnp.sum(grad * seen_wide, axis=0, keepdims=True)
        prob_grad = nn(value, grad_low)
        score_grad = (probs * (prob_grad - delta) * scale).astype(jnp.bfloat16)
        low = nn(key_turned, score_grad).astype(jnp.bfloat16).astype(jnp.float32)
        along = low * gain
        back = factor * (along - unit * jnp.mean(along * unit, axis=0, keepdims=True))
        term = low * unit
        for n, h in enumerate(heads):
            part = slice(n * HD, (n + 1) * HD)
            cols = slice(h * HD, (h + 1) * HD)
            attended[:, cols] = seen_wide[:, part].T.astype(jnp.bfloat16)
            query_back[:, cols] = back[:, part].T.astype(jnp.bfloat16)
            query_sums[:, cols] = modality_sums(picks, term[:, part])
        key_step = nt(score_grad, query_norm)
        value_step = nt(probs_low, grad_low)
        key_acc = key_step if key_acc is None else key_acc + key_step
        value_acc = value_step if value_acc is None else value_acc + value_step

    for n, ref in enumerate(back_refs):
        part = slice(n * rows, (n + 1) * rows)
        ref[:, :HD] = key_acc[part].astype(ref.dtype)
        ref[:, HD:] = value_acc[part].astype(ref.dtype)
    term = key_acc * key_unit
    of_motion = jnp.sum(jnp.where(key_mod, term, 0.0), axis=0, keepdims=True)
    of_text = jnp.sum(jnp.where(key_mod, 0.0, term), axis=0, keepdims=True)
    lines = lax.broadcasted_iota(jnp.int32, (8, HD), 0)
    key_sums[...] = jnp.where(lines == 0, of_text, jnp.where(lines == 1, of_motion, 0.0))


def attend(first_head, kv, starts, mod_row, queries, grads, query_gain, key_gain, held, mods, before):
    rows, width = queries.shape
    repeat = width // HD // (key_gain.shape[1] // HD)
    blocks = len(held)
    group = repeat * HD

    def at(shape, index):
        return pl.BlockSpec(shape, index)

    whole = lambda g: (0, 0)
    here = lambda g: (0, first_head + g)
    in_specs = [
        at((1, rows), whole),
        at((1, rows), whole),
        at((rows, group), here),
        at((rows, group), here),
        at((group, 2), lambda g: (first_head + g, 0)),
        at((2, HD), here),
    ]
    in_specs += [at((rows, HD), lambda g: (0, g))] * blocks
    in_specs += [at((rows, HD), lambda g: (0, kv + g))] * blocks
    in_specs += [at((rows, HD), lambda g, lane=mods[1]: (0, lane))] * blocks
    operands = [starts, mod_row, queries, grads, query_gain, key_gain, *held, *held, *mods[0]]
    aliases = {}
    if before is not None:
        aliases = {len(operands): 0, len(operands) + 1: 1}
        operands += list(before)
        in_specs += [pl.BlockSpec(memory_space=pl.ANY)] * 2
    big = jax.ShapeDtypeStruct((rows, width), jnp.bfloat16)
    pair = lambda dtype: jax.ShapeDtypeStruct((rows, kv * 2 * HD), dtype)
    outs = [big, big, pair(jnp.bfloat16)] + [pair(jnp.float32)] * (blocks - 1)
    outs += [
        jax.ShapeDtypeStruct((8, kv * group), jnp.float32),
        jax.ShapeDtypeStruct((8, kv * HD), jnp.float32),
    ]
    out_specs = [at((rows, group), here)] * 2
    out_specs += [at((rows, 2 * HD), lambda g: (0, g))] * blocks
    out_specs += [at((8, group), lambda g: (0, g)), at((8, HD), lambda g: (0, g))]
    return pl.pallas_call(
        functools.partial(attend_kernel, blocks - 1, repeat, before is not None),
        grid=(kv,),
        in_specs=in_specs,
        out_specs=out_specs,
        out_shape=outs,
        scratch_shapes=[pltpu.VMEM((blocks * rows, rows), jnp.float32)],
        input_output_aliases=aliases,
        compiler_params=pltpu.CompilerParams(vmem_limit_bytes=40 * 1024 * 1024),
        cost_estimate=pl.CostEstimate(
            flops=kv * repeat * 12 * rows * blocks * rows * HD,
            bytes_accessed=kv * group * rows * 8 + blocks * rows * kv * HD * 12,
            transcendentals=kv * repeat * rows * blocks * rows,
        ),
        name="attend",
    )(*operands)


def finish_kernel(arrived, own, keys, mod, key_gain, key_back, value_back):
    total = arrived[...].astype(jnp.float32) + own[...]
    low = total[:, :HD].astype(jnp.bfloat16).astype(jnp.float32)
    raw = keys[...].astype(jnp.float32)
    factor = lax.rsqrt(jnp.mean(raw * raw, axis=1, keepdims=True) + EPS)
    unit = raw * factor
    gain = jnp.where(mod[...].astype(jnp.float32) > 0.5, key_gain[1:2, :], key_gain[0:1, :])
    along = low * gain
    back = factor * (along - unit * jnp.mean(along * unit, axis=1, keepdims=True))
    key_back[...] = back.astype(jnp.bfloat16)
    value_back[...] = total[:, HD:].astype(jnp.bfloat16)


def finish(first_head, kv, arrived, own, keys, mods, key_gain):
    rows = keys.shape[0]
    here = lambda g: (0, first_head + g)
    low = jax.ShapeDtypeStruct((rows, kv * HD), jnp.bfloat16)
    return pl.pallas_call(
        finish_kernel,
        grid=(kv,),
        in_specs=[
            pl.BlockSpec((rows, 2 * HD), lambda g: (0, g)),
            pl.BlockSpec((rows, 2 * HD), lambda g: (0, g)),
            pl.BlockSpec((rows, HD), here),
            pl.BlockSpec((rows, HD), lambda g: (0, mods[1])),
            pl.BlockSpec((2, HD), here),
        ],
        out_specs=[pl.BlockSpec((rows, HD), lambda g: (0, g))] * 2,
        out_shape=[low, low],
        name="finish",
    )(arrived, own, keys, mods[0][-1], key_gain)


def summed(value):
    count = lax.axis_size(AXES)
    bit = 1
    while bit < count:
        value = value + lax.ppermute(value, AXES, [(i, i ^ bit) for i in range(count)])
        bit *= 2
    return value


def on_device(queries, keys, values, modality, clip_lengths, query_gains, key_gains, out_grad):
    count, width = queries.shape
    kv_heads = keys.shape[1] // HD
    kv = kv_heads // CHUNKS
    depth = (MOST + count - 1) // count
    first = lax.axis_index(AXES) * count
    mod_lanes = jnp.broadcast_to(modality.astype(jnp.bfloat16)[:, None], (count, HD))
    held = []
    for chunk in range(CHUNKS):
        part = slice(chunk * kv * HD, (chunk + 1) * kv * HD)
        block = [keys[:, part], values[:, part]] + ([mod_lanes] if chunk == 0 else [])
        held.append([jnp.concatenate(block, 1)])
    for chunk in range(CHUNKS):
        for _ in range(depth):
            held[chunk].append(shifted(held[chunk][-1], 1))
    held = [blocks[::-1] for blocks in held]
    mods = (held[0], 2 * kv)

    starts = clip_start(clip_lengths, first + jnp.arange(count, dtype=jnp.int32))
    starts = (starts - first + depth * count)[None, :]
    mod_row = modality[None, :]
    gain_columns = query_gains.T
    before = None
    sums = []
    key_parts = []
    value_parts = []
    rings = []
    for chunk in range(CHUNKS):
        outs = attend(
            chunk * kv,
            kv,
            starts,
            mod_row,
            queries,
            out_grad,
            gain_columns,
            key_gains,
            held[chunk],
            mods,
            before,
        )
        before = outs[:2]
        sums.append(outs[-2:])
        rings.append(outs[2:-2])
    for chunk in range(CHUNKS):
        backs = rings[chunk]
        moving = backs[0]
        for n in range(1, depth + 1):
            moving = shifted(moving, -1)
            if n < depth:
                moving = (moving.astype(jnp.float32) + backs[n]).astype(jnp.bfloat16)
        key_part, value_part = finish(
            chunk * kv, kv, moving, backs[depth], keys, mods, key_gains
        )
        key_parts.append(key_part)
        value_parts.append(value_part)
    attended, query_grad = before
    gains = jnp.concatenate([q[:2] for q, _ in sums] + [k[:2] for _, k in sums], 1)
    gains = summed(gains.reshape(-1, HD)).reshape(2, -1)
    return (
        attended,
        query_grad,
        jnp.concatenate(key_parts, 1),
        jnp.concatenate(value_parts, 1),
        gains[:, :width],
        gains[:, width:],
    )


def solution(mesh):
    rows = P(AXES, None)
    return jax.shard_map(
        on_device,
        mesh=mesh,
        in_specs=(rows, rows, rows, P(AXES), P(), P(), P(), rows),
        out_specs=(rows, rows, rows, rows, P(), P()),
        check_vma=False,
    )
```

time: 339 us -> 196 us (0.58)
  blocking collectives: 84 us -> 0 us
  Pallas kernels: 0 us -> 37.3 us
  matrix products: 32.2 us -> 0 us
  local copies, waits for them, and re-layouts: 36.7 us -> 10.8 us
  waiting for transfers between devices: 96.5 us -> 73.7 us
  other arithmetic: 14.2 us -> 5.82 us
  starting transfers between devices: 71.3 us -> 66 us
    psum x1 -> x0, blocking collectives: 84 us -> none  [on_device(): lax.psum((query_gain, key_gain), ('seq', 'head'))]
    pallas_call x0 -> x4, Pallas kernels: none -> 37.3 us  [the longest x2 30.3 us: attend(): pl.pallas_call(functools.partial(attend_kernel, blocks - 1, repeat, befor...]
    ppermute x16 -> x24, waiting for transfers between devices: 96.5 us -> 73.7 us  [the longest x16 48.1 us: shifted(): lax.ppermute(value, AXES, [(source, source + steps) for source in range(f...]
    dot_general x7 -> x0, matrix products: 22.8 us -> none  [the longest x1 6.78 us: visit(): jnp.einsum('qnd,knd->qnk', grad_rows, value_ext, preferred_element_type=j...]
    unnamed x48 -> x43, local copies, waits for them, and re-layouts: 20.5 us -> 8.3 us
    broadcast_in_dim x4 -> x1, local copies, waits for them, and re-layouts: 9.7 us -> 0.08 us  [on_device(): jnp.broadcast_to(modality.astype(jnp.bfloat16)[:, None], (count, HD))]
    sub x1 -> x0, matrix products: 9.41 us -> none  [visit(): expo = jnp.exp(scores - top)]
    ppermute x16 -> x24, starting transfers between devices: 71.3 us -> 66 us  [the longest x16 63.2 us: shifted(): lax.ppermute(value, AXES, [(source, source + steps) for source in range(f...]
  transfers between devices with their start and end apart: 16 -> 24, of which waited for: 7 -> 15; matrix products, arithmetic and copies ran while one was open for 8% -> 2% of each run, Pallas kernels for 0% -> 10%
where the time goes in v2:
time: 196 us; the launch traced here: 195 us
  waiting for transfers between devices  73.7 us (38%)
  starting transfers between devices  66 us (34%)
  Pallas kernels  37.3 us (19%)
  local copies, waits for them, and re-layouts  10.8 us (6%)
  other arithmetic  5.82 us (3%)
    ppermute x16, starting transfers between devices, shifted(): lax.ppermute(value, AXES, [(source, source + steps) for source in range(f...  63.2 us
    ppermute x16, waiting for transfers between devices, shifted(): lax.ppermute(value, AXES, [(source, source + steps) for source in range(f...  48.1 us
    pallas_call x2, Pallas kernels, attend(): pl.pallas_call(functools.partial(attend_kernel, blocks - 1, repeat, befor...  30.3 us
    ppermute x8, waiting for transfers between devices, summed(): lax.ppermute(value, AXES, [(i, i ^ bit) for i in range(count)])  25.6 us
    unnamed x43, local copies, waits for them, and re-layouts  8.3 us
    pallas_call x2, Pallas kernels, finish(): pl.pallas_call(finish_kernel, grid=(kv,), in_specs=[pl.BlockSpec((rows, 2...  7.01 us
  transfers between devices with their start and end apart: 24, of which 15 were waited for; matrix products, arithmetic and copies ran while one was open for 2% of the time, Pallas kernels for 10%

profile of v2, /device:TPU:2, one launch (start us, length us, event | category | flops | bytes accessed | tf_op | source)
XLA Modules:
  0.0 194.8 jit_solution(12770696116245032333)
XLA Ops:
  2.6 3.8 %collective-permute-start.4 = (bf16[128,1152]{1,0:T(8,128)(2,1)S(1)}, bf16[128,1152]{1,0:T(8,128)(2,1)S(1)}, u32[]{:S(2)}, u32[]{:S(2)}) collective-permute-start(bf16[128,1152]{1,0:T(8,128)(2,1)S(1)} %pad_maximum_fusion.refs_10_.refs_15_.refs_20_.mod), channel_id=1, source_target_pairs={{0,1},{1,2},{2,3},{3,4},{4,5},{5,6},{6,7},{7,8},{8,9},{9,10},{10,1... | collective-permute-start | bytes 884744 | tf_op jit(solution)/shard_map/ppermute | solution.py:23
  6.5 3.8 %collective-permute-start = (bf16[128,1024]{1,0:T(8,128)(2,1)S(1)}, bf16[128,1024]{1,0:T(8,128)(2,1)S(1)}, u32[]{:S(2)}, u32[]{:S(2)}) collective-permute-start(bf16[128,1024]{1,0:T(8,128)(2,1)S(1)} %pad_maximum_fusion.1.refs_10_.refs_15_), channel_id=1, source_target_pairs={{0,1},{1,2},{2,3},{3,4},{4,5},{5,6},{6,7},{7,8},{8,9},{9,10},{10,1... | collective-permute-start | bytes 786440 | tf_op jit(solution)/shard_map/ppermute | solution.py:23
  10.3 8.7 %collective-permute-done.4.refs_9_.refs_14_.refs_19_ = bf16[128,1152]{1,0:T(8,128)(2,1)S(1)} collective-permute-done((bf16[128,1152]{1,0:T(8,128)(2,1)S(1)}, bf16[128,1152]{1,0:T(8,128)(2,1)S(1)}, u32[]{:S(2)}, u32[]{:S(2)}) %collective-permute-start.4) | collective-permute-done | bytes 294944 | tf_op jit(solution)/shard_map/ppermute | solution.py:23
  20.9 3.7 %collective-permute-done.refs_9_.refs_14_ = bf16[128,1024]{1,0:T(8,128)(2,1)S(1)} collective-permute-done((bf16[128,1024]{1,0:T(8,128)(2,1)S(1)}, bf16[128,1024]{1,0:T(8,128)(2,1)S(1)}, u32[]{:S(2)}, u32[]{:S(2)}) %collective-permute-start) | collective-permute-done | bytes 262176 | tf_op jit(solution)/shard_map/ppermute | solution.py:23
  27.2 6.6 %collective-permute-done.5.refs_8_.refs_13_.refs_18_ = bf16[128,1152]{1,0:T(8,128)(2,1)S(1)} collective-permute-done((bf16[128,1152]{1,0:T(8,128)(2,1)S(1)}, bf16[128,1152]{1,0:T(8,128)(2,1)S(1)}, u32[]{:S(2)}, u32[]{:S(2)}) %collective-permute-start.5) | collective-permute-done | bytes 294944 | tf_op jit(solution)/shard_map/ppermute | solution.py:23
  35.7 3.8 %collective-permute-done.1.refs_8_.refs_13_ = bf16[128,1024]{1,0:T(8,128)(2,1)S(1)} collective-permute-done((bf16[128,1024]{1,0:T(8,128)(2,1)S(1)}, bf16[128,1024]{1,0:T(8,128)(2,1)S(1)}, u32[]{:S(2)}, u32[]{:S(2)}) %collective-permute-start.1) | collective-permute-done | bytes 262176 | tf_op jit(solution)/shard_map/ppermute | solution.py:23
  42.3 6.8 %collective-permute-done.6.refs_7_.refs_12_.refs_17_ = bf16[128,1152]{1,0:T(8,128)(2,1)S(1)} collective-permute-done((bf16[128,1152]{1,0:T(8,128)(2,1)S(1)}, bf16[128,1152]{1,0:T(8,128)(2,1)S(1)}, u32[]{:S(2)}, u32[]{:S(2)}) %collective-permute-start.6) | collective-permute-done | bytes 294944 | tf_op jit(solution)/shard_map/ppermute | solution.py:23
  51.2 3.8 %collective-permute-done.2.refs_7_.refs_12_ = bf16[128,1024]{1,0:T(8,128)(2,1)} collective-permute-done((bf16[128,1024]{1,0:T(8,128)(2,1)S(1)}, bf16[128,1024]{1,0:T(8,128)(2,1)}, u32[]{:S(2)}, u32[]{:S(2)}) %collective-permute-start.2) | collective-permute-done | bytes 262176 | tf_op jit(solution)/shard_map/ppermute | solution.py:23
  58.3 6.3 %collective-permute-done.7.refs_6_.refs_11_.refs_16_ = bf16[128,1152]{1,0:T(8,128)(2,1)} collective-permute-done((bf16[128,1152]{1,0:T(8,128)(2,1)S(1)}, bf16[128,1152]{1,0:T(8,128)(2,1)}, u32[]{:S(2)}, u32[]{:S(2)}) %collective-permute-start.7) | collective-permute-done | bytes 294944 | tf_op jit(solution)/shard_map/ppermute | solution.py:23
  67.0 15.1 %attend.2 = (bf16[128,4096]{1,0:T(8,128)(2,1)}, bf16[128,4096]{1,0:T(8,128)(2,1)}, bf16[128,1024]{1,0:T(8,128)(2,1)S(1)}, f32[128,1024]{1,0:T(8,128)S(1)}, f32[1...) custom-call(s32[1,128]{1,0:T(1,128)S(1)} %add_bitcast_fusion.refs_0_, ...), custom_call_target="tpu_custom_call" | custom-call | flops 2013265920 | bytes 6029312 | tf_op jit(solution)/shard_map/attend/pallas_call | solution.py:190
  83.8 15.2 %attend.3 = (bf16[128,4096]{1,0:T(8,128)(2,1)}, bf16[128,4096]{1,0:T(8,128)(2,1)}, bf16[128,1024]{1,0:T(8,128)(2,1)S(1)}, f32[128,1024]{1,0:T(8,128)S(1)}, f32[1...) custom-call(s32[1,128]{1,0:T(1,128)S(1)} %add_bitcast_fusion.refs_0_, ...), custom_call_target="tpu_custom_call", output_to_operand_aliasing={{0}: (21, {}), {1}: (22, {})} | custom-call | flops 2013265920 | bytes 6029312 | tf_op jit(solution)/shard_map/attend/pallas_call | solution.py:190
  103.1 7.2 %collective-permute-done.12 = bf16[128,1024]{1,0:T(8,128)(2,1)S(1)} collective-permute-done((bf16[128,1024]{1,0:T(8,128)(2,1)S(1)}, bf16[128,1024]{1,0:T(8,128)(2,1)S(1)}, u32[]{:S(2)}, u32[]{:S(2)}) %collective-permute-start.12) | collective-permute-done | bytes 262176 | tf_op jit(solution)/shard_map/ppermute | solution.py:23
  110.3 5.8 %collective-permute-start.13 = (bf16[128,1024]{1,0:T(8,128)(2,1)S(1)}, bf16[128,1024]{1,0:T(8,128)(2,1)S(1)}, u32[]{:S(2)}, u32[]{:S(2)}) collective-permute-start(bf16[128,1024]{1,0:T(8,128)(2,1)S(1)} %add_convert_fusion.2), channel_id=1, source_target_pairs={{1,0},{2,1},{3,2},{4,3},{5,4},{6,5},{7,6},{8,7},{9,8},{10,9},{11,1... | collective-permute-start | bytes 786440 | tf_op jit(solution)/shard_map/ppermute | solution.py:23
  116.2 6.0 %collective-permute-start.9 = (bf16[128,1024]{1,0:T(8,128)(2,1)S(1)}, bf16[128,1024]{1,0:T(8,128)(2,1)S(1)}, u32[]{:S(2)}, u32[]{:S(2)}) collective-permute-start(bf16[128,1024]{1,0:T(8,128)(2,1)S(1)} %add_convert_fusion.5), channel_id=1, source_target_pairs={{1,0},{2,1},{3,2},{4,3},{5,4},{6,5},{7,6},{8,7},{9,8},{10,9},{11,1... | collective-permute-start | bytes 786440 | tf_op jit(solution)/shard_map/ppermute | solution.py:23
  123.4 6.7 %collective-permute-start.14 = (bf16[128,1024]{1,0:T(8,128)(2,1)S(1)}, bf16[128,1024]{1,0:T(8,128)(2,1)S(1)}, u32[]{:S(2)}, u32[]{:S(2)}) collective-permute-start(bf16[128,1024]{1,0:T(8,128)(2,1)S(1)} %add_convert_fusion.1), channel_id=1, source_target_pairs={{1,0},{2,1},{3,2},{4,3},{5,4},{6,5},{7,6},{8,7},{9,8},{10,9},{11,1... | collective-permute-start | bytes 786440 | tf_op jit(solution)/shard_map/ppermute | solution.py:23
  130.2 7.7 %collective-permute-start.10 = (bf16[128,1024]{1,0:T(8,128)(2,1)S(1)}, bf16[128,1024]{1,0:T(8,128)(2,1)S(1)}, u32[]{:S(2)}, u32[]{:S(2)}) collective-permute-start(bf16[128,1024]{1,0:T(8,128)(2,1)S(1)} %add_convert_fusion.4), channel_id=1, source_target_pairs={{1,0},{2,1},{3,2},{4,3},{5,4},{6,5},{7,6},{8,7},{9,8},{10,9},{11,1... | collective-permute-start | bytes 786440 | tf_op jit(solution)/shard_map/ppermute | solution.py:23
  138.2 4.9 %collective-permute-start.15 = (bf16[128,1024]{1,0:T(8,128)(2,1)S(1)}, bf16[128,1024]{1,0:T(8,128)(2,1)S(1)}, u32[]{:S(2)}, u32[]{:S(2)}) collective-permute-start(bf16[128,1024]{1,0:T(8,128)(2,1)S(1)} %add_convert_fusion), channel_id=1, source_target_pairs={{1,0},{2,1},{3,2},{4,3},{5,4},{6,5},{7,6},{8,7},{9,8},{10,9},{11,1... | collective-permute-start | bytes 786440 | tf_op jit(solution)/shard_map/ppermute | solution.py:23
  144.4 9.0 %collective-permute-start.11 = (bf16[128,1024]{1,0:T(8,128)(2,1)S(1)}, bf16[128,1024]{1,0:T(8,128)(2,1)S(1)}, u32[]{:S(2)}, u32[]{:S(2)}) collective-permute-start(bf16[128,1024]{1,0:T(8,128)(2,1)S(1)} %add_convert_fusion.3), channel_id=1, source_target_pairs={{1,0},{2,1},{3,2},{4,3},{5,4},{6,5},{7,6},{8,7},{9,8},{10,9},{11,1... | collective-permute-start | bytes 786440 | tf_op jit(solution)/shard_map/ppermute | solution.py:23
  153.6 7.9 %collective-permute-done.18 = f32[80,128]{1,0:T(8,128)S(1)} collective-permute-done((f32[80,128]{1,0:T(8,128)S(1)}, f32[80,128]{1,0:T(8,128)S(1)}, u32[]{:S(2)}, u32[]{:S(2)}) %collective-permute-start.18) | collective-permute-done | bytes 40992 | tf_op jit(solution)/shard_map/ppermute | solution.py:245
  161.5 4.0 %collective-permute-done.19 = f32[80,128]{1,0:T(8,128)S(1)} collective-permute-done((f32[80,128]{1,0:T(8,128)S(1)}, f32[80,128]{1,0:T(8,128)S(1)}, u32[]{:S(2)}, u32[]{:S(2)}) %collective-permute-start.19) | collective-permute-done | bytes 40992 | tf_op jit(solution)/shard_map/ppermute | solution.py:245
  165.5 5.5 %collective-permute-done.20 = f32[80,128]{1,0:T(8,128)S(1)} collective-permute-done((f32[80,128]{1,0:T(8,128)S(1)}, f32[80,128]{1,0:T(8,128)S(1)}, u32[]{:S(2)}, u32[]{:S(2)}) %collective-permute-start.20) | collective-permute-done | bytes 40992 | tf_op jit(solution)/shard_map/ppermute | solution.py:245
  172.2 4.0 %collective-permute-done.22 = f32[80,128]{1,0:T(8,128)S(1)} collective-permute-done((f32[80,128]{1,0:T(8,128)S(1)}, f32[80,128]{1,0:T(8,128)S(1)}, u32[]{:S(2)}, u32[]{:S(2)}) %collective-permute-start.22) | collective-permute-done | bytes 40992 | tf_op jit(solution)/shard_map/ppermute | solution.py:245
  183.7 3.5 %finish.3 = (bf16[128,512]{1,0:T(8,128)(2,1)}, bf16[128,512]{1,0:T(8,128)(2,1)}) custom-call(bf16[128,1024]{1,0:T(8,128)(2,1)} %copy-done.18, f32[128,1024]{1,0:T(8,128)} %copy-done.15, bf16[128,1024]{1,0:T(8,128)(2,1)} %keys.3, bf16[128,1152]{1,0:T(8,128)(2,1)} %copy-done, f32[2,1024]{1,0:T(2,128)} %key_gain.3), custom_call_target="tpu_custom_call" | custom-call | tf_op jit(solution)/shard_map/finish/pallas_call | solution.py:225
  187.9 3.5 %finish.2 = (bf16[128,512]{1,0:T(8,128)(2,1)}, bf16[128,512]{1,0:T(8,128)(2,1)}) custom-call(bf16[128,1024]{1,0:T(8,128)(2,1)} %copy-done.19, f32[128,1024]{1,0:T(8,128)} %copy-done.14, bf16[128,1024]{1,0:T(8,128)(2,1)} %keys.3, bf16[128,1152]{1,0:T(8,128)(2,1)} %copy-done, f32[2,1024]{1,0:T(2,128)} %key_gain.3), custom_call_target="tpu_custom_call" | custom-call | tf_op jit(solution)/shard_map/finish/pallas_call | solution.py:225
  (105 shorter events, 40.3 us)
Async XLA Ops:
  2.6 16.4 %collective-permute-start.4 = (bf16[128,1152]{1,0:T(8,128)(2,1)S(1)}, bf16[128,1152]{1,0:T(8,128)(2,1)S(1)}, u32[]{:S(2)}, u32[]{:S(2)}) collective-permute-start(bf16[128,1152]{1,0:T(8,128)(2,1)S(1)} %pad_maximum_fusion.refs_10_.refs_15_.refs_20_.mod), channel_id=1, source_target_pairs={{0,1},{1,2},{2,3},{3,4},{4,5},{5,6},{6,7},{7,8},{8,9},{9,10},{10,1... | collective-permute-start | bytes 884744 | tf_op jit(solution)/shard_map/ppermute | solution.py:23
  6.5 18.1 %collective-permute-start = (bf16[128,1024]{1,0:T(8,128)(2,1)S(1)}, bf16[128,1024]{1,0:T(8,128)(2,1)S(1)}, u32[]{:S(2)}, u32[]{:S(2)}) collective-permute-start(bf16[128,1024]{1,0:T(8,128)(2,1)S(1)} %pad_maximum_fusion.1.refs_10_.refs_15_), channel_id=1, source_target_pairs={{0,1},{1,2},{2,3},{3,4},{4,5},{5,6},{6,7},{7,8},{8,9},{9,10},{10,1... | collective-permute-start | bytes 786440 | tf_op jit(solution)/shard_map/ppermute | solution.py:23
  19.0 14.8 %collective-permute-start.5 = (bf16[128,1152]{1,0:T(8,128)(2,1)S(1)}, bf16[128,1152]{1,0:T(8,128)(2,1)S(1)}, u32[]{:S(2)}, u32[]{:S(2)}) collective-permute-start(bf16[128,1152]{1,0:T(8,128)(2,1)S(1)} %collective-permute-done.4.refs_9_.refs_14_.refs_19_), channel_id=1, source_target_pairs={{0,1},{1,2},{2,3},{3,4},{4,5},{5,6},{6,7},{7,8},{8,9},{9,10},{10,1... | collective-permute-start | bytes 884744 | tf_op jit(solution)/shard_map/ppermute | solution.py:23
  24.6 14.9 %collective-permute-start.1 = (bf16[128,1024]{1,0:T(8,128)(2,1)S(1)}, bf16[128,1024]{1,0:T(8,128)(2,1)S(1)}, u32[]{:S(2)}, u32[]{:S(2)}) collective-permute-start(bf16[128,1024]{1,0:T(8,128)(2,1)S(1)} %collective-permute-done.refs_9_.refs_14_), channel_id=1, source_target_pairs={{0,1},{1,2},{2,3},{3,4},{4,5},{5,6},{6,7},{7,8},{8,9},{9,10},{10,1... | collective-permute-start | bytes 786440 | tf_op jit(solution)/shard_map/ppermute | solution.py:23
  33.8 15.3 %collective-permute-start.6 = (bf16[128,1152]{1,0:T(8,128)(2,1)S(1)}, bf16[128,1152]{1,0:T(8,128)(2,1)S(1)}, u32[]{:S(2)}, u32[]{:S(2)}) collective-permute-start(bf16[128,1152]{1,0:T(8,128)(2,1)S(1)} %collective-permute-done.5.refs_8_.refs_13_.refs_18_), channel_id=1, source_target_pairs={{0,1},{1,2},{2,3},{3,4},{4,5},{5,6},{6,7},{7,8},{8,9},{9,10},{10,1... | collective-permute-start | bytes 884744 | tf_op jit(solution)/shard_map/ppermute | solution.py:23
  39.5 15.4 %collective-permute-start.2 = (bf16[128,1024]{1,0:T(8,128)(2,1)S(1)}, bf16[128,1024]{1,0:T(8,128)(2,1)}, u32[]{:S(2)}, u32[]{:S(2)}) collective-permute-start(bf16[128,1024]{1,0:T(8,128)(2,1)S(1)} %collective-permute-done.1.refs_8_.refs_13_), channel_id=1, source_target_pairs={{0,1},{1,2},{2,3},{3,4},{4,5},{5,6},{6,7},{7,8},{8,9},{9,10},{10,1... | collective-permute-start | bytes 786440 | tf_op jit(solution)/shard_map/ppermute | solution.py:23
  49.1 15.5 %collective-permute-start.7 = (bf16[128,1152]{1,0:T(8,128)(2,1)S(1)}, bf16[128,1152]{1,0:T(8,128)(2,1)}, u32[]{:S(2)}, u32[]{:S(2)}) collective-permute-start(bf16[128,1152]{1,0:T(8,128)(2,1)S(1)} %collective-permute-done.6.refs_7_.refs_12_.refs_17_), channel_id=1, source_target_pairs={{0,1},{1,2},{2,3},{3,4},{4,5},{5,6},{6,7},{7,8},{8,9},{9,10},{10,1... | collective-permute-start | bytes 884744 | tf_op jit(solution)/shard_map/ppermute | solution.py:23
  54.9 28.8 %collective-permute-start.3 = (bf16[128,1024]{1,0:T(8,128)(2,1)}, bf16[128,1024]{1,0:T(8,128)(2,1)}, u32[]{:S(2)}, u32[]{:S(2)}) collective-permute-start(bf16[128,1024]{1,0:T(8,128)(2,1)} %collective-permute-done.2.refs_7_.refs_12_), channel_id=1, source_target_pairs={{0,1},{1,2},{2,3},{3,4},{4,5},{5,6},{6,7},{7,8},{8,9},{9,10},{10,1... | collective-permute-start | bytes 786440 | tf_op jit(solution)/shard_map/ppermute | solution.py:23
  99.0 11.2 %collective-permute-start.12 = (bf16[128,1024]{1,0:T(8,128)(2,1)S(1)}, bf16[128,1024]{1,0:T(8,128)(2,1)S(1)}, u32[]{:S(2)}, u32[]{:S(2)}) collective-permute-start(bf16[128,1024]{1,0:T(8,128)(2,1)S(1)} %get-tuple-element.38), channel_id=1, source_target_pairs={{1,0},{2,1},{3,2},{4,3},{5,4},{6,5},{7,6},{8,7},{9,8},{10,9},{11,1... | collective-permute-start | bytes 786440 | tf_op jit(solution)/shard_map/ppermute | solution.py:23
  101.1 15.0 %collective-permute-start.8 = (bf16[128,1024]{1,0:T(8,128)(2,1)S(1)}, bf16[128,1024]{1,0:T(8,128)(2,1)S(1)}, u32[]{:S(2)}, u32[]{:S(2)}) collective-permute-start(bf16[128,1024]{1,0:T(8,128)(2,1)S(1)} %get-tuple-element.32), channel_id=1, source_target_pairs={{1,0},{2,1},{3,2},{4,3},{5,4},{6,5},{7,6},{8,7},{9,8},{10,9},{11,1... | collective-permute-start | bytes 786440 | tf_op jit(solution)/shard_map/ppermute | solution.py:23
  110.3 12.0 %collective-permute-start.13 = (bf16[128,1024]{1,0:T(8,128)(2,1)S(1)}, bf16[128,1024]{1,0:T(8,128)(2,1)S(1)}, u32[]{:S(2)}, u32[]{:S(2)}) collective-permute-start(bf16[128,1024]{1,0:T(8,128)(2,1)S(1)} %add_convert_fusion.2), channel_id=1, source_target_pairs={{1,0},{2,1},{3,2},{4,3},{5,4},{6,5},{7,6},{8,7},{9,8},{10,9},{11,1... | collective-permute-start | bytes 786440 | tf_op jit(solution)/shard_map/ppermute | solution.py:23
  116.2 14.0 %collective-permute-start.9 = (bf16[128,1024]{1,0:T(8,128)(2,1)S(1)}, bf16[128,1024]{1,0:T(8,128)(2,1)S(1)}, u32[]{:S(2)}, u32[]{:S(2)}) collective-permute-start(bf16[128,1024]{1,0:T(8,128)(2,1)S(1)} %add_convert_fusion.5), channel_id=1, source_target_pairs={{1,0},{2,1},{3,2},{4,3},{5,4},{6,5},{7,6},{8,7},{9,8},{10,9},{11,1... | collective-permute-start | bytes 786440 | tf_op jit(solution)/shard_map/ppermute | solution.py:23
  123.4 14.7 %collective-permute-start.14 = (bf16[128,1024]{1,0:T(8,128)(2,1)S(1)}, bf16[128,1024]{1,0:T(8,128)(2,1)S(1)}, u32[]{:S(2)}, u32[]{:S(2)}) collective-permute-start(bf16[128,1024]{1,0:T(8,128)(2,1)S(1)} %add_convert_fusion.1), channel_id=1, source_target_pairs={{1,0},{2,1},{3,2},{4,3},{5,4},{6,5},{7,6},{8,7},{9,8},{10,9},{11,1... | collective-permute-start | bytes 786440 | tf_op jit(solution)/shard_map/ppermute | solution.py:23
  130.1 7.9 %collective-permute-start.16 = (f32[80,128]{1,0:T(8,128)S(1)}, f32[80,128]{1,0:T(8,128)S(1)}, u32[]{:S(2)}, u32[]{:S(2)}) collective-permute-start(f32[80,128]{1,0:T(8,128)S(1)} %reshape.39), channel_id=1, source_target_pairs={{0,1},{1,0},{2,3},{3,2},{4,5},{5,4},{6,7},{7,6},{8,9},{9,8},{10,11... | collective-permute-start | bytes 122888 | tf_op jit(solution)/shard_map/ppermute | solution.py:245
  130.2 14.1 %collective-permute-start.10 = (bf16[128,1024]{1,0:T(8,128)(2,1)S(1)}, bf16[128,1024]{1,0:T(8,128)(2,1)S(1)}, u32[]{:S(2)}, u32[]{:S(2)}) collective-permute-start(bf16[128,1024]{1,0:T(8,128)(2,1)S(1)} %add_convert_fusion.4), channel_id=1, source_target_pairs={{1,0},{2,1},{3,2},{4,3},{5,4},{6,5},{7,6},{8,7},{9,8},{10,9},{11,1... | collective-permute-start | bytes 786440 | tf_op jit(solution)/shard_map/ppermute | solution.py:23
  138.0 15.5 %collective-permute-start.17 = (f32[80,128]{1,0:T(8,128)S(1)}, f32[80,128]{1,0:T(8,128)S(1)}, u32[]{:S(2)}, u32[]{:S(2)}) collective-permute-start(f32[80,128]{1,0:T(8,128)S(1)} %add.83), channel_id=1, source_target_pairs={{0,2},{1,3},{2,0},{3,1},{4,6},{5,7},{6,4},{7,5},{8,10},{9,11},{10,... | collective-permute-start | bytes 122888 | tf_op jit(solution)/shard_map/ppermute | solution.py:245
  138.2 44.8 %collective-permute-start.15 = (bf16[128,1024]{1,0:T(8,128)(2,1)S(1)}, bf16[128,1024]{1,0:T(8,128)(2,1)S(1)}, u32[]{:S(2)}, u32[]{:S(2)}) collective-permute-start(bf16[128,1024]{1,0:T(8,128)(2,1)S(1)} %add_convert_fusion), channel_id=1, source_target_pairs={{1,0},{2,1},{3,2},{4,3},{5,4},{6,5},{7,6},{8,7},{9,8},{10,9},{11,1... | collective-permute-start | bytes 786440 | tf_op jit(solution)/shard_map/ppermute | solution.py:23
  144.4 42.8 %collective-permute-start.11 = (bf16[128,1024]{1,0:T(8,128)(2,1)S(1)}, bf16[128,1024]{1,0:T(8,128)(2,1)S(1)}, u32[]{:S(2)}, u32[]{:S(2)}) collective-permute-start(bf16[128,1024]{1,0:T(8,128)(2,1)S(1)} %add_convert_fusion.3), channel_id=1, source_target_pairs={{1,0},{2,1},{3,2},{4,3},{5,4},{6,5},{7,6},{8,7},{9,8},{10,9},{11,1... | collective-permute-start | bytes 786440 | tf_op jit(solution)/shard_map/ppermute | solution.py:23
  153.5 8.0 %collective-permute-start.18 = (f32[80,128]{1,0:T(8,128)S(1)}, f32[80,128]{1,0:T(8,128)S(1)}, u32[]{:S(2)}, u32[]{:S(2)}) collective-permute-start(f32[80,128]{1,0:T(8,128)S(1)} %add.84), channel_id=1, source_target_pairs={{0,4},{1,5},{2,6},{3,7},{4,0},{5,1},{6,2},{7,3},{8,12},{9,13},{10,... | collective-permute-start | bytes 122888 | tf_op jit(solution)/shard_map/ppermute | solution.py:245
  161.5 4.0 %collective-permute-start.19 = (f32[80,128]{1,0:T(8,128)S(1)}, f32[80,128]{1,0:T(8,128)S(1)}, u32[]{:S(2)}, u32[]{:S(2)}) collective-permute-start(f32[80,128]{1,0:T(8,128)S(1)} %add.85), channel_id=1, source_target_pairs={{0,8},{1,9},{2,10},{3,11},{4,12},{5,13},{6,14},{7,15},{8,0},{9,1},... | collective-permute-start | bytes 122888 | tf_op jit(solution)/shard_map/ppermute | solution.py:245
  165.5 5.5 %collective-permute-start.20 = (f32[80,128]{1,0:T(8,128)S(1)}, f32[80,128]{1,0:T(8,128)S(1)}, u32[]{:S(2)}, u32[]{:S(2)}) collective-permute-start(f32[80,128]{1,0:T(8,128)S(1)} %add.86), channel_id=1, source_target_pairs={{0,16},{1,17},{2,18},{3,19},{4,20},{5,21},{6,22},{7,23},{8,24},{9,... | collective-permute-start | bytes 122888 | tf_op jit(solution)/shard_map/ppermute | solution.py:245
  171.0 1.2 collective-permute-start.21
  172.2 4.0 %collective-permute-start.22 = (f32[80,128]{1,0:T(8,128)S(1)}, f32[80,128]{1,0:T(8,128)S(1)}, u32[]{:S(2)}, u32[]{:S(2)}) collective-permute-start(f32[80,128]{1,0:T(8,128)S(1)} %add.88), channel_id=1, source_target_pairs={{0,64},{1,65},{2,66},{3,67},{4,68},{5,69},{6,70},{7,71},{8,72},{9,... | collective-permute-start | bytes 122888 | tf_op jit(solution)/shard_map/ppermute | solution.py:245
  176.2 5.5 %collective-permute-start.23 = (f32[80,128]{1,0:T(8,128)S(1)}, f32[80,128]{1,0:T(8,128)S(1)}, u32[]{:S(2)}, u32[]{:S(2)}) collective-permute-start(f32[80,128]{1,0:T(8,128)S(1)} %add.89), channel_id=1, source_target_pairs={{0,128},{1,129},{2,130},{3,131},{4,132},{5,133},{6,134},{7,135},{8... | collective-permute-start | bytes 122888 | tf_op jit(solution)/shard_map/ppermute | solution.py:245
  (21 other events, 437.6 us)

commit v3 on v2

--- a/solution.py
+++ b/solution.py
@@ -13,7 +13,12 @@
 EPS = 1e-06
 AXES = ("seq", "head")
 CHUNKS = 2
-SLAB = 2
+NEAR = 3
+TURNS = (2, 2, 2, 2)
+TIED = True
+VMEM = 62 * 1024 * 1024
+COST = 1
+SLAB = 4
 FAR = -1e30
 
 
@@ -50,13 +55,13 @@
     )
 
 
-def attend_kernel(depth, repeat, aliased, *refs):
+def attend_kernel(depth, repeat, skip, *refs):
     blocks = depth + 1
     starts, mod_row, queries, grads, query_gain, key_gain = refs[:6]
     key_refs = refs[6 : 6 + blocks]
     value_refs = refs[6 + blocks : 6 + 2 * blocks]
     mod_refs = refs[6 + 2 * blocks : 6 + 3 * blocks]
-    rest = refs[6 + 3 * blocks + (2 if aliased else 0) :]
+    rest = refs[6 + 3 * blocks + skip :]
     attended, query_back = rest[:2]
     back_refs = rest[2 : 2 + blocks]
     query_sums, key_sums, bias = rest[2 + blocks :]
@@ -149,7 +154,8 @@
     key_sums[...] = jnp.where(lines == 0, of_text, jnp.where(lines == 1, of_motion, 0.0))
 
 
-def attend(first_head, kv, starts, mod_row, queries, grads, query_gain, key_gain, held, mods, before):
+def attend(first_head, kv, chunk, starts, mod_row, queries, grads, query_gain, key_gain, held, mods, before, token):
+    start_head, chunk_kv = chunk
     rows, width = queries.shape
     repeat = width // HD // (key_gain.shape[1] // HD)
     blocks = len(held)
@@ -159,45 +165,50 @@
         return pl.BlockSpec(shape, index)
 
     whole = lambda g: (0, 0)
-    here = lambda g: (0, first_head + g)
+    here = lambda g: (0, start_head + first_head + g)
+    local = lambda g: (0, first_head + g)
     in_specs = [
         at((1, rows), whole),
         at((1, rows), whole),
         at((rows, group), here),
         at((rows, group), here),
-        at((group, 2), lambda g: (first_head + g, 0)),
+        at((group, 2), lambda g: (start_head + first_head + g, 0)),
         at((2, HD), here),
     ]
-    in_specs += [at((rows, HD), lambda g: (0, g))] * blocks
-    in_specs += [at((rows, HD), lambda g: (0, kv + g))] * blocks
+    in_specs += [at((rows, HD), local)] * blocks
+    in_specs += [at((rows, HD), lambda g: (0, chunk_kv + first_head + g))] * blocks
     in_specs += [at((rows, HD), lambda g, lane=mods[1]: (0, lane))] * blocks
     operands = [starts, mod_row, queries, grads, query_gain, key_gain, *held, *held, *mods[0]]
     aliases = {}
-    if before is not None:
-        aliases = {len(operands): 0, len(operands) + 1: 1}
-        operands += list(before)
-        in_specs += [pl.BlockSpec(memory_space=pl.ANY)] * 2
+    extra = [(n, x) for n, x in enumerate(before) if x is not None]
+    for n, x in extra:
+        aliases[len(operands)] = n
+        operands.append(x)
+    if token is not None:
+        operands.append(token)
+    in_specs += [pl.BlockSpec(memory_space=pl.ANY)] * (len(operands) - len(in_specs))
+    skip = len(operands) - 6 - 3 * blocks
     big = jax.ShapeDtypeStruct((rows, width), jnp.bfloat16)
-    pair = lambda dtype: jax.ShapeDtypeStruct((rows, kv * 2 * HD), dtype)
+    pair = lambda dtype: jax.ShapeDtypeStruct((rows, chunk_kv * 2 * HD), dtype)
     outs = [big, big, pair(jnp.bfloat16)] + [pair(jnp.float32)] * (blocks - 1)
     outs += [
-        jax.ShapeDtypeStruct((8, kv * group), jnp.float32),
-        jax.ShapeDtypeStruct((8, kv * HD), jnp.float32),
+        jax.ShapeDtypeStruct((8, chunk_kv * group), jnp.float32),
+        jax.ShapeDtypeStruct((8, chunk_kv * HD), jnp.float32),
     ]
     out_specs = [at((rows, group), here)] * 2
-    out_specs += [at((rows, 2 * HD), lambda g: (0, g))] * blocks
-    out_specs += [at((8, group), lambda g: (0, g)), at((8, HD), lambda g: (0, g))]
+    out_specs += [at((rows, 2 * HD), local)] * blocks
+    out_specs += [at((8, group), local), at((8, HD), local)]
     return pl.pallas_call(
-        functools.partial(attend_kernel, blocks - 1, repeat, before is not None),
+        functools.partial(attend_kernel, blocks - 1, repeat, skip),
         grid=(kv,),
         in_specs=in_specs,
         out_specs=out_specs,
         out_shape=outs,
         scratch_shapes=[pltpu.VMEM((blocks * rows, rows), jnp.float32)],
         input_output_aliases=aliases,
-        compiler_params=pltpu.CompilerParams(vmem_limit_bytes=40 * 1024 * 1024),
+        compiler_params=pltpu.CompilerParams(vmem_limit_bytes=VMEM),
         cost_estimate=pl.CostEstimate(
-            flops=kv * repeat * 12 * rows * blocks * rows * HD,
+            flops=COST * kv * repeat * 12 * rows * blocks * rows * HD,
             bytes_accessed=kv * group * rows * 8 + blocks * rows * kv * HD * 12,
             transcendentals=kv * repeat * rows * blocks * rows,
         ),
@@ -205,115 +216,121 @@
     )(*operands)
 
 
-def finish_kernel(arrived, own, keys, mod, key_gain, key_back, value_back):
-    total = arrived[...].astype(jnp.float32) + own[...]
-    low = total[:, :HD].astype(jnp.bfloat16).astype(jnp.float32)
-    raw = keys[...].astype(jnp.float32)
-    factor = lax.rsqrt(jnp.mean(raw * raw, axis=1, keepdims=True) + EPS)
-    unit = raw * factor
-    gain = jnp.where(mod[...].astype(jnp.float32) > 0.5, key_gain[1:2, :], key_gain[0:1, :])
-    along = low * gain
-    back = factor * (along - unit * jnp.mean(along * unit, axis=1, keepdims=True))
-    key_back[...] = back.astype(jnp.bfloat16)
-    value_back[...] = total[:, HD:].astype(jnp.bfloat16)
-
-
-def finish(first_head, kv, arrived, own, keys, mods, key_gain):
-    rows = keys.shape[0]
-    here = lambda g: (0, first_head + g)
-    low = jax.ShapeDtypeStruct((rows, kv * HD), jnp.bfloat16)
+def finish_kernel(*refs):
+    pairs, (keys, mod, key_gain, key_back, value_back) = refs[: 2 * CHUNKS], refs[2 * CHUNKS :]
+    motion = mod[...].astype(jnp.float32) > 0.5
+    kv = keys.shape[1] // HD // CHUNKS
+    for g in range(CHUNKS * kv):
+        arrived, own = pairs[2 * (g // kv) : 2 * (g // kv) + 2]
+        cols = slice(g * HD, (g + 1) * HD)
+        at = 2 * (g % kv) * HD
+        both = arrived[:, at : at + 2 * HD].astype(jnp.float32) + own[:, at : at + 2 * HD]
+        low = both[:, :HD].astype(jnp.bfloat16).astype(jnp.float32)
+        raw = keys[:, cols].astype(jnp.float32)
+        factor = lax.rsqrt(jnp.mean(raw * raw, axis=1, keepdims=True) + EPS)
+        unit = raw * factor
+        along = low * jnp.where(motion, key_gain[1:2, cols], key_gain[0:1, cols])
+        back = factor * (along - unit * jnp.mean(along * unit, axis=1, keepdims=True))
+        key_back[:, cols] = back.astype(jnp.bfloat16)
+        value_back[:, cols] = both[:, HD:].astype(jnp.bfloat16)
+
+
+def finish(pairs, keys, mods, key_gain):
+    low = jax.ShapeDtypeStruct(keys.shape, jnp.bfloat16)
+    full = lambda x: pl.BlockSpec(x.shape, lambda g: (0, 0))
+    operands = [x for pair in pairs for x in pair] + [keys]
     return pl.pallas_call(
         finish_kernel,
-        grid=(kv,),
-        in_specs=[
-            pl.BlockSpec((rows, 2 * HD), lambda g: (0, g)),
-            pl.BlockSpec((rows, 2 * HD), lambda g: (0, g)),
-            pl.BlockSpec((rows, HD), here),
-            pl.BlockSpec((rows, HD), lambda g: (0, mods[1])),
-            pl.BlockSpec((2, HD), here),
-        ],
-        out_specs=[pl.BlockSpec((rows, HD), lambda g: (0, g))] * 2,
+        grid=(1,),
+        in_specs=[full(x) for x in operands]
+        + [pl.BlockSpec((keys.shape[0], HD), lambda g: (0, mods[1])), full(key_gain)],
+        out_specs=[full(keys)] * 2,
         out_shape=[low, low],
+        compiler_params=pltpu.CompilerParams(vmem_limit_bytes=VMEM),
         name="finish",
-    )(arrived, own, keys, mods[0][-1], key_gain)
-
-
-def summed(value):
-    count = lax.axis_size(AXES)
-    bit = 1
-    while bit < count:
-        value = value + lax.ppermute(value, AXES, [(i, i ^ bit) for i in range(count)])
-        bit *= 2
-    return value
+    )(*operands, mods[0][-1], key_gain)
+
+
+def after(value, *others):
+    return lax.optimization_barrier((value, *others))[0]
 
 
 def on_device(queries, keys, values, modality, clip_lengths, query_gains, key_gains, out_grad):
     count, width = queries.shape
+    devices = lax.axis_size(AXES)
     kv_heads = keys.shape[1] // HD
     kv = kv_heads // CHUNKS
     depth = (MOST + count - 1) // count
     first = lax.axis_index(AXES) * count
     mod_lanes = jnp.broadcast_to(modality.astype(jnp.bfloat16)[:, None], (count, HD))
-    held = []
-    for chunk in range(CHUNKS):
-        part = slice(chunk * kv * HD, (chunk + 1) * kv * HD)
-        block = [keys[:, part], values[:, part]] + ([mod_lanes] if chunk == 0 else [])
-        held.append([jnp.concatenate(block, 1)])
-    for chunk in range(CHUNKS):
-        for _ in range(depth):
-            held[chunk].append(shifted(held[chunk][-1], 1))
-    held = [blocks[::-1] for blocks in held]
-    mods = (held[0], 2 * kv)
+    low_part = slice(0, kv * HD)
+    high_part = slice(kv * HD, 2 * kv * HD)
+    ahead = [jnp.concatenate([keys[:, low_part], values[:, low_part], mod_lanes], 1)]
+    behind = [jnp.concatenate([keys[:, high_part], values[:, high_part]], 1)]
+    for n in range(depth):
+        ahead.append(shifted(ahead[-1], 1))
+        behind.append(shifted(behind[-1], 1))
+    mods = (ahead[::-1], 2 * kv)
 
     starts = clip_start(clip_lengths, first + jnp.arange(count, dtype=jnp.int32))
     starts = (starts - first + depth * count)[None, :]
     mod_row = modality[None, :]
     gain_columns = query_gains.T
-    before = None
-    sums = []
-    key_parts = []
-    value_parts = []
-    rings = []
-    for chunk in range(CHUNKS):
-        outs = attend(
-            chunk * kv,
-            kv,
-            starts,
-            mod_row,
-            queries,
-            out_grad,
-            gain_columns,
-            key_gains,
-            held[chunk],
-            mods,
-            before,
-        )
-        before = outs[:2]
-        sums.append(outs[-2:])
-        rings.append(outs[2:-2])
-    for chunk in range(CHUNKS):
-        backs = rings[chunk]
-        moving = backs[0]
-        for n in range(1, depth + 1):
-            moving = shifted(moving, -1)
-            if n < depth:
-                moving = (moving.astype(jnp.float32) + backs[n]).astype(jnp.bfloat16)
-        key_part, value_part = finish(
-            chunk * kv, kv, moving, backs[depth], keys, mods, key_gains
-        )
-        key_parts.append(key_part)
-        value_parts.append(value_part)
-    attended, query_grad = before
-    gains = jnp.concatenate([q[:2] for q, _ in sums] + [k[:2] for _, k in sums], 1)
-    gains = summed(gains.reshape(-1, HD)).reshape(2, -1)
-    return (
-        attended,
-        query_grad,
-        jnp.concatenate(key_parts, 1),
-        jnp.concatenate(value_parts, 1),
-        gains[:, :width],
-        gains[:, width:],
-    )
+    outputs = depth + 5
+
+    def attended_chunk(chunk, held, large, sizes, tokens):
+        outs = [*large] + [None] * (outputs - 2)
+        head = 0
+        for size, token in zip(sizes, tokens):
+            outs = attend(
+                head,
+                size,
+                (chunk * kv, kv),
+                starts,
+                mod_row,
+                queries,
+                out_grad,
+                gain_columns,
+                key_gains,
+                held[::-1],
+                mods,
+                outs,
+                token(),
+            )
+            head += size
+            yield outs
+
+    def add(arrived, part):
+        return (arrived.astype(jnp.float32) + part).astype(jnp.bfloat16)
+
+    (one,) = attended_chunk(0, ahead, [None, None], [kv], [lambda: None])
+    (two,) = attended_chunk(1, behind, one[:2], [kv], [lambda: None])
+    backs = (one[2:-2], two[2:-2])
+    attended, query_grad = two[:2]
+    gains = jnp.concatenate([one[-2][:2], two[-2][:2], one[-1][:2], two[-1][:2]], 1).reshape(-1, HD)
+    bits = [1 << n for n in range(devices.bit_length() - 1)]
+    bits = bits[NEAR:] + bits[:NEAR]
+    done = 0
+    moved = [shifted(part[0], -1) for part in backs]
+    for n in range(1, depth + 1):
+        for bit in bits[done : done + TURNS[n - 1]]:
+            gains = gains + lax.ppermute(gains, AXES, [(i, i ^ bit) for i in range(devices)])
+        done += TURNS[n - 1]
+        if n < depth:
+            sent = [add(arrived, part[n]) for arrived, part in zip(moved, backs)]
+            if TIED:
+                gains = after(gains, sent[0])
+                sent[1] = after(sent[1], gains)
+            moved = [shifted(x, -1) for x in sent]
+    if TURNS == (0, 0, 0, 0):
+        gains = after(gains, *moved)
+        for bit in bits:
+            gains = gains + lax.ppermute(gains, AXES, [(i, i ^ bit) for i in range(devices)])
+    key_grad, value_grad = finish(
+        [(arrived, part[depth]) for arrived, part in zip(moved, backs)], keys, mods, key_gains
+    )
+    gains = gains.reshape(2, -1)
+    return attended, query_grad, key_grad, value_grad, gains[:, :width], gains[:, width:]
 
 
 def solution(mesh):

time: 196 us -> 170 us (0.87)
  Pallas kernels: 37.3 us -> 26.4 us
  starting transfers between devices: 66 us -> 60.4 us
  waiting for transfers between devices: 73.7 us -> 68.6 us
  other arithmetic: 5.82 us -> 3.05 us
    pallas_call x4 -> x3, Pallas kernels: 37.3 us -> 26.4 us  [the longest x2 23.7 us: attend(): pl.pallas_call(functools.partial(attend_kernel, blocks - 1, repeat, skip)...]
    ppermute x16, starting transfers between devices: 63.2 us -> 54.5 us  [shifted(): lax.ppermute(value, AXES, [(source, source + steps) for source in range(f...]
    unnamed x43 -> x37, local copies, waits for them, and re-layouts: 8.3 us -> 3.54 us
    concatenate x5 -> x3, other arithmetic: 3.45 us -> 0.07 us  [the longest x1 0.02 us: on_device(): jnp.concatenate([keys[:, low_part], values[:, low_part], mod_lanes], 1)]
    slice x5, local copies, waits for them, and re-layouts: 1.17 us -> 4.34 us  [the longest x1 1.13 us: on_device(): keys[:, low_part]]
    ppermute x8, starting transfers between devices: 2.79 us -> 5.9 us  [on_device(): lax.ppermute(gains, AXES, [(i, i ^ bit) for i in range(devices)])]
    ppermute x8, waiting for transfers between devices: 25.6 us -> 23 us  [on_device(): lax.ppermute(gains, AXES, [(i, i ^ bit) for i in range(devices)])]
    ppermute x16, waiting for transfers between devices: 48.1 us -> 45.6 us  [shifted(): lax.ppermute(value, AXES, [(source, source + steps) for source in range(f...]
  transfers between devices with their start and end apart: 24 -> 24, of which waited for: 15 -> 14; matrix products, arithmetic and copies ran while one was open for 2% -> 3% of each run, Pallas kernels for 10% -> 7%
where the time goes in v3:
time: 170 us; the launch traced here: 169 us
  waiting for transfers between devices  68.6 us (40%)
  starting transfers between devices  60.4 us (36%)
  Pallas kernels  26.4 us (16%)
  local copies, waits for them, and re-layouts  9.24 us (5%)
  other arithmetic  3.05 us (2%)
    ppermute x16, starting transfers between devices, shifted(): lax.ppermute(value, AXES, [(source, source + steps) for source in range(f...  54.5 us
    ppermute x16, waiting for transfers between devices, shifted(): lax.ppermute(value, AXES, [(source, source + steps) for source in range(f...  45.6 us
    pallas_call x2, Pallas kernels, attend(): pl.pallas_call(functools.partial(attend_kernel, blocks - 1, repeat, skip)...  23.7 us
    ppermute x8, waiting for transfers between devices, on_device(): lax.ppermute(gains, AXES, [(i, i ^ bit) for i in range(devices)])  23 us
    ppermute x8, starting transfers between devices, on_device(): lax.ppermute(gains, AXES, [(i, i ^ bit) for i in range(devices)])  5.9 us
    unnamed x37, local copies, waits for them, and re-layouts  3.54 us
  transfers between devices with their start and end apart: 24, of which 14 were waited for; matrix products, arithmetic and copies ran while one was open for 3% of the time, Pallas kernels for 7%

profile of v3, /device:TPU:2, one launch (start us, length us, event | category | flops | bytes accessed | tf_op | source)
XLA Modules:
  0.0 168.9 jit_solution(3694183401511937476)
XLA Ops:
  2.6 3.8 %collective-permute-start.4 = (bf16[128,1152]{1,0:T(8,128)(2,1)S(1)}, bf16[128,1152]{1,0:T(8,128)(2,1)S(1)}, u32[]{:S(2)}, u32[]{:S(2)}) collective-permute-start(bf16[128,1152]{1,0:T(8,128)(2,1)S(1)} %pad_maximum_fusion.refs_10_.refs_15_.refs_20_.refs_5_), channel_id=1, source_target_pairs={{0,1},{1,2},{2,3},{3,4},{4,5},{5,6},{6,7},{7,8},{8,9},{9,10},{10,1... | collective-permute-start | bytes 884744 | tf_op jit(solution)/shard_map/ppermute | solution.py:28
  6.5 3.8 %collective-permute-start = (bf16[128,1024]{1,0:T(8,128)(2,1)S(1)}, bf16[128,1024]{1,0:T(8,128)(2,1)S(1)}, u32[]{:S(2)}, u32[]{:S(2)}) collective-permute-start(bf16[128,1024]{1,0:T(8,128)(2,1)S(1)} %pad_maximum_fusion.1.refs_10_.refs_15_), channel_id=1, source_target_pairs={{0,1},{1,2},{2,3},{3,4},{4,5},{5,6},{6,7},{7,8},{8,9},{9,10},{10,1... | collective-permute-start | bytes 786440 | tf_op jit(solution)/shard_map/ppermute | solution.py:28
  10.3 8.7 %collective-permute-done.4.refs_9_.refs_14_.refs_19_ = bf16[128,1152]{1,0:T(8,128)(2,1)S(1)} collective-permute-done((bf16[128,1152]{1,0:T(8,128)(2,1)S(1)}, bf16[128,1152]{1,0:T(8,128)(2,1)S(1)}, u32[]{:S(2)}, u32[]{:S(2)}) %collective-permute-start.4) | collective-permute-done | bytes 294944 | tf_op jit(solution)/shard_map/ppermute | solution.py:28
  20.9 3.7 %collective-permute-done.refs_9_.refs_14_ = bf16[128,1024]{1,0:T(8,128)(2,1)S(1)} collective-permute-done((bf16[128,1024]{1,0:T(8,128)(2,1)S(1)}, bf16[128,1024]{1,0:T(8,128)(2,1)S(1)}, u32[]{:S(2)}, u32[]{:S(2)}) %collective-permute-start) | collective-permute-done | bytes 262176 | tf_op jit(solution)/shard_map/ppermute | solution.py:28
  26.5 7.3 %collective-permute-done.5.refs_8_.refs_13_.refs_18_ = bf16[128,1152]{1,0:T(8,128)(2,1)S(1)} collective-permute-done((bf16[128,1152]{1,0:T(8,128)(2,1)S(1)}, bf16[128,1152]{1,0:T(8,128)(2,1)S(1)}, u32[]{:S(2)}, u32[]{:S(2)}) %collective-permute-start.5) | collective-permute-done | bytes 294944 | tf_op jit(solution)/shard_map/ppermute | solution.py:28
  35.7 3.8 %collective-permute-done.1.refs_8_.refs_13_ = bf16[128,1024]{1,0:T(8,128)(2,1)S(1)} collective-permute-done((bf16[128,1024]{1,0:T(8,128)(2,1)S(1)}, bf16[128,1024]{1,0:T(8,128)(2,1)S(1)}, u32[]{:S(2)}, u32[]{:S(2)}) %collective-permute-start.1) | collective-permute-done | bytes 262176 | tf_op jit(solution)/shard_map/ppermute | solution.py:28
  41.6 7.5 %collective-permute-done.6.refs_7_.refs_12_.refs_17_ = bf16[128,1152]{1,0:T(8,128)(2,1)S(1)} collective-permute-done((bf16[128,1152]{1,0:T(8,128)(2,1)S(1)}, bf16[128,1152]{1,0:T(8,128)(2,1)S(1)}, u32[]{:S(2)}, u32[]{:S(2)}) %collective-permute-start.6) | collective-permute-done | bytes 294944 | tf_op jit(solution)/shard_map/ppermute | solution.py:28
  51.2 3.8 %collective-permute-done.2.refs_7_.refs_12_ = bf16[128,1024]{1,0:T(8,128)(2,1)} collective-permute-done((bf16[128,1024]{1,0:T(8,128)(2,1)S(1)}, bf16[128,1024]{1,0:T(8,128)(2,1)}, u32[]{:S(2)}, u32[]{:S(2)}) %collective-permute-start.2) | collective-permute-done | bytes 262176 | tf_op jit(solution)/shard_map/ppermute | solution.py:28
  57.4 2.0 %copy.17 = f32[2,4096]{0,1:T(8,128)} copy(f32[2,4096]{1,0:T(2,128)S(1)} %copy-done.15) | data formatting | bytes 65536 | tf_op args[5]
  59.4 5.1 %collective-permute-done.7.refs_6_.refs_11_.refs_16_ = bf16[128,1152]{1,0:T(8,128)(2,1)S(1)} collective-permute-done((bf16[128,1152]{1,0:T(8,128)(2,1)S(1)}, bf16[128,1152]{1,0:T(8,128)(2,1)S(1)}, u32[]{:S(2)}, u32[]{:S(2)}) %collective-permute-start.7) | collective-permute-done | bytes 294944 | tf_op jit(solution)/shard_map/ppermute | solution.py:28
  65.2 11.8 %attend.2 = (bf16[128,4096]{1,0:T(8,128)(2,1)}, bf16[128,4096]{1,0:T(8,128)(2,1)}, bf16[128,1024]{1,0:T(8,128)(2,1)}, f32[128,1024]{1,0:T(8,128)}, f32[128,1024]...) custom-call(s32[1,128]{1,0:T(1,128)} %add_bitcast_fusion.refs_0_, ...), custom_call_target="tpu_custom_call" | custom-call | flops 2013265920 | bytes 6029312 | tf_op jit(solution)/shard_map/attend/pallas_call | solution.py:201
  77.0 11.9 %attend.3 = (bf16[128,4096]{1,0:T(8,128)(2,1)}, bf16[128,4096]{1,0:T(8,128)(2,1)}, bf16[128,1024]{1,0:T(8,128)(2,1)}, f32[128,1024]{1,0:T(8,128)}, f32[128,1024]...) custom-call(s32[1,128]{1,0:T(1,128)} %add_bitcast_fusion.refs_0_, ...), custom_call_target="tpu_custom_call", output_to_operand_aliasing={{0}: (21, {}), {1}: (22, {})} | custom-call | flops 2013265920 | bytes 6029312 | tf_op jit(solution)/shard_map/attend/pallas_call | solution.py:201
  92.2 2.8 %collective-permute-start.8 = (bf16[128,1024]{1,0:T(8,128)(2,1)S(1)}, bf16[128,1024]{1,0:T(8,128)(2,1)S(1)}, u32[]{:S(2)}, u32[]{:S(2)}) collective-permute-start(bf16[128,1024]{1,0:T(8,128)(2,1)S(1)} %copy-done.16), channel_id=1, source_target_pairs={{1,0},{2,1},{3,2},{4,3},{5,4},{6,5},{7,6},{8,7},{9,8},{10,9},{11,1... | collective-permute-start | bytes 786440 | tf_op jit(solution)/shard_map/ppermute | solution.py:28
  95.2 4.0 %collective-permute-done.13 = f32[80,128]{1,0:T(8,128)S(1)} collective-permute-done((f32[80,128]{1,0:T(8,128)S(1)}, f32[80,128]{1,0:T(8,128)S(1)}, u32[]{:S(2)}, u32[]{:S(2)}) %collective-permute-start.13) | collective-permute-done | bytes 40992 | tf_op jit(solution)/shard_map/ppermute | solution.py:317
  101.1 3.6 %collective-permute-done.14 = f32[80,128]{1,0:T(8,128)S(1)} collective-permute-done((f32[80,128]{1,0:T(8,128)S(1)}, f32[80,128]{1,0:T(8,128)S(1)}, u32[]{:S(2)}, u32[]{:S(2)}) %collective-permute-start.14) | collective-permute-done | bytes 40992 | tf_op jit(solution)/shard_map/ppermute | solution.py:317
  104.9 3.8 %collective-permute-start.9 = (bf16[128,1024]{1,0:T(8,128)(2,1)S(1)}, bf16[128,1024]{1,0:T(8,128)(2,1)S(1)}, u32[]{:S(2)}, u32[]{:S(2)}) collective-permute-start(bf16[128,1024]{1,0:T(8,128)(2,1)S(1)} %add_convert_fusion.5), channel_id=1, source_target_pairs={{1,0},{2,1},{3,2},{4,3},{5,4},{6,5},{7,6},{8,7},{9,8},{10,9},{11,1... | collective-permute-start | bytes 786440 | tf_op jit(solution)/shard_map/ppermute | solution.py:28
  110.0 5.7 %collective-permute-start.15 = (bf16[128,1024]{1,0:T(8,128)(2,1)S(1)}, bf16[128,1024]{1,0:T(8,128)(2,1)S(1)}, u32[]{:S(2)}, u32[]{:S(2)}) collective-permute-start(bf16[128,1024]{1,0:T(8,128)(2,1)S(1)} %add_convert_fusion.2), channel_id=1, source_target_pairs={{1,0},{2,1},{3,2},{4,3},{5,4},{6,5},{7,6},{8,7},{9,8},{10,9},{11,1... | collective-permute-start | bytes 786440 | tf_op jit(solution)/shard_map/ppermute | solution.py:28
  115.9 4.9 %collective-permute-start.19 = (f32[80,128]{1,0:T(8,128)S(1)}, f32[80,128]{1,0:T(8,128)S(1)}, u32[]{:S(2)}, u32[]{:S(2)}) collective-permute-start(f32[80,128]{1,0:T(8,128)S(1)} %add.85), channel_id=1, source_target_pairs={{0,128},{1,129},{2,130},{3,131},{4,132},{5,133},{6,134},{7,135},{8... | collective-permute-start | bytes 122888 | tf_op jit(solution)/shard_map/ppermute | solution.py:317
  120.8 10.2 %collective-permute-start.10 = (bf16[128,1024]{1,0:T(8,128)(2,1)S(1)}, bf16[128,1024]{1,0:T(8,128)(2,1)S(1)}, u32[]{:S(2)}, u32[]{:S(2)}) collective-permute-start(bf16[128,1024]{1,0:T(8,128)(2,1)S(1)} %add_convert_fusion.4), channel_id=1, source_target_pairs={{1,0},{2,1},{3,2},{4,3},{5,4},{6,5},{7,6},{8,7},{9,8},{10,9},{11,1... | collective-permute-start | bytes 786440 | tf_op jit(solution)/shard_map/ppermute | solution.py:28
  135.5 5.3 %collective-permute-done.18 = bf16[128,1024]{1,0:T(8,128)(2,1)S(1)} collective-permute-done((bf16[128,1024]{1,0:T(8,128)(2,1)S(1)}, bf16[128,1024]{1,0:T(8,128)(2,1)S(1)}, u32[]{:S(2)}, u32[]{:S(2)}) %collective-permute-start.18) | collective-permute-done | bytes 262176 | tf_op jit(solution)/shard_map/ppermute | solution.py:28
  140.9 7.2 %collective-permute-start.21 = (bf16[128,1024]{1,0:T(8,128)(2,1)S(1)}, bf16[128,1024]{1,0:T(8,128)(2,1)S(1)}, u32[]{:S(2)}, u32[]{:S(2)}) collective-permute-start(bf16[128,1024]{1,0:T(8,128)(2,1)S(1)} %add_convert_fusion), channel_id=1, source_target_pairs={{1,0},{2,1},{3,2},{4,3},{5,4},{6,5},{7,6},{8,7},{9,8},{10,9},{11,1... | collective-permute-start | bytes 786440 | tf_op jit(solution)/shard_map/ppermute | solution.py:28
  150.1 6.1 %collective-permute-done.22 = f32[80,128]{1,0:T(8,128)S(1)} collective-permute-done((f32[80,128]{1,0:T(8,128)S(1)}, f32[80,128]{1,0:T(8,128)S(1)}, u32[]{:S(2)}, u32[]{:S(2)}) %collective-permute-start.22) | collective-permute-done | bytes 40992 | tf_op jit(solution)/shard_map/ppermute | solution.py:317
  156.7 7.4 %collective-permute-done.23 = f32[80,128]{1,0:T(8,128)S(1)} collective-permute-done((f32[80,128]{1,0:T(8,128)S(1)}, f32[80,128]{1,0:T(8,128)S(1)}, u32[]{:S(2)}, u32[]{:S(2)}) %collective-permute-start.23) | collective-permute-done | bytes 40992 | tf_op jit(solution)/shard_map/ppermute | solution.py:317
  166.2 2.7 %finish.1 = (bf16[128,1024]{1,0:T(8,128)(2,1)}, bf16[128,1024]{1,0:T(8,128)(2,1)}) custom-call(bf16[128,1024]{1,0:T(8,128)(2,1)} %copy-done.14, f32[128,1024]{1,0:T(8,128)} %get-tuple-element.40.refs_1_, bf16[128,1024]{1,0:T(8,128)(2,1)} %copy-done.13, f32[128,1024]{1,0:T(8,128)} %get-tuple-element.55.refs_3_, bf16[128,1024]{1,0:T(8,128)(2,1)} %refs_4_.1, ...), custom_call_target="tpu_custom_call" | custom-call | tf_op jit(solution)/shard_map/finish/pallas_call | solution.py:242
  (96 shorter events, 30.9 us)
Async XLA Ops:
  2.6 16.4 %collective-permute-start.4 = (bf16[128,1152]{1,0:T(8,128)(2,1)S(1)}, bf16[128,1152]{1,0:T(8,128)(2,1)S(1)}, u32[]{:S(2)}, u32[]{:S(2)}) collective-permute-start(bf16[128,1152]{1,0:T(8,128)(2,1)S(1)} %pad_maximum_fusion.refs_10_.refs_15_.refs_20_.refs_5_), channel_id=1, source_target_pairs={{0,1},{1,2},{2,3},{3,4},{4,5},{5,6},{6,7},{7,8},{8,9},{9,10},{10,1... | collective-permute-start | bytes 884744 | tf_op jit(solution)/shard_map/ppermute | solution.py:28
  6.5 18.1 %collective-permute-start = (bf16[128,1024]{1,0:T(8,128)(2,1)S(1)}, bf16[128,1024]{1,0:T(8,128)(2,1)S(1)}, u32[]{:S(2)}, u32[]{:S(2)}) collective-permute-start(bf16[128,1024]{1,0:T(8,128)(2,1)S(1)} %pad_maximum_fusion.1.refs_10_.refs_15_), channel_id=1, source_target_pairs={{0,1},{1,2},{2,3},{3,4},{4,5},{5,6},{6,7},{7,8},{8,9},{9,10},{10,1... | collective-permute-start | bytes 786440 | tf_op jit(solution)/shard_map/ppermute | solution.py:28
  18.9 14.8 %collective-permute-start.5 = (bf16[128,1152]{1,0:T(8,128)(2,1)S(1)}, bf16[128,1152]{1,0:T(8,128)(2,1)S(1)}, u32[]{:S(2)}, u32[]{:S(2)}) collective-permute-start(bf16[128,1152]{1,0:T(8,128)(2,1)S(1)} %collective-permute-done.4.refs_9_.refs_14_.refs_19_), channel_id=1, source_target_pairs={{0,1},{1,2},{2,3},{3,4},{4,5},{5,6},{6,7},{7,8},{8,9},{9,10},{10,1... | collective-permute-start | bytes 884744 | tf_op jit(solution)/shard_map/ppermute | solution.py:28
  24.6 14.9 %collective-permute-start.1 = (bf16[128,1024]{1,0:T(8,128)(2,1)S(1)}, bf16[128,1024]{1,0:T(8,128)(2,1)S(1)}, u32[]{:S(2)}, u32[]{:S(2)}) collective-permute-start(bf16[128,1024]{1,0:T(8,128)(2,1)S(1)} %collective-permute-done.refs_9_.refs_14_), channel_id=1, source_target_pairs={{0,1},{1,2},{2,3},{3,4},{4,5},{5,6},{6,7},{7,8},{8,9},{9,10},{10,1... | collective-permute-start | bytes 786440 | tf_op jit(solution)/shard_map/ppermute | solution.py:28
  33.8 15.3 %collective-permute-start.6 = (bf16[128,1152]{1,0:T(8,128)(2,1)S(1)}, bf16[128,1152]{1,0:T(8,128)(2,1)S(1)}, u32[]{:S(2)}, u32[]{:S(2)}) collective-permute-start(bf16[128,1152]{1,0:T(8,128)(2,1)S(1)} %collective-permute-done.5.refs_8_.refs_13_.refs_18_), channel_id=1, source_target_pairs={{0,1},{1,2},{2,3},{3,4},{4,5},{5,6},{6,7},{7,8},{8,9},{9,10},{10,1... | collective-permute-start | bytes 884744 | tf_op jit(solution)/shard_map/ppermute | solution.py:28
  39.5 15.4 %collective-permute-start.2 = (bf16[128,1024]{1,0:T(8,128)(2,1)S(1)}, bf16[128,1024]{1,0:T(8,128)(2,1)}, u32[]{:S(2)}, u32[]{:S(2)}) collective-permute-start(bf16[128,1024]{1,0:T(8,128)(2,1)S(1)} %collective-permute-done.1.refs_8_.refs_13_), channel_id=1, source_target_pairs={{0,1},{1,2},{2,3},{3,4},{4,5},{5,6},{6,7},{7,8},{8,9},{9,10},{10,1... | collective-permute-start | bytes 786440 | tf_op jit(solution)/shard_map/ppermute | solution.py:28
  49.1 15.4 %collective-permute-start.7 = (bf16[128,1152]{1,0:T(8,128)(2,1)S(1)}, bf16[128,1152]{1,0:T(8,128)(2,1)S(1)}, u32[]{:S(2)}, u32[]{:S(2)}) collective-permute-start(bf16[128,1152]{1,0:T(8,128)(2,1)S(1)} %collective-permute-done.6.refs_7_.refs_12_.refs_17_), channel_id=1, source_target_pairs={{0,1},{1,2},{2,3},{3,4},{4,5},{5,6},{6,7},{7,8},{8,9},{9,10},{10,1... | collective-permute-start | bytes 884744 | tf_op jit(solution)/shard_map/ppermute | solution.py:28
  54.9 22.1 %collective-permute-start.3 = (bf16[128,1024]{1,0:T(8,128)(2,1)}, bf16[128,1024]{1,0:T(8,128)(2,1)}, u32[]{:S(2)}, u32[]{:S(2)}) collective-permute-start(bf16[128,1024]{1,0:T(8,128)(2,1)} %collective-permute-done.2.refs_7_.refs_12_), channel_id=1, source_target_pairs={{0,1},{1,2},{2,3},{3,4},{4,5},{5,6},{6,7},{7,8},{8,9},{9,10},{10,1... | collective-permute-start | bytes 786440 | tf_op jit(solution)/shard_map/ppermute | solution.py:28
  92.2 12.5 %collective-permute-start.8 = (bf16[128,1024]{1,0:T(8,128)(2,1)S(1)}, bf16[128,1024]{1,0:T(8,128)(2,1)S(1)}, u32[]{:S(2)}, u32[]{:S(2)}) collective-permute-start(bf16[128,1024]{1,0:T(8,128)(2,1)S(1)} %copy-done.16), channel_id=1, source_target_pairs={{1,0},{2,1},{3,2},{4,3},{5,4},{6,5},{7,6},{8,7},{9,8},{10,9},{11,1... | collective-permute-start | bytes 786440 | tf_op jit(solution)/shard_map/ppermute | solution.py:28
  95.1 4.1 %collective-permute-start.13 = (f32[80,128]{1,0:T(8,128)S(1)}, f32[80,128]{1,0:T(8,128)S(1)}, u32[]{:S(2)}, u32[]{:S(2)}) collective-permute-start(f32[80,128]{1,0:T(8,128)S(1)} %reshape.39), channel_id=1, source_target_pairs={{0,8},{1,9},{2,10},{3,11},{4,12},{5,13},{6,14},{7,15},{8,0},{9,1},... | collective-permute-start | bytes 122888 | tf_op jit(solution)/shard_map/ppermute | solution.py:317
  99.2 5.5 %collective-permute-start.14 = (f32[80,128]{1,0:T(8,128)S(1)}, f32[80,128]{1,0:T(8,128)S(1)}, u32[]{:S(2)}, u32[]{:S(2)}) collective-permute-start(f32[80,128]{1,0:T(8,128)S(1)} %add.81), channel_id=1, source_target_pairs={{0,16},{1,17},{2,18},{3,19},{4,20},{5,21},{6,22},{7,23},{8,24},{9,... | collective-permute-start | bytes 122888 | tf_op jit(solution)/shard_map/ppermute | solution.py:317
  99.2 9.7 %collective-permute-start.12 = (bf16[128,1024]{1,0:T(8,128)(2,1)}, bf16[128,1024]{1,0:T(8,128)(2,1)S(1)}, u32[]{:S(2)}, u32[]{:S(2)}) collective-permute-start(bf16[128,1024]{1,0:T(8,128)(2,1)} %get-tuple-element.41), channel_id=1, source_target_pairs={{1,0},{2,1},{3,2},{4,3},{5,4},{6,5},{7,6},{8,7},{9,8},{10,9},{11,1... | collective-permute-start | bytes 786440 | tf_op jit(solution)/shard_map/ppermute | solution.py:28
  104.8 3.9 %collective-permute-start.16 = (f32[80,128]{1,0:T(8,128)S(1)}, f32[80,128]{1,0:T(8,128)S(1)}, u32[]{:S(2)}, u32[]{:S(2)}) collective-permute-start(f32[80,128]{1,0:T(8,128)S(1)} %add.82), channel_id=1, source_target_pairs={{0,32},{1,33},{2,34},{3,35},{4,36},{5,37},{6,38},{7,39},{8,40},{9,... | collective-permute-start | bytes 122888 | tf_op jit(solution)/shard_map/ppermute | solution.py:317
  104.9 10.9 %collective-permute-start.9 = (bf16[128,1024]{1,0:T(8,128)(2,1)S(1)}, bf16[128,1024]{1,0:T(8,128)(2,1)S(1)}, u32[]{:S(2)}, u32[]{:S(2)}) collective-permute-start(bf16[128,1024]{1,0:T(8,128)(2,1)S(1)} %add_convert_fusion.5), channel_id=1, source_target_pairs={{1,0},{2,1},{3,2},{4,3},{5,4},{6,5},{7,6},{8,7},{9,8},{10,9},{11,1... | collective-permute-start | bytes 786440 | tf_op jit(solution)/shard_map/ppermute | solution.py:28
  108.7 7.0 %collective-permute-start.17 = (f32[80,128]{1,0:T(8,128)S(1)}, f32[80,128]{1,0:T(8,128)S(1)}, u32[]{:S(2)}, u32[]{:S(2)}) collective-permute-start(f32[80,128]{1,0:T(8,128)S(1)} %add.84), channel_id=1, source_target_pairs={{0,64},{1,65},{2,66},{3,67},{4,68},{5,69},{6,70},{7,71},{8,72},{9,... | collective-permute-start | bytes 122888 | tf_op jit(solution)/shard_map/ppermute | solution.py:317
  110.0 21.0 %collective-permute-start.15 = (bf16[128,1024]{1,0:T(8,128)(2,1)S(1)}, bf16[128,1024]{1,0:T(8,128)(2,1)S(1)}, u32[]{:S(2)}, u32[]{:S(2)}) collective-permute-start(bf16[128,1024]{1,0:T(8,128)(2,1)S(1)} %add_convert_fusion.2), channel_id=1, source_target_pairs={{1,0},{2,1},{3,2},{4,3},{5,4},{6,5},{7,6},{8,7},{9,8},{10,9},{11,1... | collective-permute-start | bytes 786440 | tf_op jit(solution)/shard_map/ppermute | solution.py:28
  115.9 15.1 %collective-permute-start.19 = (f32[80,128]{1,0:T(8,128)S(1)}, f32[80,128]{1,0:T(8,128)S(1)}, u32[]{:S(2)}, u32[]{:S(2)}) collective-permute-start(f32[80,128]{1,0:T(8,128)S(1)} %add.85), channel_id=1, source_target_pairs={{0,128},{1,129},{2,130},{3,131},{4,132},{5,133},{6,134},{7,135},{8... | collective-permute-start | bytes 122888 | tf_op jit(solution)/shard_map/ppermute | solution.py:317
  120.8 14.7 %collective-permute-start.10 = (bf16[128,1024]{1,0:T(8,128)(2,1)S(1)}, bf16[128,1024]{1,0:T(8,128)(2,1)S(1)}, u32[]{:S(2)}, u32[]{:S(2)}) collective-permute-start(bf16[128,1024]{1,0:T(8,128)(2,1)S(1)} %add_convert_fusion.4), channel_id=1, source_target_pairs={{1,0},{2,1},{3,2},{4,3},{5,4},{6,5},{7,6},{8,7},{9,8},{10,9},{11,1... | collective-permute-start | bytes 786440 | tf_op jit(solution)/shard_map/ppermute | solution.py:28
  131.0 4.1 %collective-permute-start.20 = (f32[80,128]{1,0:T(8,128)S(1)}, f32[80,128]{1,0:T(8,128)S(1)}, u32[]{:S(2)}, u32[]{:S(2)}) collective-permute-start(f32[80,128]{1,0:T(8,128)S(1)} %add.87), channel_id=1, source_target_pairs={{0,1},{1,0},{2,3},{3,2},{4,5},{5,4},{6,7},{7,6},{8,9},{9,8},{10,11... | collective-permute-start | bytes 122888 | tf_op jit(solution)/shard_map/ppermute | solution.py:317
  131.2 9.7 %collective-permute-start.18 = (bf16[128,1024]{1,0:T(8,128)(2,1)S(1)}, bf16[128,1024]{1,0:T(8,128)(2,1)S(1)}, u32[]{:S(2)}, u32[]{:S(2)}) collective-permute-start(bf16[128,1024]{1,0:T(8,128)(2,1)S(1)} %add_convert_fusion.1), channel_id=1, source_target_pairs={{1,0},{2,1},{3,2},{4,3},{5,4},{6,5},{7,6},{8,7},{9,8},{10,9},{11,1... | collective-permute-start | bytes 786440 | tf_op jit(solution)/shard_map/ppermute | solution.py:28
  140.9 24.5 %collective-permute-start.21 = (bf16[128,1024]{1,0:T(8,128)(2,1)S(1)}, bf16[128,1024]{1,0:T(8,128)(2,1)S(1)}, u32[]{:S(2)}, u32[]{:S(2)}) collective-permute-start(bf16[128,1024]{1,0:T(8,128)(2,1)S(1)} %add_convert_fusion), channel_id=1, source_target_pairs={{1,0},{2,1},{3,2},{4,3},{5,4},{6,5},{7,6},{8,7},{9,8},{10,9},{11,1... | collective-permute-start | bytes 786440 | tf_op jit(solution)/shard_map/ppermute | solution.py:28
  148.1 17.3 %collective-permute-start.11 = (bf16[128,1024]{1,0:T(8,128)(2,1)S(1)}, bf16[128,1024]{1,0:T(8,128)(2,1)S(1)}, u32[]{:S(2)}, u32[]{:S(2)}) collective-permute-start(bf16[128,1024]{1,0:T(8,128)(2,1)S(1)} %add_convert_fusion.3), channel_id=1, source_target_pairs={{1,0},{2,1},{3,2},{4,3},{5,4},{6,5},{7,6},{8,7},{9,8},{10,9},{11,1... | collective-permute-start | bytes 786440 | tf_op jit(solution)/shard_map/ppermute | solution.py:28
  150.0 6.2 %collective-permute-start.22 = (f32[80,128]{1,0:T(8,128)S(1)}, f32[80,128]{1,0:T(8,128)S(1)}, u32[]{:S(2)}, u32[]{:S(2)}) collective-permute-start(f32[80,128]{1,0:T(8,128)S(1)} %add.88), channel_id=1, source_target_pairs={{0,2},{1,3},{2,0},{3,1},{4,6},{5,7},{6,4},{7,5},{8,10},{9,11},{10,... | collective-permute-start | bytes 122888 | tf_op jit(solution)/shard_map/ppermute | solution.py:317
  156.2 7.9 %collective-permute-start.23 = (f32[80,128]{1,0:T(8,128)S(1)}, f32[80,128]{1,0:T(8,128)S(1)}, u32[]{:S(2)}, u32[]{:S(2)}) collective-permute-start(f32[80,128]{1,0:T(8,128)S(1)} %add.89), channel_id=1, source_target_pairs={{0,4},{1,5},{2,6},{3,7},{4,0},{5,1},{6,2},{7,3},{8,12},{9,13},{10,... | collective-permute-start | bytes 122888 | tf_op jit(solution)/shard_map/ppermute | solution.py:317
  (18 other events, 575.7 us)

commit v4 on v3

v4 whole, which is shorter than its diff:
```python
import functools
import math

import jax
import jax.numpy as jnp
from jax import lax
from jax.experimental import pallas as pl
from jax.experimental.pallas import tpu as pltpu
from jax.sharding import PartitionSpec as P

HD = 128
MOST = 512
EPS = 1e-06
AXES = ("seq", "head")
CHUNKS = 2
NEAR = 3
TURNS = (2, 2, 2, 2)
RINGS = 2
VMEM = 62 * 1024 * 1024
COST = 1
SLAB = 4
FAR = -1e30


def shifted(value, steps):
    count = lax.axis_size(AXES)
    first, last = (max(0, -steps), min(count, count - steps))
    return lax.ppermute(value, AXES, [(source, source + steps) for source in range(first, last)])


def clip_start(clip_lengths, positions):
    order = jnp.arange(clip_lengths.shape[0], dtype=jnp.int32)
    begins = jnp.sum(jnp.where(order[None, :] < order[:, None], clip_lengths[None, :], 0), axis=1)
    chosen = jnp.where(
        begins[None, :] <= positions[:, None], begins[None, :], jnp.zeros((), jnp.int32)
    )
    return jnp.max(chosen, axis=1)


def nn(a, b):
    return lax.dot_general(a, b, (((1,), (0,)), ((), ())), preferred_element_type=jnp.float32)


def nt(a, b):
    return lax.dot_general(a, b, (((1,), (1,)), ((), ())), preferred_element_type=jnp.float32)


def attend_kernel(depth, repeat, skip, *refs):
    blocks = depth + 1
    starts, mod_row, queries, grads, query_gain, key_gain = refs[:6]
    key_refs = refs[6 : 6 + blocks]
    value_refs = refs[6 + blocks : 6 + 2 * blocks]
    mod_refs = refs[6 + 2 * blocks : 6 + 3 * blocks]
    rest = refs[6 + 3 * blocks + skip :]
    attended, query_back = rest[:2]
    back_refs = rest[2 : 2 + blocks]
    sums, bias, kinds = rest[2 + blocks :]
    rows = queries.shape[0]
    span = blocks * rows
    scale = 1.0 / math.sqrt(HD)
    width = SLAB * HD

    @pl.when(pl.program_id(0) == 0)
    def _():
        key_at = lax.broadcasted_iota(jnp.int32, (span, rows), 0)
        query_at = lax.broadcasted_iota(jnp.int32, (span, rows), 1) + depth * rows
        allowed = (key_at >= starts[...]) & (key_at <= query_at)
        bias[...] = jnp.where(allowed, 0.0, FAR)
        for n, ref in enumerate(mod_refs):
            row = ref[...].astype(jnp.float32)[0:1, :]
            kinds[n * rows : (n + 1) * rows, :] = jnp.broadcast_to(row, (HD, rows)).T

    key_raw = jnp.concatenate([r[...] for r in key_refs], 0).astype(jnp.float32)
    key_factor = lax.rsqrt(jnp.mean(key_raw * key_raw, axis=1, keepdims=True) + EPS)
    key_unit = key_raw * key_factor
    key_mod = kinds[...] > 0.5
    own_mod = kinds[depth * rows :, :] > 0.5
    key_norm = (key_unit * jnp.where(key_mod, key_gain[1:2, :], key_gain[0:1, :])).astype(
        jnp.bfloat16
    )
    value = jnp.concatenate([r[...] for r in value_refs], 0)
    key_turned = key_norm.T
    value_turned = value.T
    motion = mod_row[...] == 1

    sums[8:16, :] = jnp.zeros((8, HD), jnp.float32)
    key_acc = None
    value_acc = None
    for slab in range(repeat // SLAB):
        heads = [slab * SLAB + n for n in range(SLAB)]

        def turned(ref):
            return jnp.concatenate(
                [ref[:, h * HD : (h + 1) * HD].astype(jnp.float32).T for h in heads], 1
            )

        raw = turned(queries)
        grad = turned(grads)
        grad_low = grad.astype(jnp.bfloat16)
        factor = lax.rsqrt(jnp.mean(raw * raw, axis=0, keepdims=True) + EPS)
        unit = raw * factor
        gain = jnp.concatenate(
            [
                jnp.where(
                    motion,
                    query_gain[h * HD : (h + 1) * HD, 1:2],
                    query_gain[h * HD : (h + 1) * HD, 0:1],
                )
                for h in heads
            ],
            1,
        )
        query_norm = (unit * gain).astype(jnp.bfloat16)
        shield = jnp.concatenate([bias[...]] * SLAB, 1)
        scores = nn(key_norm, query_norm) * (scale * math.log2(math.e)) + shield
        expo = jnp.exp2(scores - jnp.max(scores, axis=0, keepdims=True))
        probs = expo * (1.0 / jnp.sum(expo, axis=0, keepdims=True))
        probs_low = probs.astype(jnp.bfloat16)
        seen = nn(value_turned, probs_low).astype(jnp.bfloat16)
        seen_wide = seen.astype(jnp.float32)
        delta = jnp.sum(grad * seen_wide, axis=0, keepdims=True)
        prob_grad = nn(value, grad_low)
        score_grad = (probs * (prob_grad - delta) * scale).astype(jnp.bfloat16)
        low = nn(key_turned, score_grad).astype(jnp.bfloat16).astype(jnp.float32)
        along = low * gain
        back = factor * (along - unit * jnp.mean(along * unit, axis=0, keepdims=True))
        term = low * unit
        for n, h in enumerate(heads):
            part = slice(n * HD, (n + 1) * HD)
            cols = slice(h * HD, (h + 1) * HD)
            attended[:, cols] = seen_wide[:, part].T.astype(jnp.bfloat16)
            query_back[:, cols] = back[:, part].T.astype(jnp.bfloat16)
            turn = term[:, part].T
            sums[2 * h : 2 * h + 1, :] = jnp.sum(jnp.where(own_mod, 0.0, turn), axis=0, keepdims=True)
            sums[2 * h + 1 : 2 * h + 2, :] = jnp.sum(jnp.where(own_mod, turn, 0.0), axis=0, keepdims=True)
        key_step = nt(score_grad, query_norm)
        value_step = nt(probs_low, grad_low)
        key_acc = key_step if key_acc is None else key_acc + key_step
        value_acc = value_step if value_acc is None else value_acc + value_step

    for n, ref in enumerate(back_refs):
        part = slice(n * rows, (n + 1) * rows)
        ref[:, :HD] = key_acc[part].astype(ref.dtype)
        ref[:, HD:] = value_acc[part].astype(ref.dtype)
    term = key_acc * key_unit
    of_motion = jnp.sum(jnp.where(key_mod, term, 0.0), axis=0, keepdims=True)
    of_text = jnp.sum(jnp.where(key_mod, 0.0, term), axis=0, keepdims=True)
    sums[2 * repeat : 2 * repeat + 1, :] = of_text
    sums[2 * repeat + 1 : 2 * repeat + 2, :] = of_motion


def attend(first_head, chunk_kv, starts, mod_row, queries, grads, query_gain, key_gain, held, mods, before, wide):
    rows, width = queries.shape
    kv_heads = key_gain.shape[1] // HD
    repeat = width // HD // kv_heads
    blocks = len(held)
    group = repeat * HD

    def at(shape, index):
        return pl.BlockSpec(shape, index)

    whole = lambda g: (0, 0)
    here = lambda g: (0, first_head + g)
    down = lambda g: (first_head + g, 0)
    local = here if wide else lambda g: (0, g)
    mod_at = mods[0].shape[0] // 16 - 1
    in_specs = [
        at((1, rows), whole),
        at((1, rows), whole),
        at((rows, group), here),
        at((rows, group), here),
        at((group, 2), down),
        at((2, HD), here),
    ]
    in_specs += [at((rows, HD), lambda g: (g, 0))] * blocks
    in_specs += [at((rows, HD), lambda g: (chunk_kv + g, 0))] * blocks
    in_specs += [at((16, HD), lambda g: (mod_at, 0))] * blocks
    operands = [starts, mod_row, queries, grads, query_gain, key_gain, *held, *held, *mods]
    aliases = {}
    for n, x in enumerate(before):
        if x is not None:
            aliases[len(operands)] = n
            operands.append(x)
    in_specs += [pl.BlockSpec(memory_space=pl.ANY)] * len(aliases)
    big = jax.ShapeDtypeStruct((rows, width), jnp.bfloat16)
    pair = lambda dtype: jax.ShapeDtypeStruct((rows, (kv_heads if wide else chunk_kv) * 2 * HD), dtype)
    outs = [big, big, pair(jnp.bfloat16)] + [pair(jnp.float32)] * (blocks - 1)
    outs += [jax.ShapeDtypeStruct((kv_heads * 16, HD), jnp.float32)]
    out_specs = [at((rows, group), here)] * 2
    out_specs += [at((rows, 2 * HD), local)] * blocks
    out_specs += [at((16, HD), down)]
    return pl.pallas_call(
        functools.partial(attend_kernel, blocks - 1, repeat, len(aliases)),
        grid=(chunk_kv,),
        in_specs=in_specs,
        out_specs=out_specs,
        out_shape=outs,
        scratch_shapes=[
            pltpu.VMEM((blocks * rows, rows), jnp.float32),
            pltpu.VMEM((blocks * rows, HD), jnp.float32),
        ],
        input_output_aliases=aliases,
        compiler_params=pltpu.CompilerParams(vmem_limit_bytes=VMEM),
        cost_estimate=pl.CostEstimate(
            flops=COST * chunk_kv * repeat * 12 * rows * blocks * rows * HD,
            bytes_accessed=chunk_kv * group * rows * 8 + blocks * rows * chunk_kv * HD * 12,
            transcendentals=chunk_kv * repeat * rows * blocks * rows,
        ),
        name="attend",
    )(*operands)


def finish_kernel(*refs):
    pairs, (keys, mod, key_gain, key_back, value_back) = refs[:-5], refs[-5:]
    motion = mod[...].astype(jnp.float32) > 0.5
    kv_heads = keys.shape[1] // HD
    kv = kv_heads // (len(pairs) // 2)
    for g in range(kv_heads):
        arrived, own = pairs[2 * (g // kv) : 2 * (g // kv) + 2]
        cols = slice(g * HD, (g + 1) * HD)
        at = 2 * (g % kv) * HD
        both = arrived[:, at : at + 2 * HD].astype(jnp.float32) + own[:, at : at + 2 * HD]
        low = both[:, :HD].astype(jnp.bfloat16).astype(jnp.float32)
        raw = keys[:, cols].astype(jnp.float32)
        factor = lax.rsqrt(jnp.mean(raw * raw, axis=1, keepdims=True) + EPS)
        unit = raw * factor
        along = low * jnp.where(motion, key_gain[1:2, cols], key_gain[0:1, cols])
        back = factor * (along - unit * jnp.mean(along * unit, axis=1, keepdims=True))
        key_back[:, cols] = back.astype(jnp.bfloat16)
        value_back[:, cols] = both[:, HD:].astype(jnp.bfloat16)


def finish(pairs, keys, mod_lanes, key_gain):
    low = jax.ShapeDtypeStruct(keys.shape, jnp.bfloat16)
    full = lambda x: pl.BlockSpec(x.shape, lambda g: (0, 0))
    operands = [x for pair in pairs for x in pair] + [keys, mod_lanes, key_gain]
    return pl.pallas_call(
        finish_kernel,
        grid=(1,),
        in_specs=[full(x) for x in operands],
        out_specs=[full(keys)] * 2,
        out_shape=[low, low],
        compiler_params=pltpu.CompilerParams(vmem_limit_bytes=VMEM),
        name="finish",
    )(*operands)


def after(value, *others):
    return lax.optimization_barrier((value, *others))[0]


def on_device(queries, keys, values, modality, clip_lengths, query_gains, key_gains, out_grad):
    count, width = queries.shape
    devices = lax.axis_size(AXES)
    kv_heads = keys.shape[1] // HD
    kv = kv_heads // CHUNKS
    depth = (MOST + count - 1) // count
    first = lax.axis_index(AXES) * count
    mod_lanes = jnp.broadcast_to(modality.astype(jnp.bfloat16)[:, None], (count, HD))
    mod_rows = jnp.broadcast_to(modality.astype(jnp.bfloat16)[None, :], (16, count))

    def payload(chunk):
        heads = range(chunk * kv, (chunk + 1) * kv)
        blocks = [x[:, h * HD : (h + 1) * HD] for x in (keys, values) for h in heads]
        return jnp.concatenate(blocks + ([mod_rows] if chunk == 0 else []), 0)

    ahead = [payload(0)]
    behind = [payload(1)]
    for n in range(depth):
        ahead.append(shifted(ahead[-1], 1))
        behind.append(shifted(behind[-1], 1))
    mods = ahead[::-1]

    starts = clip_start(clip_lengths, first + jnp.arange(count, dtype=jnp.int32))
    starts = (starts - first + depth * count)[None, :]
    mod_row = modality[None, :]
    gain_columns = query_gains.T

    def add(arrived, part):
        return (arrived.astype(jnp.float32) + part).astype(jnp.bfloat16)

    outs = [None] * (depth + 4)
    backs = []
    for chunk, held in enumerate((ahead, behind)):
        if RINGS > 1:
            outs = [*outs[:2], *[None] * (depth + 1), outs[-1]]
        outs = attend(
            chunk * kv,
            kv,
            starts,
            mod_row,
            queries,
            out_grad,
            gain_columns,
            key_gains,
            held[::-1],
            mods,
            outs,
            RINGS == 1,
        )
        backs.append(outs[2:-1])
    backs = backs[-RINGS:]
    attended, query_grad = outs[:2]
    gains = outs[-1]
    bits = [1 << n for n in range(devices.bit_length() - 1)]
    bits = bits[NEAR:] + bits[:NEAR]
    done = 0
    moved = [shifted(part[0], -1) for part in backs]
    for n in range(1, depth + 1):
        for bit in bits[done : done + TURNS[n - 1]]:
            gains = gains + lax.ppermute(gains, AXES, [(i, i ^ bit) for i in range(devices)])
        done += TURNS[n - 1]
        if n < depth:
            sent = [add(arrived, part[n]) for arrived, part in zip(moved, backs)]
            gains = after(gains, sent[0])
            sent[-1] = after(sent[-1], gains) if RINGS > 1 else sent[-1]
            moved = [shifted(x, -1) for x in sent]
    key_grad, value_grad = finish(
        [(arrived, part[depth]) for arrived, part in zip(moved, backs)], keys, mod_lanes, key_gains
    )
    per_kv = gains.reshape(kv_heads, 8, 2, HD)
    repeat = width // HD // kv_heads
    query_gain = jnp.transpose(per_kv[:, :repeat], (2, 0, 1, 3)).reshape(2, -1)
    key_gain = jnp.transpose(per_kv[:, repeat], (1, 0, 2)).reshape(2, -1)
    return attended, query_grad, key_grad, value_grad, query_gain, key_gain


def solution(mesh):
    rows = P(AXES, None)
    return jax.shard_map(
        on_device,
        mesh=mesh,
        in_specs=(rows, rows, rows, P(AXES), P(), P(), P(), rows),
        out_specs=(rows, rows, rows, rows, P(), P()),
        check_vma=False,
    )
```

time: 170 us -> 162 us (0.953)
  waiting for transfers between devices: 68.6 us -> 62.6 us
  Pallas kernels: 26.4 us -> 23.1 us
  starting transfers between devices: 60.4 us -> 57.5 us
  local copies, waits for them, and re-layouts: 9.24 us -> 11.8 us
    unnamed x37 -> x39, local copies, waits for them, and re-layouts: 3.54 us -> 9.82 us
    slice x7 -> x1, local copies, waits for them, and re-layouts: 5.56 us -> 0.62 us  [on_device(): query_gain = jnp.transpose(per_kv[:, :repeat], (2, 0, 1, 3)).reshape(2, -1)]
    ppermute x8, waiting for transfers between devices: 23 us -> 18.2 us  [on_device(): lax.ppermute(gains, AXES, [(i, i ^ bit) for i in range(devices)])]
    pallas_call x2, Pallas kernels: 23.7 us -> 20.4 us  [attend(): pl.pallas_call(functools.partial(attend_kernel, blocks - 1, repeat, len(a...]
    ppermute x16, starting transfers between devices: 54.5 us -> 52.3 us  [shifted(): lax.ppermute(value, AXES, [(source, source + steps) for source in range(f...]
  transfers between devices with their start and end apart: 24 -> 24, of which waited for: 14 -> 16; matrix products, arithmetic and copies ran while one was open for 3% -> 5% of each run, Pallas kernels for 7% -> 13%
where the time goes in v4:
time: 162 us; the launch traced here: 161 us
  waiting for transfers between devices  62.6 us (39%)
  starting transfers between devices  57.5 us (35%)
  Pallas kernels  23.1 us (14%)
  local copies, waits for them, and re-layouts  11.8 us (7%)
  other arithmetic  4.4 us (3%)
    ppermute x16, starting transfers between devices, shifted(): lax.ppermute(value, AXES, [(source, source + steps) for source in range(f...  52.3 us
    ppermute x16, waiting for transfers between devices, shifted(): lax.ppermute(value, AXES, [(source, source + steps) for source in range(f...  44.4 us
    pallas_call x2, Pallas kernels, attend(): pl.pallas_call(functools.partial(attend_kernel, blocks - 1, repeat, len(a...  20.4 us
    ppermute x8, waiting for transfers between devices, on_device(): lax.ppermute(gains, AXES, [(i, i ^ bit) for i in range(devices)])  18.2 us
    unnamed x39, local copies, waits for them, and re-layouts  9.82 us
    ppermute x8, starting transfers between devices, on_device(): lax.ppermute(gains, AXES, [(i, i ^ bit) for i in range(devices)])  5.22 us
  transfers between devices with their start and end apart: 24, of which 16 were waited for; matrix products, arithmetic and copies ran while one was open for 5% of the time, Pallas kernels for 13%

profile of v4, /device:TPU:2, one launch (start us, length us, event | category | flops | bytes accessed | tf_op | source)
XLA Modules:
  0.0 160.6 jit_solution(15241159703120178853)
XLA Ops:
  7.6 3.8 %collective-permute-start.4 = (bf16[1040,128]{1,0:T(8,128)(2,1)S(1)}, bf16[1040,128]{1,0:T(8,128)(2,1)S(1)}, u32[]{:S(2)}, u32[]{:S(2)}) collective-permute-start(bf16[1040,128]{1,0:T(8,128)(2,1)S(1)} %constant_dynamic-update-slice_fusion.8.refs_10_.refs_15_.refs_20_), channel_id=1, source_target_pairs={{0,1},{1,2},{2,3},{3,4},{4,5},{5,6},{6,7},{7,8},{8,9},{9,10},{10,1... | collective-permute-start | bytes 798728 | tf_op jit(solution)/shard_map/ppermute | solution.py:28
  11.5 3.8 %collective-permute-start = (bf16[1024,128]{1,0:T(8,128)(2,1)S(1)}, bf16[1024,128]{1,0:T(8,128)(2,1)S(1)}, u32[]{:S(2)}, u32[]{:S(2)}) collective-permute-start(bf16[1024,128]{1,0:T(8,128)(2,1)S(1)} %get-tuple-element.55.refs_10_.refs_15_), channel_id=1, source_target_pairs={{0,1},{1,2},{2,3},{3,4},{4,5},{5,6},{6,7},{7,8},{8,9},{9,10},{10,1... | collective-permute-start | bytes 786440 | tf_op jit(solution)/shard_map/ppermute | solution.py:28
  15.3 8.1 %collective-permute-done.4.refs_9_.refs_14_.refs_19_ = bf16[1040,128]{1,0:T(8,128)(2,1)S(1)} collective-permute-done((bf16[1040,128]{1,0:T(8,128)(2,1)S(1)}, bf16[1040,128]{1,0:T(8,128)(2,1)S(1)}, u32[]{:S(2)}, u32[]{:S(2)}) %collective-permute-start.4) | collective-permute-done | bytes 266272 | tf_op jit(solution)/shard_map/ppermute | solution.py:28
  25.3 3.7 %collective-permute-done.refs_9_.refs_14_ = bf16[1024,128]{1,0:T(8,128)(2,1)S(1)} collective-permute-done((bf16[1024,128]{1,0:T(8,128)(2,1)S(1)}, bf16[1024,128]{1,0:T(8,128)(2,1)S(1)}, u32[]{:S(2)}, u32[]{:S(2)}) %collective-permute-start) | collective-permute-done | bytes 262176 | tf_op jit(solution)/shard_map/ppermute | solution.py:28
  30.9 6.7 %collective-permute-done.5.refs_8_.refs_13_.refs_18_ = bf16[1040,128]{1,0:T(8,128)(2,1)S(1)} collective-permute-done((bf16[1040,128]{1,0:T(8,128)(2,1)S(1)}, bf16[1040,128]{1,0:T(8,128)(2,1)S(1)}, u32[]{:S(2)}, u32[]{:S(2)}) %collective-permute-start.5) | collective-permute-done | bytes 266272 | tf_op jit(solution)/shard_map/ppermute | solution.py:28
  39.6 4.4 %collective-permute-done.1.refs_8_.refs_13_ = bf16[1024,128]{1,0:T(8,128)(2,1)S(1)} collective-permute-done((bf16[1024,128]{1,0:T(8,128)(2,1)S(1)}, bf16[1024,128]{1,0:T(8,128)(2,1)S(1)}, u32[]{:S(2)}, u32[]{:S(2)}) %collective-permute-start.1) | collective-permute-done | bytes 262176 | tf_op jit(solution)/shard_map/ppermute | solution.py:28
  46.7 5.7 %collective-permute-done.6.refs_7_.refs_12_.refs_17_ = bf16[1040,128]{1,0:T(8,128)(2,1)S(1)} collective-permute-done((bf16[1040,128]{1,0:T(8,128)(2,1)S(1)}, bf16[1040,128]{1,0:T(8,128)(2,1)S(1)}, u32[]{:S(2)}, u32[]{:S(2)}) %collective-permute-start.6) | collective-permute-done | bytes 266272 | tf_op jit(solution)/shard_map/ppermute | solution.py:28
  54.5 3.7 %collective-permute-done.2.refs_7_.refs_12_ = bf16[1024,128]{1,0:T(8,128)(2,1)} collective-permute-done((bf16[1024,128]{1,0:T(8,128)(2,1)S(1)}, bf16[1024,128]{1,0:T(8,128)(2,1)}, u32[]{:S(2)}, u32[]{:S(2)}) %collective-permute-start.2) | collective-permute-done | bytes 262176 | tf_op jit(solution)/shard_map/ppermute | solution.py:28
  60.6 2.8 %copy.20 = f32[2,4096]{0,1:T(8,128)} copy(f32[2,4096]{1,0:T(2,128)} %param.13) | data formatting | bytes 65536 | tf_op args[5]
  63.3 3.0 %collective-permute-done.7.refs_6_.refs_11_.refs_16_ = bf16[1040,128]{1,0:T(8,128)(2,1)S(1)} collective-permute-done((bf16[1040,128]{1,0:T(8,128)(2,1)S(1)}, bf16[1040,128]{1,0:T(8,128)(2,1)S(1)}, u32[]{:S(2)}, u32[]{:S(2)}) %collective-permute-start.7) | collective-permute-done | bytes 266272 | tf_op jit(solution)/shard_map/ppermute | solution.py:28
  67.1 10.1 %attend.2 = (bf16[128,4096]{1,0:T(8,128)(2,1)}, bf16[128,4096]{1,0:T(8,128)(2,1)}, bf16[128,1024]{1,0:T(8,128)(2,1)}, f32[128,1024]{1,0:T(8,128)}, f32[128,1024]...) custom-call(s32[1,128]{1,0:T(1,128)} %add_bitcast_fusion.refs_0_, s32[1,128]{1,0:T(1,128)} %bitcast.19, ...), custom_call_target="tpu_custom_call" | custom-call | flops 2013265920 | bytes 6029312 | tf_op jit(solution)/shard_map/attend/pallas_call | solution.py:192
  77.2 4.9 %collective-permute-start.8 = (bf16[128,1024]{1,0:T(8,128)(2,1)}, bf16[128,1024]{1,0:T(8,128)(2,1)S(1)}, u32[]{:S(2)}, u32[]{:S(2)}) collective-permute-start(bf16[128,1024]{1,0:T(8,128)(2,1)} %get-tuple-element.35), channel_id=1, source_target_pairs={{1,0},{2,1},{3,2},{4,3},{5,4},{6,5},{7,6},{8,7},{9,8},{10,9},{11,1... | collective-permute-start | bytes 786440 | tf_op jit(solution)/shard_map/ppermute | solution.py:28
  82.1 10.3 %attend.3 = (bf16[128,4096]{1,0:T(8,128)(2,1)}, bf16[128,4096]{1,0:T(8,128)(2,1)}, bf16[128,1024]{1,0:T(8,128)(2,1)}, f32[128,1024]{1,0:T(8,128)}, f32[128,1024]...) custom-call(s32[1,128]{1,0:T(1,128)} %add_bitcast_fusion.refs_0_, ...), custom_call_target="tpu_custom_call", output_to_operand_aliasing={{0}: (21, {}), {1}: (22, {}), {7}: (23, {})} | custom-call | flops 2013265920 | bytes 6029312 | tf_op jit(solution)/shard_map/attend/pallas_call | solution.py:192
  92.5 5.1 %collective-permute-done.13 = f32[128,128]{1,0:T(8,128)S(1)} collective-permute-done((f32[128,128]{1,0:T(8,128)}, f32[128,128]{1,0:T(8,128)S(1)}, u32[]{:S(2)}, u32[]{:S(2)}) %collective-permute-start.13) | collective-permute-done | bytes 65568 | tf_op jit(solution)/shard_map/ppermute | solution.py:311
  100.4 3.8 %collective-permute-done.14 = f32[128,128]{1,0:T(8,128)S(1)} collective-permute-done((f32[128,128]{1,0:T(8,128)S(1)}, f32[128,128]{1,0:T(8,128)S(1)}, u32[]{:S(2)}, u32[]{:S(2)}) %collective-permute-start.14) | collective-permute-done | bytes 65568 | tf_op jit(solution)/shard_map/ppermute | solution.py:311
  108.1 6.8 %collective-permute-start.15 = (bf16[128,1024]{1,0:T(8,128)(2,1)S(1)}, bf16[128,1024]{1,0:T(8,128)(2,1)S(1)}, u32[]{:S(2)}, u32[]{:S(2)}) collective-permute-start(bf16[128,1024]{1,0:T(8,128)(2,1)S(1)} %add_convert_fusion.2), channel_id=1, source_target_pairs={{1,0},{2,1},{3,2},{4,3},{5,4},{6,5},{7,6},{8,7},{9,8},{10,9},{11,1... | collective-permute-start | bytes 786440 | tf_op jit(solution)/shard_map/ppermute | solution.py:28
  115.7 4.7 %collective-permute-start.19 = (f32[128,128]{1,0:T(8,128)S(1)}, f32[128,128]{1,0:T(8,128)S(1)}, u32[]{:S(2)}, u32[]{:S(2)}) collective-permute-start(f32[128,128]{1,0:T(8,128)S(1)} %add.85), channel_id=1, source_target_pairs={{0,128},{1,129},{2,130},{3,131},{4,132},{5,133},{6,134},{7,135},{8... | collective-permute-start | bytes 196616 | tf_op jit(solution)/shard_map/ppermute | solution.py:311
  120.3 6.5 %collective-permute-start.10 = (bf16[128,1024]{1,0:T(8,128)(2,1)S(1)}, bf16[128,1024]{1,0:T(8,128)(2,1)S(1)}, u32[]{:S(2)}, u32[]{:S(2)}) collective-permute-start(bf16[128,1024]{1,0:T(8,128)(2,1)S(1)} %add_convert_fusion.4), channel_id=1, source_target_pairs={{1,0},{2,1},{3,2},{4,3},{5,4},{6,5},{7,6},{8,7},{9,8},{10,9},{11,1... | collective-permute-start | bytes 786440 | tf_op jit(solution)/shard_map/ppermute | solution.py:28
  128.9 2.9 %collective-permute-done.20 = f32[128,128]{1,0:T(8,128)S(1)} collective-permute-done((f32[128,128]{1,0:T(8,128)S(1)}, f32[128,128]{1,0:T(8,128)S(1)}, u32[]{:S(2)}, u32[]{:S(2)}) %collective-permute-start.20) | collective-permute-done | bytes 65568 | tf_op jit(solution)/shard_map/ppermute | solution.py:311
  133.7 6.3 %collective-permute-done.22 = f32[128,128]{1,0:T(8,128)S(1)} collective-permute-done((f32[128,128]{1,0:T(8,128)S(1)}, f32[128,128]{1,0:T(8,128)S(1)}, u32[]{:S(2)}, u32[]{:S(2)}) %collective-permute-start.22) | collective-permute-done | bytes 65568 | tf_op jit(solution)/shard_map/ppermute | solution.py:311
  140.3 7.2 %collective-permute-start.21 = (bf16[128,1024]{1,0:T(8,128)(2,1)S(1)}, bf16[128,1024]{1,0:T(8,128)(2,1)S(1)}, u32[]{:S(2)}, u32[]{:S(2)}) collective-permute-start(bf16[128,1024]{1,0:T(8,128)(2,1)S(1)} %add_convert_fusion), channel_id=1, source_target_pairs={{1,0},{2,1},{3,2},{4,3},{5,4},{6,5},{7,6},{8,7},{9,8},{10,9},{11,1... | collective-permute-start | bytes 786440 | tf_op jit(solution)/shard_map/ppermute | solution.py:28
  150.7 3.6 %collective-permute-done.21.refs_2_ = bf16[128,1024]{1,0:T(8,128)(2,1)S(1)} collective-permute-done((bf16[128,1024]{1,0:T(8,128)(2,1)S(1)}, bf16[128,1024]{1,0:T(8,128)(2,1)S(1)}, u32[]{:S(2)}, u32[]{:S(2)}) %collective-permute-start.21) | collective-permute-done | bytes 262176 | tf_op jit(solution)/shard_map/ppermute | solution.py:28
  154.3 2.8 %collective-permute-done.11.refs_0_ = bf16[128,1024]{1,0:T(8,128)(2,1)S(1)} collective-permute-done((bf16[128,1024]{1,0:T(8,128)(2,1)S(1)}, bf16[128,1024]{1,0:T(8,128)(2,1)S(1)}, u32[]{:S(2)}, u32[]{:S(2)}) %collective-permute-start.11) | collective-permute-done | bytes 262176 | tf_op jit(solution)/shard_map/ppermute | solution.py:28
  157.9 2.7 %finish.1 = (bf16[128,1024]{1,0:T(8,128)(2,1)}, bf16[128,1024]{1,0:T(8,128)(2,1)}) custom-call(bf16[128,1024]{1,0:T(8,128)(2,1)} %copy-done.14, f32[128,1024]{1,0:T(8,128)} %get-tuple-element.39.refs_1_, bf16[128,1024]{1,0:T(8,128)(2,1)} %copy-done.13, f32[128,1024]{1,0:T(8,128)} %get-tuple-element.51.refs_3_, bf16[128,1024]{1,0:T(8,128)(2,1)} %refs_4_.1, ...), custom_call_target="tpu_custom_call" | custom-call | tf_op jit(solution)/shard_map/finish/pallas_call | solution.py:237
  (89 shorter events, 35.9 us)
Async XLA Ops:
  7.6 15.7 %collective-permute-start.4 = (bf16[1040,128]{1,0:T(8,128)(2,1)S(1)}, bf16[1040,128]{1,0:T(8,128)(2,1)S(1)}, u32[]{:S(2)}, u32[]{:S(2)}) collective-permute-start(bf16[1040,128]{1,0:T(8,128)(2,1)S(1)} %constant_dynamic-update-slice_fusion.8.refs_10_.refs_15_.refs_20_), channel_id=1, source_target_pairs={{0,1},{1,2},{2,3},{3,4},{4,5},{5,6},{6,7},{7,8},{8,9},{9,10},{10,1... | collective-permute-start | bytes 798728 | tf_op jit(solution)/shard_map/ppermute | solution.py:28
  11.5 17.5 %collective-permute-start = (bf16[1024,128]{1,0:T(8,128)(2,1)S(1)}, bf16[1024,128]{1,0:T(8,128)(2,1)S(1)}, u32[]{:S(2)}, u32[]{:S(2)}) collective-permute-start(bf16[1024,128]{1,0:T(8,128)(2,1)S(1)} %get-tuple-element.55.refs_10_.refs_15_), channel_id=1, source_target_pairs={{0,1},{1,2},{2,3},{3,4},{4,5},{5,6},{6,7},{7,8},{8,9},{9,10},{10,1... | collective-permute-start | bytes 786440 | tf_op jit(solution)/shard_map/ppermute | solution.py:28
  23.4 14.2 %collective-permute-start.5 = (bf16[1040,128]{1,0:T(8,128)(2,1)S(1)}, bf16[1040,128]{1,0:T(8,128)(2,1)S(1)}, u32[]{:S(2)}, u32[]{:S(2)}) collective-permute-start(bf16[1040,128]{1,0:T(8,128)(2,1)S(1)} %collective-permute-done.4.refs_9_.refs_14_.refs_19_), channel_id=1, source_target_pairs={{0,1},{1,2},{2,3},{3,4},{4,5},{5,6},{6,7},{7,8},{8,9},{9,10},{10,1... | collective-permute-start | bytes 798728 | tf_op jit(solution)/shard_map/ppermute | solution.py:28
  29.0 14.9 %collective-permute-start.1 = (bf16[1024,128]{1,0:T(8,128)(2,1)S(1)}, bf16[1024,128]{1,0:T(8,128)(2,1)S(1)}, u32[]{:S(2)}, u32[]{:S(2)}) collective-permute-start(bf16[1024,128]{1,0:T(8,128)(2,1)S(1)} %collective-permute-done.refs_9_.refs_14_), channel_id=1, source_target_pairs={{0,1},{1,2},{2,3},{3,4},{4,5},{5,6},{6,7},{7,8},{8,9},{9,10},{10,1... | collective-permute-start | bytes 786440 | tf_op jit(solution)/shard_map/ppermute | solution.py:28
  37.6 14.7 %collective-permute-start.6 = (bf16[1040,128]{1,0:T(8,128)(2,1)S(1)}, bf16[1040,128]{1,0:T(8,128)(2,1)S(1)}, u32[]{:S(2)}, u32[]{:S(2)}) collective-permute-start(bf16[1040,128]{1,0:T(8,128)(2,1)S(1)} %collective-permute-done.5.refs_8_.refs_13_.refs_18_), channel_id=1, source_target_pairs={{0,1},{1,2},{2,3},{3,4},{4,5},{5,6},{6,7},{7,8},{8,9},{9,10},{10,1... | collective-permute-start | bytes 798728 | tf_op jit(solution)/shard_map/ppermute | solution.py:28
  44.0 14.2 %collective-permute-start.2 = (bf16[1024,128]{1,0:T(8,128)(2,1)S(1)}, bf16[1024,128]{1,0:T(8,128)(2,1)}, u32[]{:S(2)}, u32[]{:S(2)}) collective-permute-start(bf16[1024,128]{1,0:T(8,128)(2,1)S(1)} %collective-permute-done.1.refs_8_.refs_13_), channel_id=1, source_target_pairs={{0,1},{1,2},{2,3},{3,4},{4,5},{5,6},{6,7},{7,8},{8,9},{9,10},{10,1... | collective-permute-start | bytes 786440 | tf_op jit(solution)/shard_map/ppermute | solution.py:28
  52.4 14.0 %collective-permute-start.7 = (bf16[1040,128]{1,0:T(8,128)(2,1)S(1)}, bf16[1040,128]{1,0:T(8,128)(2,1)S(1)}, u32[]{:S(2)}, u32[]{:S(2)}) collective-permute-start(bf16[1040,128]{1,0:T(8,128)(2,1)S(1)} %collective-permute-done.6.refs_7_.refs_12_.refs_17_), channel_id=1, source_target_pairs={{0,1},{1,2},{2,3},{3,4},{4,5},{5,6},{6,7},{7,8},{8,9},{9,10},{10,1... | collective-permute-start | bytes 798728 | tf_op jit(solution)/shard_map/ppermute | solution.py:28
  58.2 24.0 %collective-permute-start.3 = (bf16[1024,128]{1,0:T(8,128)(2,1)}, bf16[1024,128]{1,0:T(8,128)(2,1)}, u32[]{:S(2)}, u32[]{:S(2)}) collective-permute-start(bf16[1024,128]{1,0:T(8,128)(2,1)} %collective-permute-done.2.refs_7_.refs_12_), channel_id=1, source_target_pairs={{0,1},{1,2},{2,3},{3,4},{4,5},{5,6},{6,7},{7,8},{8,9},{9,10},{10,1... | collective-permute-start | bytes 786440 | tf_op jit(solution)/shard_map/ppermute | solution.py:28
  77.2 27.0 %collective-permute-start.8 = (bf16[128,1024]{1,0:T(8,128)(2,1)}, bf16[128,1024]{1,0:T(8,128)(2,1)S(1)}, u32[]{:S(2)}, u32[]{:S(2)}) collective-permute-start(bf16[128,1024]{1,0:T(8,128)(2,1)} %get-tuple-element.35), channel_id=1, source_target_pairs={{1,0},{2,1},{3,2},{4,3},{5,4},{6,5},{7,6},{8,7},{9,8},{10,9},{11,1... | collective-permute-start | bytes 786440 | tf_op jit(solution)/shard_map/ppermute | solution.py:28
  92.4 5.2 %collective-permute-start.13 = (f32[128,128]{1,0:T(8,128)}, f32[128,128]{1,0:T(8,128)S(1)}, u32[]{:S(2)}, u32[]{:S(2)}) collective-permute-start(f32[128,128]{1,0:T(8,128)} %get-tuple-element.42), channel_id=1, source_target_pairs={{0,8},{1,9},{2,10},{3,11},{4,12},{5,13},{6,14},{7,15},{8,0},{9,1},... | collective-permute-start | bytes 196616 | tf_op jit(solution)/shard_map/ppermute | solution.py:311
  98.5 5.8 %collective-permute-start.14 = (f32[128,128]{1,0:T(8,128)S(1)}, f32[128,128]{1,0:T(8,128)S(1)}, u32[]{:S(2)}, u32[]{:S(2)}) collective-permute-start(f32[128,128]{1,0:T(8,128)S(1)} %add.81), channel_id=1, source_target_pairs={{0,16},{1,17},{2,18},{3,19},{4,20},{5,21},{6,22},{7,23},{8,24},{9,... | collective-permute-start | bytes 196616 | tf_op jit(solution)/shard_map/ppermute | solution.py:311
  98.5 8.5 %collective-permute-start.12 = (bf16[128,1024]{1,0:T(8,128)(2,1)}, bf16[128,1024]{1,0:T(8,128)(2,1)S(1)}, u32[]{:S(2)}, u32[]{:S(2)}) collective-permute-start(bf16[128,1024]{1,0:T(8,128)(2,1)} %get-tuple-element.40), channel_id=1, source_target_pairs={{1,0},{2,1},{3,2},{4,3},{5,4},{6,5},{7,6},{8,7},{9,8},{10,9},{11,1... | collective-permute-start | bytes 786440 | tf_op jit(solution)/shard_map/ppermute | solution.py:28
  104.3 2.2 %collective-permute-start.16 = (f32[128,128]{1,0:T(8,128)S(1)}, f32[128,128]{1,0:T(8,128)S(1)}, u32[]{:S(2)}, u32[]{:S(2)}) collective-permute-start(f32[128,128]{1,0:T(8,128)S(1)} %add.82), channel_id=1, source_target_pairs={{0,32},{1,33},{2,34},{3,35},{4,36},{5,37},{6,38},{7,39},{8,40},{9,... | collective-permute-start | bytes 196616 | tf_op jit(solution)/shard_map/ppermute | solution.py:311
  104.4 11.1 %collective-permute-start.9 = (bf16[128,1024]{1,0:T(8,128)(2,1)S(1)}, bf16[128,1024]{1,0:T(8,128)(2,1)S(1)}, u32[]{:S(2)}, u32[]{:S(2)}) collective-permute-start(bf16[128,1024]{1,0:T(8,128)(2,1)S(1)} %add_convert_fusion.5), channel_id=1, source_target_pairs={{1,0},{2,1},{3,2},{4,3},{5,4},{6,5},{7,6},{8,7},{9,8},{10,9},{11,1... | collective-permute-start | bytes 786440 | tf_op jit(solution)/shard_map/ppermute | solution.py:28
  106.5 8.4 %collective-permute-start.17 = (f32[128,128]{1,0:T(8,128)S(1)}, f32[128,128]{1,0:T(8,128)S(1)}, u32[]{:S(2)}, u32[]{:S(2)}) collective-permute-start(f32[128,128]{1,0:T(8,128)S(1)} %add.84), channel_id=1, source_target_pairs={{0,64},{1,65},{2,66},{3,67},{4,68},{5,69},{6,70},{7,71},{8,72},{9,... | collective-permute-start | bytes 196616 | tf_op jit(solution)/shard_map/ppermute | solution.py:311
  108.1 18.8 %collective-permute-start.15 = (bf16[128,1024]{1,0:T(8,128)(2,1)S(1)}, bf16[128,1024]{1,0:T(8,128)(2,1)S(1)}, u32[]{:S(2)}, u32[]{:S(2)}) collective-permute-start(bf16[128,1024]{1,0:T(8,128)(2,1)S(1)} %add_convert_fusion.2), channel_id=1, source_target_pairs={{1,0},{2,1},{3,2},{4,3},{5,4},{6,5},{7,6},{8,7},{9,8},{10,9},{11,1... | collective-permute-start | bytes 786440 | tf_op jit(solution)/shard_map/ppermute | solution.py:28
  115.7 11.1 %collective-permute-start.19 = (f32[128,128]{1,0:T(8,128)S(1)}, f32[128,128]{1,0:T(8,128)S(1)}, u32[]{:S(2)}, u32[]{:S(2)}) collective-permute-start(f32[128,128]{1,0:T(8,128)S(1)} %add.85), channel_id=1, source_target_pairs={{0,128},{1,129},{2,130},{3,131},{4,132},{5,133},{6,134},{7,135},{8... | collective-permute-start | bytes 196616 | tf_op jit(solution)/shard_map/ppermute | solution.py:311
  120.3 13.2 %collective-permute-start.10 = (bf16[128,1024]{1,0:T(8,128)(2,1)S(1)}, bf16[128,1024]{1,0:T(8,128)(2,1)S(1)}, u32[]{:S(2)}, u32[]{:S(2)}) collective-permute-start(bf16[128,1024]{1,0:T(8,128)(2,1)S(1)} %add_convert_fusion.4), channel_id=1, source_target_pairs={{1,0},{2,1},{3,2},{4,3},{5,4},{6,5},{7,6},{8,7},{9,8},{10,9},{11,1... | collective-permute-start | bytes 786440 | tf_op jit(solution)/shard_map/ppermute | solution.py:28
  126.8 5.0 %collective-permute-start.20 = (f32[128,128]{1,0:T(8,128)S(1)}, f32[128,128]{1,0:T(8,128)S(1)}, u32[]{:S(2)}, u32[]{:S(2)}) collective-permute-start(f32[128,128]{1,0:T(8,128)S(1)} %add.87), channel_id=1, source_target_pairs={{0,1},{1,0},{2,3},{3,2},{4,5},{5,4},{6,7},{7,6},{8,9},{9,8},{10,11... | collective-permute-start | bytes 196616 | tf_op jit(solution)/shard_map/ppermute | solution.py:311
  127.0 13.2 %collective-permute-start.18 = (bf16[128,1024]{1,0:T(8,128)(2,1)S(1)}, bf16[128,1024]{1,0:T(8,128)(2,1)S(1)}, u32[]{:S(2)}, u32[]{:S(2)}) collective-permute-start(bf16[128,1024]{1,0:T(8,128)(2,1)S(1)} %add_convert_fusion.1), channel_id=1, source_target_pairs={{1,0},{2,1},{3,2},{4,3},{5,4},{6,5},{7,6},{8,7},{9,8},{10,9},{11,1... | collective-permute-start | bytes 786440 | tf_op jit(solution)/shard_map/ppermute | solution.py:28
  133.6 6.4 %collective-permute-start.22 = (f32[128,128]{1,0:T(8,128)S(1)}, f32[128,128]{1,0:T(8,128)S(1)}, u32[]{:S(2)}, u32[]{:S(2)}) collective-permute-start(f32[128,128]{1,0:T(8,128)S(1)} %add.88), channel_id=1, source_target_pairs={{0,2},{1,3},{2,0},{3,1},{4,6},{5,7},{6,4},{7,5},{8,10},{9,11},{10,... | collective-permute-start | bytes 196616 | tf_op jit(solution)/shard_map/ppermute | solution.py:311
  140.1 9.4 %collective-permute-start.23 = (f32[128,128]{1,0:T(8,128)S(1)}, f32[128,128]{1,0:T(8,128)S(1)}, u32[]{:S(2)}, u32[]{:S(2)}) collective-permute-start(f32[128,128]{1,0:T(8,128)S(1)} %add.89), channel_id=1, source_target_pairs={{0,4},{1,5},{2,6},{3,7},{4,0},{5,1},{6,2},{7,3},{8,12},{9,13},{10,... | collective-permute-start | bytes 196616 | tf_op jit(solution)/shard_map/ppermute | solution.py:311
  140.3 14.0 %collective-permute-start.21 = (bf16[128,1024]{1,0:T(8,128)(2,1)S(1)}, bf16[128,1024]{1,0:T(8,128)(2,1)S(1)}, u32[]{:S(2)}, u32[]{:S(2)}) collective-permute-start(bf16[128,1024]{1,0:T(8,128)(2,1)S(1)} %add_convert_fusion), channel_id=1, source_target_pairs={{1,0},{2,1},{3,2},{4,3},{5,4},{6,5},{7,6},{8,7},{9,8},{10,9},{11,1... | collective-permute-start | bytes 786440 | tf_op jit(solution)/shard_map/ppermute | solution.py:28
  147.5 9.6 %collective-permute-start.11 = (bf16[128,1024]{1,0:T(8,128)(2,1)S(1)}, bf16[128,1024]{1,0:T(8,128)(2,1)S(1)}, u32[]{:S(2)}, u32[]{:S(2)}) collective-permute-start(bf16[128,1024]{1,0:T(8,128)(2,1)S(1)} %add_convert_fusion.3), channel_id=1, source_target_pairs={{1,0},{2,1},{3,2},{4,3},{5,4},{6,5},{7,6},{8,7},{9,8},{10,9},{11,1... | collective-permute-start | bytes 786440 | tf_op jit(solution)/shard_map/ppermute | solution.py:28
  (15 other events, 430.8 us)

commit v5 on v4

--- a/solution.py
+++ b/solution.py
@@ -16,6 +16,9 @@
 NEAR = 3
 TURNS = (2, 2, 2, 2)
 RINGS = 2
+PRE = False
+TIEB = True
+EARLY = True
 VMEM = 62 * 1024 * 1024
 COST = 1
 SLAB = 4
@@ -264,17 +267,17 @@
         blocks = [x[:, h * HD : (h + 1) * HD] for x in (keys, values) for h in heads]
         return jnp.concatenate(blocks + ([mod_rows] if chunk == 0 else []), 0)
 
+    starts = clip_start(clip_lengths, first + jnp.arange(count, dtype=jnp.int32))
+    starts = (starts - first + depth * count)[None, :]
+    gain_columns = query_gains.T
     ahead = [payload(0)]
     behind = [payload(1)]
     for n in range(depth):
-        ahead.append(shifted(ahead[-1], 1))
+        ahead.append(shifted(after(ahead[-1], gain_columns, starts) if EARLY and n == 2 else ahead[-1], 1))
         behind.append(shifted(behind[-1], 1))
     mods = ahead[::-1]
 
-    starts = clip_start(clip_lengths, first + jnp.arange(count, dtype=jnp.int32))
-    starts = (starts - first + depth * count)[None, :]
     mod_row = modality[None, :]
-    gain_columns = query_gains.T
 
     def add(arrived, part):
         return (arrived.astype(jnp.float32) + part).astype(jnp.bfloat16)
@@ -304,16 +307,22 @@
     gains = outs[-1]
     bits = [1 << n for n in range(devices.bit_length() - 1)]
     bits = bits[NEAR:] + bits[:NEAR]
-    done = 0
     moved = [shifted(part[0], -1) for part in backs]
+    if PRE:
+        gains = after(gains, moved[0])
     for n in range(1, depth + 1):
-        for bit in bits[done : done + TURNS[n - 1]]:
-            gains = gains + lax.ppermute(gains, AXES, [(i, i ^ bit) for i in range(devices)])
-        done += TURNS[n - 1]
         if n < depth:
             sent = [add(arrived, part[n]) for arrived, part in zip(moved, backs)]
-            gains = after(gains, sent[0])
-            sent[-1] = after(sent[-1], gains) if RINGS > 1 else sent[-1]
+            if PRE:
+                gains = after(gains, sent[0])
+        for _ in range(TURNS[n - 1]):
+            bit = bits.pop(0)
+            gains = gains + lax.ppermute(gains, AXES, [(i, i ^ bit) for i in range(devices)])
+        if n < depth:
+            if not PRE:
+                gains = after(gains, sent[0])
+            if TIEB:
+                sent[-1] = after(sent[-1], gains)
             moved = [shifted(x, -1) for x in sent]
     key_grad, value_grad = finish(
         [(arrived, part[depth]) for arrived, part in zip(moved, backs)], keys, mod_lanes, key_gains

time: 162 us -> 158 us (0.975)
  starting transfers between devices: 57.5 us -> 54.1 us
    ppermute x16, starting transfers between devices: 52.3 us -> 49.5 us  [shifted(): lax.ppermute(value, AXES, [(source, source + steps) for source in range(f...]
where the time goes in v5:
time: 158 us; the launch traced here: 156 us
  waiting for transfers between devices  61.4 us (39%)
  starting transfers between devices  54.1 us (34%)
  Pallas kernels  23.1 us (15%)
  local copies, waits for them, and re-layouts  11.8 us (7%)
  other arithmetic  4.4 us (3%)
    ppermute x16, starting transfers between devices, shifted(): lax.ppermute(value, AXES, [(source, source + steps) for source in range(f...  49.5 us
    ppermute x16, waiting for transfers between devices, shifted(): lax.ppermute(value, AXES, [(source, source + steps) for source in range(f...  43.7 us
    pallas_call x2, Pallas kernels, attend(): pl.pallas_call(functools.partial(attend_kernel, blocks - 1, repeat, len(a...  20.4 us
    ppermute x8, waiting for transfers between devices, on_device(): lax.ppermute(gains, AXES, [(i, i ^ bit) for i in range(devices)])  17.7 us
    unnamed x39, local copies, waits for them, and re-layouts  9.82 us
    ppermute x8, starting transfers between devices, on_device(): lax.ppermute(gains, AXES, [(i, i ^ bit) for i in range(devices)])  4.59 us
  transfers between devices with their start and end apart: 24, of which 16 were waited for; matrix products, arithmetic and copies ran while one was open for 5% of the time, Pallas kernels for 13%

profile of v5, /device:TPU:2, one launch (start us, length us, event | category | flops | bytes accessed | tf_op | source)
XLA Modules:
  0.0 155.9 jit_solution(18078565752758603393)
XLA Ops:
  7.6 3.8 %collective-permute-start.4 = (bf16[1040,128]{1,0:T(8,128)(2,1)S(1)}, bf16[1040,128]{1,0:T(8,128)(2,1)S(1)}, u32[]{:S(2)}, u32[]{:S(2)}) collective-permute-start(bf16[1040,128]{1,0:T(8,128)(2,1)S(1)} %constant_dynamic-update-slice_fusion.8.refs_10_.refs_15_.refs_20_), channel_id=1, source_target_pairs={{0,1},{1,2},{2,3},{3,4},{4,5},{5,6},{6,7},{7,8},{8,9},{9,10},{10,1... | collective-permute-start | bytes 798728 | tf_op jit(solution)/shard_map/ppermute | solution.py:31
  11.5 3.8 %collective-permute-start = (bf16[1024,128]{1,0:T(8,128)(2,1)S(1)}, bf16[1024,128]{1,0:T(8,128)(2,1)S(1)}, u32[]{:S(2)}, u32[]{:S(2)}) collective-permute-start(bf16[1024,128]{1,0:T(8,128)(2,1)S(1)} %get-tuple-element.57.refs_10_.refs_15_), channel_id=1, source_target_pairs={{0,1},{1,2},{2,3},{3,4},{4,5},{5,6},{6,7},{7,8},{8,9},{9,10},{10,1... | collective-permute-start | bytes 786440 | tf_op jit(solution)/shard_map/ppermute | solution.py:31
  16.1 7.3 %collective-permute-done.4.refs_9_.refs_14_.refs_19_ = bf16[1040,128]{1,0:T(8,128)(2,1)S(1)} collective-permute-done((bf16[1040,128]{1,0:T(8,128)(2,1)S(1)}, bf16[1040,128]{1,0:T(8,128)(2,1)S(1)}, u32[]{:S(2)}, u32[]{:S(2)}) %collective-permute-start.4) | collective-permute-done | bytes 266272 | tf_op jit(solution)/shard_map/ppermute | solution.py:31
  25.5 3.5 %collective-permute-done.refs_9_.refs_14_ = bf16[1024,128]{1,0:T(8,128)(2,1)S(1)} collective-permute-done((bf16[1024,128]{1,0:T(8,128)(2,1)S(1)}, bf16[1024,128]{1,0:T(8,128)(2,1)S(1)}, u32[]{:S(2)}, u32[]{:S(2)}) %collective-permute-start) | collective-permute-done | bytes 262176 | tf_op jit(solution)/shard_map/ppermute | solution.py:31
  31.4 2.8 %copy.20 = f32[2,4096]{0,1:T(8,128)} copy(f32[2,4096]{1,0:T(2,128)} %param.13) | data formatting | bytes 65536 | tf_op args[5]
  34.2 3.4 %collective-permute-done.5.refs_8_.refs_13_.refs_18_ = bf16[1040,128]{1,0:T(8,128)(2,1)S(1)} collective-permute-done((bf16[1040,128]{1,0:T(8,128)(2,1)S(1)}, bf16[1040,128]{1,0:T(8,128)(2,1)S(1)}, u32[]{:S(2)}, u32[]{:S(2)}) %collective-permute-start.5) | collective-permute-done | bytes 266272 | tf_op jit(solution)/shard_map/ppermute | solution.py:31
  39.5 4.4 %collective-permute-done.1.refs_8_.refs_13_ = bf16[1024,128]{1,0:T(8,128)(2,1)S(1)} collective-permute-done((bf16[1024,128]{1,0:T(8,128)(2,1)S(1)}, bf16[1024,128]{1,0:T(8,128)(2,1)S(1)}, u32[]{:S(2)}, u32[]{:S(2)}) %collective-permute-start.1) | collective-permute-done | bytes 262176 | tf_op jit(solution)/shard_map/ppermute | solution.py:31
  45.9 6.5 %collective-permute-done.6.refs_7_.refs_12_.refs_17_ = bf16[1040,128]{1,0:T(8,128)(2,1)S(1)} collective-permute-done((bf16[1040,128]{1,0:T(8,128)(2,1)S(1)}, bf16[1040,128]{1,0:T(8,128)(2,1)S(1)}, u32[]{:S(2)}, u32[]{:S(2)}) %collective-permute-start.6) | collective-permute-done | bytes 266272 | tf_op jit(solution)/shard_map/ppermute | solution.py:31
  54.3 3.9 %collective-permute-done.2.refs_7_.refs_12_ = bf16[1024,128]{1,0:T(8,128)(2,1)} collective-permute-done((bf16[1024,128]{1,0:T(8,128)(2,1)S(1)}, bf16[1024,128]{1,0:T(8,128)(2,1)}, u32[]{:S(2)}, u32[]{:S(2)}) %collective-permute-start.2) | collective-permute-done | bytes 262176 | tf_op jit(solution)/shard_map/ppermute | solution.py:31
  60.1 6.3 %collective-permute-done.7.refs_6_.refs_11_.refs_16_ = bf16[1040,128]{1,0:T(8,128)(2,1)S(1)} collective-permute-done((bf16[1040,128]{1,0:T(8,128)(2,1)S(1)}, bf16[1040,128]{1,0:T(8,128)(2,1)S(1)}, u32[]{:S(2)}, u32[]{:S(2)}) %collective-permute-start.7) | collective-permute-done | bytes 266272 | tf_op jit(solution)/shard_map/ppermute | solution.py:31
  67.1 10.1 %attend.2 = (bf16[128,4096]{1,0:T(8,128)(2,1)}, bf16[128,4096]{1,0:T(8,128)(2,1)}, bf16[128,1024]{1,0:T(8,128)(2,1)}, f32[128,1024]{1,0:T(8,128)}, f32[128,1024]...) custom-call(s32[1,128]{1,0:T(1,128)} %add_bitcast_fusion.refs_0_, s32[1,128]{1,0:T(1,128)} %bitcast.19, ...), custom_call_target="tpu_custom_call" | custom-call | flops 2013265920 | bytes 6029312 | tf_op jit(solution)/shard_map/attend/pallas_call | solution.py:195
  79.2 10.3 %attend.3 = (bf16[128,4096]{1,0:T(8,128)(2,1)}, bf16[128,4096]{1,0:T(8,128)(2,1)}, bf16[128,1024]{1,0:T(8,128)(2,1)}, f32[128,1024]{1,0:T(8,128)}, f32[128,1024]...) custom-call(s32[1,128]{1,0:T(1,128)} %add_bitcast_fusion.refs_0_, ...), custom_call_target="tpu_custom_call", output_to_operand_aliasing={{0}: (21, {}), {1}: (22, {}), {7}: (23, {})} | custom-call | flops 2013265920 | bytes 6029312 | tf_op jit(solution)/shard_map/attend/pallas_call | solution.py:195
  89.5 4.5 %collective-permute-done.13 = f32[128,128]{1,0:T(8,128)S(1)} collective-permute-done((f32[128,128]{1,0:T(8,128)}, f32[128,128]{1,0:T(8,128)S(1)}, u32[]{:S(2)}, u32[]{:S(2)}) %collective-permute-start.13) | collective-permute-done | bytes 65568 | tf_op jit(solution)/shard_map/ppermute | solution.py:320
  96.8 3.8 %collective-permute-done.14 = f32[128,128]{1,0:T(8,128)S(1)} collective-permute-done((f32[128,128]{1,0:T(8,128)S(1)}, f32[128,128]{1,0:T(8,128)S(1)}, u32[]{:S(2)}, u32[]{:S(2)}) %collective-permute-start.14) | collective-permute-done | bytes 65568 | tf_op jit(solution)/shard_map/ppermute | solution.py:320
  100.8 2.1 %collective-permute-start.9 = (bf16[128,1024]{1,0:T(8,128)(2,1)S(1)}, bf16[128,1024]{1,0:T(8,128)(2,1)S(1)}, u32[]{:S(2)}, u32[]{:S(2)}) collective-permute-start(bf16[128,1024]{1,0:T(8,128)(2,1)S(1)} %add_convert_fusion.5), channel_id=1, source_target_pairs={{1,0},{2,1},{3,2},{4,3},{5,4},{6,5},{7,6},{8,7},{9,8},{10,9},{11,1... | collective-permute-start | bytes 786440 | tf_op jit(solution)/shard_map/ppermute | solution.py:31
  104.6 8.3 %collective-permute-start.15 = (bf16[128,1024]{1,0:T(8,128)(2,1)S(1)}, bf16[128,1024]{1,0:T(8,128)(2,1)S(1)}, u32[]{:S(2)}, u32[]{:S(2)}) collective-permute-start(bf16[128,1024]{1,0:T(8,128)(2,1)S(1)} %add_convert_fusion.2), channel_id=1, source_target_pairs={{1,0},{2,1},{3,2},{4,3},{5,4},{6,5},{7,6},{8,7},{9,8},{10,9},{11,1... | collective-permute-start | bytes 786440 | tf_op jit(solution)/shard_map/ppermute | solution.py:31
  113.0 4.0 %collective-permute-start.19 = (f32[128,128]{1,0:T(8,128)S(1)}, f32[128,128]{1,0:T(8,128)S(1)}, u32[]{:S(2)}, u32[]{:S(2)}) collective-permute-start(f32[128,128]{1,0:T(8,128)S(1)} %add.85), channel_id=1, source_target_pairs={{0,128},{1,129},{2,130},{3,131},{4,132},{5,133},{6,134},{7,135},{8... | collective-permute-start | bytes 196616 | tf_op jit(solution)/shard_map/ppermute | solution.py:320
  117.1 6.5 %collective-permute-start.10 = (bf16[128,1024]{1,0:T(8,128)(2,1)S(1)}, bf16[128,1024]{1,0:T(8,128)(2,1)S(1)}, u32[]{:S(2)}, u32[]{:S(2)}) collective-permute-start(bf16[128,1024]{1,0:T(8,128)(2,1)S(1)} %add_convert_fusion.4), channel_id=1, source_target_pairs={{1,0},{2,1},{3,2},{4,3},{5,4},{6,5},{7,6},{8,7},{9,8},{10,9},{11,1... | collective-permute-start | bytes 786440 | tf_op jit(solution)/shard_map/ppermute | solution.py:31
  125.7 2.9 %collective-permute-done.20 = f32[128,128]{1,0:T(8,128)S(1)} collective-permute-done((f32[128,128]{1,0:T(8,128)S(1)}, f32[128,128]{1,0:T(8,128)S(1)}, u32[]{:S(2)}, u32[]{:S(2)}) %collective-permute-start.20) | collective-permute-done | bytes 65568 | tf_op jit(solution)/shard_map/ppermute | solution.py:320
  130.6 6.2 %collective-permute-done.22 = f32[128,128]{1,0:T(8,128)S(1)} collective-permute-done((f32[128,128]{1,0:T(8,128)S(1)}, f32[128,128]{1,0:T(8,128)S(1)}, u32[]{:S(2)}, u32[]{:S(2)}) %collective-permute-start.22) | collective-permute-done | bytes 65568 | tf_op jit(solution)/shard_map/ppermute | solution.py:320
  137.0 5.9 %collective-permute-start.21 = (bf16[128,1024]{1,0:T(8,128)(2,1)S(1)}, bf16[128,1024]{1,0:T(8,128)(2,1)S(1)}, u32[]{:S(2)}, u32[]{:S(2)}) collective-permute-start(bf16[128,1024]{1,0:T(8,128)(2,1)S(1)} %add_convert_fusion), channel_id=1, source_target_pairs={{1,0},{2,1},{3,2},{4,3},{5,4},{6,5},{7,6},{8,7},{9,8},{10,9},{11,1... | collective-permute-start | bytes 786440 | tf_op jit(solution)/shard_map/ppermute | solution.py:31
  146.3 3.1 %collective-permute-done.21.refs_2_ = bf16[128,1024]{1,0:T(8,128)(2,1)S(1)} collective-permute-done((bf16[128,1024]{1,0:T(8,128)(2,1)S(1)}, bf16[128,1024]{1,0:T(8,128)(2,1)S(1)}, u32[]{:S(2)}, u32[]{:S(2)}) %collective-permute-start.21) | collective-permute-done | bytes 262176 | tf_op jit(solution)/shard_map/ppermute | solution.py:31
  149.4 3.1 %collective-permute-done.11.refs_0_ = bf16[128,1024]{1,0:T(8,128)(2,1)S(1)} collective-permute-done((bf16[128,1024]{1,0:T(8,128)(2,1)S(1)}, bf16[128,1024]{1,0:T(8,128)(2,1)S(1)}, u32[]{:S(2)}, u32[]{:S(2)}) %collective-permute-start.11) | collective-permute-done | bytes 262176 | tf_op jit(solution)/shard_map/ppermute | solution.py:31
  153.2 2.7 %finish.1 = (bf16[128,1024]{1,0:T(8,128)(2,1)}, bf16[128,1024]{1,0:T(8,128)(2,1)}) custom-call(bf16[128,1024]{1,0:T(8,128)(2,1)} %copy-done.14, f32[128,1024]{1,0:T(8,128)} %get-tuple-element.41.refs_1_, bf16[128,1024]{1,0:T(8,128)(2,1)} %copy-done.13, f32[128,1024]{1,0:T(8,128)} %get-tuple-element.53.refs_3_, bf16[128,1024]{1,0:T(8,128)(2,1)} %refs_4_.1, ...), custom_call_target="tpu_custom_call" | custom-call | tf_op jit(solution)/shard_map/finish/pallas_call | solution.py:240
  (89 shorter events, 35.6 us)
Async XLA Ops:
  7.6 15.7 %collective-permute-start.4 = (bf16[1040,128]{1,0:T(8,128)(2,1)S(1)}, bf16[1040,128]{1,0:T(8,128)(2,1)S(1)}, u32[]{:S(2)}, u32[]{:S(2)}) collective-permute-start(bf16[1040,128]{1,0:T(8,128)(2,1)S(1)} %constant_dynamic-update-slice_fusion.8.refs_10_.refs_15_.refs_20_), channel_id=1, source_target_pairs={{0,1},{1,2},{2,3},{3,4},{4,5},{5,6},{6,7},{7,8},{8,9},{9,10},{10,1... | collective-permute-start | bytes 798728 | tf_op jit(solution)/shard_map/ppermute | solution.py:31
  11.5 17.5 %collective-permute-start = (bf16[1024,128]{1,0:T(8,128)(2,1)S(1)}, bf16[1024,128]{1,0:T(8,128)(2,1)S(1)}, u32[]{:S(2)}, u32[]{:S(2)}) collective-permute-start(bf16[1024,128]{1,0:T(8,128)(2,1)S(1)} %get-tuple-element.57.refs_10_.refs_15_), channel_id=1, source_target_pairs={{0,1},{1,2},{2,3},{3,4},{4,5},{5,6},{6,7},{7,8},{8,9},{9,10},{10,1... | collective-permute-start | bytes 786440 | tf_op jit(solution)/shard_map/ppermute | solution.py:31
  23.4 14.2 %collective-permute-start.5 = (bf16[1040,128]{1,0:T(8,128)(2,1)S(1)}, bf16[1040,128]{1,0:T(8,128)(2,1)S(1)}, u32[]{:S(2)}, u32[]{:S(2)}) collective-permute-start(bf16[1040,128]{1,0:T(8,128)(2,1)S(1)} %collective-permute-done.4.refs_9_.refs_14_.refs_19_), channel_id=1, source_target_pairs={{0,1},{1,2},{2,3},{3,4},{4,5},{5,6},{6,7},{7,8},{8,9},{9,10},{10,1... | collective-permute-start | bytes 798728 | tf_op jit(solution)/shard_map/ppermute | solution.py:31
  29.0 14.9 %collective-permute-start.1 = (bf16[1024,128]{1,0:T(8,128)(2,1)S(1)}, bf16[1024,128]{1,0:T(8,128)(2,1)S(1)}, u32[]{:S(2)}, u32[]{:S(2)}) collective-permute-start(bf16[1024,128]{1,0:T(8,128)(2,1)S(1)} %collective-permute-done.refs_9_.refs_14_), channel_id=1, source_target_pairs={{0,1},{1,2},{2,3},{3,4},{4,5},{5,6},{6,7},{7,8},{8,9},{9,10},{10,1... | collective-permute-start | bytes 786440 | tf_op jit(solution)/shard_map/ppermute | solution.py:31
  37.6 14.7 %collective-permute-start.6 = (bf16[1040,128]{1,0:T(8,128)(2,1)S(1)}, bf16[1040,128]{1,0:T(8,128)(2,1)S(1)}, u32[]{:S(2)}, u32[]{:S(2)}) collective-permute-start(bf16[1040,128]{1,0:T(8,128)(2,1)S(1)} %collective-permute-done.5.refs_8_.refs_13_.refs_18_), channel_id=1, source_target_pairs={{0,1},{1,2},{2,3},{3,4},{4,5},{5,6},{6,7},{7,8},{8,9},{9,10},{10,1... | collective-permute-start | bytes 798728 | tf_op jit(solution)/shard_map/ppermute | solution.py:31
  44.0 14.2 %collective-permute-start.2 = (bf16[1024,128]{1,0:T(8,128)(2,1)S(1)}, bf16[1024,128]{1,0:T(8,128)(2,1)}, u32[]{:S(2)}, u32[]{:S(2)}) collective-permute-start(bf16[1024,128]{1,0:T(8,128)(2,1)S(1)} %collective-permute-done.1.refs_8_.refs_13_), channel_id=1, source_target_pairs={{0,1},{1,2},{2,3},{3,4},{4,5},{5,6},{6,7},{7,8},{8,9},{9,10},{10,1... | collective-permute-start | bytes 786440 | tf_op jit(solution)/shard_map/ppermute | solution.py:31
  52.4 14.0 %collective-permute-start.7 = (bf16[1040,128]{1,0:T(8,128)(2,1)S(1)}, bf16[1040,128]{1,0:T(8,128)(2,1)S(1)}, u32[]{:S(2)}, u32[]{:S(2)}) collective-permute-start(bf16[1040,128]{1,0:T(8,128)(2,1)S(1)} %collective-permute-done.6.refs_7_.refs_12_.refs_17_), channel_id=1, source_target_pairs={{0,1},{1,2},{2,3},{3,4},{4,5},{5,6},{6,7},{7,8},{8,9},{9,10},{10,1... | collective-permute-start | bytes 798728 | tf_op jit(solution)/shard_map/ppermute | solution.py:31
  58.2 21.0 %collective-permute-start.3 = (bf16[1024,128]{1,0:T(8,128)(2,1)}, bf16[1024,128]{1,0:T(8,128)(2,1)}, u32[]{:S(2)}, u32[]{:S(2)}) collective-permute-start(bf16[1024,128]{1,0:T(8,128)(2,1)} %collective-permute-done.2.refs_7_.refs_12_), channel_id=1, source_target_pairs={{0,1},{1,2},{2,3},{3,4},{4,5},{5,6},{6,7},{7,8},{8,9},{9,10},{10,1... | collective-permute-start | bytes 786440 | tf_op jit(solution)/shard_map/ppermute | solution.py:31
  77.2 23.4 %collective-permute-start.8 = (bf16[128,1024]{1,0:T(8,128)(2,1)}, bf16[128,1024]{1,0:T(8,128)(2,1)S(1)}, u32[]{:S(2)}, u32[]{:S(2)}) collective-permute-start(bf16[128,1024]{1,0:T(8,128)(2,1)} %get-tuple-element.37), channel_id=1, source_target_pairs={{1,0},{2,1},{3,2},{4,3},{5,4},{6,5},{7,6},{8,7},{9,8},{10,9},{11,1... | collective-permute-start | bytes 786440 | tf_op jit(solution)/shard_map/ppermute | solution.py:31
  89.4 4.6 %collective-permute-start.13 = (f32[128,128]{1,0:T(8,128)}, f32[128,128]{1,0:T(8,128)S(1)}, u32[]{:S(2)}, u32[]{:S(2)}) collective-permute-start(f32[128,128]{1,0:T(8,128)} %get-tuple-element.44), channel_id=1, source_target_pairs={{0,8},{1,9},{2,10},{3,11},{4,12},{5,13},{6,14},{7,15},{8,0},{9,1},... | collective-permute-start | bytes 196616 | tf_op jit(solution)/shard_map/ppermute | solution.py:320
  94.9 5.8 %collective-permute-start.14 = (f32[128,128]{1,0:T(8,128)S(1)}, f32[128,128]{1,0:T(8,128)S(1)}, u32[]{:S(2)}, u32[]{:S(2)}) collective-permute-start(f32[128,128]{1,0:T(8,128)S(1)} %add.81), channel_id=1, source_target_pairs={{0,16},{1,17},{2,18},{3,19},{4,20},{5,21},{6,22},{7,23},{8,24},{9,... | collective-permute-start | bytes 196616 | tf_op jit(solution)/shard_map/ppermute | solution.py:320
  94.9 8.6 %collective-permute-start.12 = (bf16[128,1024]{1,0:T(8,128)(2,1)}, bf16[128,1024]{1,0:T(8,128)(2,1)S(1)}, u32[]{:S(2)}, u32[]{:S(2)}) collective-permute-start(bf16[128,1024]{1,0:T(8,128)(2,1)} %get-tuple-element.42), channel_id=1, source_target_pairs={{1,0},{2,1},{3,2},{4,3},{5,4},{6,5},{7,6},{8,7},{9,8},{10,9},{11,1... | collective-permute-start | bytes 786440 | tf_op jit(solution)/shard_map/ppermute | solution.py:31
  100.7 2.2 %collective-permute-start.16 = (f32[128,128]{1,0:T(8,128)S(1)}, f32[128,128]{1,0:T(8,128)S(1)}, u32[]{:S(2)}, u32[]{:S(2)}) collective-permute-start(f32[128,128]{1,0:T(8,128)S(1)} %add.82), channel_id=1, source_target_pairs={{0,32},{1,33},{2,34},{3,35},{4,36},{5,37},{6,38},{7,39},{8,40},{9,... | collective-permute-start | bytes 196616 | tf_op jit(solution)/shard_map/ppermute | solution.py:320
  100.8 12.1 %collective-permute-start.9 = (bf16[128,1024]{1,0:T(8,128)(2,1)S(1)}, bf16[128,1024]{1,0:T(8,128)(2,1)S(1)}, u32[]{:S(2)}, u32[]{:S(2)}) collective-permute-start(bf16[128,1024]{1,0:T(8,128)(2,1)S(1)} %add_convert_fusion.5), channel_id=1, source_target_pairs={{1,0},{2,1},{3,2},{4,3},{5,4},{6,5},{7,6},{8,7},{9,8},{10,9},{11,1... | collective-permute-start | bytes 786440 | tf_op jit(solution)/shard_map/ppermute | solution.py:31
  102.9 10.0 %collective-permute-start.17 = (f32[128,128]{1,0:T(8,128)S(1)}, f32[128,128]{1,0:T(8,128)S(1)}, u32[]{:S(2)}, u32[]{:S(2)}) collective-permute-start(f32[128,128]{1,0:T(8,128)S(1)} %add.84), channel_id=1, source_target_pairs={{0,64},{1,65},{2,66},{3,67},{4,68},{5,69},{6,70},{7,71},{8,72},{9,... | collective-permute-start | bytes 196616 | tf_op jit(solution)/shard_map/ppermute | solution.py:320
  104.6 19.1 %collective-permute-start.15 = (bf16[128,1024]{1,0:T(8,128)(2,1)S(1)}, bf16[128,1024]{1,0:T(8,128)(2,1)S(1)}, u32[]{:S(2)}, u32[]{:S(2)}) collective-permute-start(bf16[128,1024]{1,0:T(8,128)(2,1)S(1)} %add_convert_fusion.2), channel_id=1, source_target_pairs={{1,0},{2,1},{3,2},{4,3},{5,4},{6,5},{7,6},{8,7},{9,8},{10,9},{11,1... | collective-permute-start | bytes 786440 | tf_op jit(solution)/shard_map/ppermute | solution.py:31
  113.0 10.6 %collective-permute-start.19 = (f32[128,128]{1,0:T(8,128)S(1)}, f32[128,128]{1,0:T(8,128)S(1)}, u32[]{:S(2)}, u32[]{:S(2)}) collective-permute-start(f32[128,128]{1,0:T(8,128)S(1)} %add.85), channel_id=1, source_target_pairs={{0,128},{1,129},{2,130},{3,131},{4,132},{5,133},{6,134},{7,135},{8... | collective-permute-start | bytes 196616 | tf_op jit(solution)/shard_map/ppermute | solution.py:320
  117.1 13.3 %collective-permute-start.10 = (bf16[128,1024]{1,0:T(8,128)(2,1)S(1)}, bf16[128,1024]{1,0:T(8,128)(2,1)S(1)}, u32[]{:S(2)}, u32[]{:S(2)}) collective-permute-start(bf16[128,1024]{1,0:T(8,128)(2,1)S(1)} %add_convert_fusion.4), channel_id=1, source_target_pairs={{1,0},{2,1},{3,2},{4,3},{5,4},{6,5},{7,6},{8,7},{9,8},{10,9},{11,1... | collective-permute-start | bytes 786440 | tf_op jit(solution)/shard_map/ppermute | solution.py:31
  123.6 5.0 %collective-permute-start.20 = (f32[128,128]{1,0:T(8,128)S(1)}, f32[128,128]{1,0:T(8,128)S(1)}, u32[]{:S(2)}, u32[]{:S(2)}) collective-permute-start(f32[128,128]{1,0:T(8,128)S(1)} %add.87), channel_id=1, source_target_pairs={{0,1},{1,0},{2,3},{3,2},{4,5},{5,4},{6,7},{7,6},{8,9},{9,8},{10,11... | collective-permute-start | bytes 196616 | tf_op jit(solution)/shard_map/ppermute | solution.py:320
  123.8 13.1 %collective-permute-start.18 = (bf16[128,1024]{1,0:T(8,128)(2,1)S(1)}, bf16[128,1024]{1,0:T(8,128)(2,1)S(1)}, u32[]{:S(2)}, u32[]{:S(2)}) collective-permute-start(bf16[128,1024]{1,0:T(8,128)(2,1)S(1)} %add_convert_fusion.1), channel_id=1, source_target_pairs={{1,0},{2,1},{3,2},{4,3},{5,4},{6,5},{7,6},{8,7},{9,8},{10,9},{11,1... | collective-permute-start | bytes 786440 | tf_op jit(solution)/shard_map/ppermute | solution.py:31
  130.5 6.3 %collective-permute-start.22 = (f32[128,128]{1,0:T(8,128)S(1)}, f32[128,128]{1,0:T(8,128)S(1)}, u32[]{:S(2)}, u32[]{:S(2)}) collective-permute-start(f32[128,128]{1,0:T(8,128)S(1)} %add.88), channel_id=1, source_target_pairs={{0,2},{1,3},{2,0},{3,1},{4,6},{5,7},{6,4},{7,5},{8,10},{9,11},{10,... | collective-permute-start | bytes 196616 | tf_op jit(solution)/shard_map/ppermute | solution.py:320
  136.8 8.3 %collective-permute-start.23 = (f32[128,128]{1,0:T(8,128)S(1)}, f32[128,128]{1,0:T(8,128)S(1)}, u32[]{:S(2)}, u32[]{:S(2)}) collective-permute-start(f32[128,128]{1,0:T(8,128)S(1)} %add.89), channel_id=1, source_target_pairs={{0,4},{1,5},{2,6},{3,7},{4,0},{5,1},{6,2},{7,3},{8,12},{9,13},{10,... | collective-permute-start | bytes 196616 | tf_op jit(solution)/shard_map/ppermute | solution.py:320
  137.0 12.4 %collective-permute-start.21 = (bf16[128,1024]{1,0:T(8,128)(2,1)S(1)}, bf16[128,1024]{1,0:T(8,128)(2,1)S(1)}, u32[]{:S(2)}, u32[]{:S(2)}) collective-permute-start(bf16[128,1024]{1,0:T(8,128)(2,1)S(1)} %add_convert_fusion), channel_id=1, source_target_pairs={{1,0},{2,1},{3,2},{4,3},{5,4},{6,5},{7,6},{8,7},{9,8},{10,9},{11,1... | collective-permute-start | bytes 786440 | tf_op jit(solution)/shard_map/ppermute | solution.py:31
  142.9 9.6 %collective-permute-start.11 = (bf16[128,1024]{1,0:T(8,128)(2,1)S(1)}, bf16[128,1024]{1,0:T(8,128)(2,1)S(1)}, u32[]{:S(2)}, u32[]{:S(2)}) collective-permute-start(bf16[128,1024]{1,0:T(8,128)(2,1)S(1)} %add_convert_fusion.3), channel_id=1, source_target_pairs={{1,0},{2,1},{3,2},{4,3},{5,4},{6,5},{7,6},{8,7},{9,8},{10,9},{11,1... | collective-permute-start | bytes 786440 | tf_op jit(solution)/shard_map/ppermute | solution.py:31
  (15 other events, 431.1 us)

commit v6 on v5

--- a/solution.py
+++ b/solution.py
@@ -306,7 +306,7 @@
     attended, query_grad = outs[:2]
     gains = outs[-1]
     bits = [1 << n for n in range(devices.bit_length() - 1)]
-    bits = bits[NEAR:] + bits[:NEAR]
+    bits = bits[NEAR:] + bits[:NEAR][::-1]
     moved = [shifted(part[0], -1) for part in backs]
     if PRE:
         gains = after(gains, moved[0])

time: 158 us -> 159 us (level)
  starting transfers between devices: 54.1 us -> 56.3 us
    ppermute x16, waiting for transfers between devices: 43.7 us -> 41.1 us  [shifted(): lax.ppermute(value, AXES, [(source, source + steps) for source in range(f...]
    ppermute x8, waiting for transfers between devices: 17.7 us -> 20 us  [on_device(): lax.ppermute(gains, AXES, [(i, i ^ bit) for i in range(devices)])]
    ppermute x16, starting transfers between devices: 49.5 us -> 51.7 us  [shifted(): lax.ppermute(value, AXES, [(source, source + steps) for source in range(f...]
  transfers between devices with their start and end apart: 24 -> 24, of which waited for: 16 -> 15; matrix products, arithmetic and copies ran while one was open for 5% -> 5% of each run, Pallas kernels for 13% -> 13%
where the time goes in v6:
time: 159 us; the launch traced here: 158 us
  waiting for transfers between devices  61 us (38%)
  starting transfers between devices  56.3 us (35%)
  Pallas kernels  23.1 us (15%)
  local copies, waits for them, and re-layouts  11.8 us (7%)
  other arithmetic  4.4 us (3%)
    ppermute x16, starting transfers between devices, shifted(): lax.ppermute(value, AXES, [(source, source + steps) for source in range(f...  51.7 us
    ppermute x16, waiting for transfers between devices, shifted(): lax.ppermute(value, AXES, [(source, source + steps) for source in range(f...  41.1 us
    pallas_call x2, Pallas kernels, attend(): pl.pallas_call(functools.partial(attend_kernel, blocks - 1, repeat, len(a...  20.4 us
    ppermute x8, waiting for transfers between devices, on_device(): lax.ppermute(gains, AXES, [(i, i ^ bit) for i in range(devices)])  20 us
    unnamed x39, local copies, waits for them, and re-layouts  9.82 us
    ppermute x8, starting transfers between devices, on_device(): lax.ppermute(gains, AXES, [(i, i ^ bit) for i in range(devices)])  4.6 us
  transfers between devices with their start and end apart: 24, of which 15 were waited for; matrix products, arithmetic and copies ran while one was open for 5% of the time, Pallas kernels for 13%

profile of v6, /device:TPU:2, one launch (start us, length us, event | category | flops | bytes accessed | tf_op | source)
XLA Modules:
  0.0 157.8 jit_solution(4715802467846028358)
XLA Ops:
  7.6 3.8 %collective-permute-start.4 = (bf16[1040,128]{1,0:T(8,128)(2,1)S(1)}, bf16[1040,128]{1,0:T(8,128)(2,1)S(1)}, u32[]{:S(2)}, u32[]{:S(2)}) collective-permute-start(bf16[1040,128]{1,0:T(8,128)(2,1)S(1)} %constant_dynamic-update-slice_fusion.8.refs_10_.refs_15_.refs_20_), channel_id=1, source_target_pairs={{0,1},{1,2},{2,3},{3,4},{4,5},{5,6},{6,7},{7,8},{8,9},{9,10},{10,1... | collective-permute-start | bytes 798728 | tf_op jit(solution)/shard_map/ppermute | solution.py:31
  11.5 3.8 %collective-permute-start = (bf16[1024,128]{1,0:T(8,128)(2,1)S(1)}, bf16[1024,128]{1,0:T(8,128)(2,1)S(1)}, u32[]{:S(2)}, u32[]{:S(2)}) collective-permute-start(bf16[1024,128]{1,0:T(8,128)(2,1)S(1)} %get-tuple-element.57.refs_10_.refs_15_), channel_id=1, source_target_pairs={{0,1},{1,2},{2,3},{3,4},{4,5},{5,6},{6,7},{7,8},{8,9},{9,10},{10,1... | collective-permute-start | bytes 786440 | tf_op jit(solution)/shard_map/ppermute | solution.py:31
  16.1 7.3 %collective-permute-done.4.refs_9_.refs_14_.refs_19_ = bf16[1040,128]{1,0:T(8,128)(2,1)S(1)} collective-permute-done((bf16[1040,128]{1,0:T(8,128)(2,1)S(1)}, bf16[1040,128]{1,0:T(8,128)(2,1)S(1)}, u32[]{:S(2)}, u32[]{:S(2)}) %collective-permute-start.4) | collective-permute-done | bytes 266272 | tf_op jit(solution)/shard_map/ppermute | solution.py:31
  25.5 3.5 %collective-permute-done.refs_9_.refs_14_ = bf16[1024,128]{1,0:T(8,128)(2,1)S(1)} collective-permute-done((bf16[1024,128]{1,0:T(8,128)(2,1)S(1)}, bf16[1024,128]{1,0:T(8,128)(2,1)S(1)}, u32[]{:S(2)}, u32[]{:S(2)}) %collective-permute-start) | collective-permute-done | bytes 262176 | tf_op jit(solution)/shard_map/ppermute | solution.py:31
  31.4 2.8 %copy.20 = f32[2,4096]{0,1:T(8,128)} copy(f32[2,4096]{1,0:T(2,128)} %param.13) | data formatting | bytes 65536 | tf_op args[5]
  34.2 3.4 %collective-permute-done.5.refs_8_.refs_13_.refs_18_ = bf16[1040,128]{1,0:T(8,128)(2,1)S(1)} collective-permute-done((bf16[1040,128]{1,0:T(8,128)(2,1)S(1)}, bf16[1040,128]{1,0:T(8,128)(2,1)S(1)}, u32[]{:S(2)}, u32[]{:S(2)}) %collective-permute-start.5) | collective-permute-done | bytes 266272 | tf_op jit(solution)/shard_map/ppermute | solution.py:31
  39.5 4.4 %collective-permute-done.1.refs_8_.refs_13_ = bf16[1024,128]{1,0:T(8,128)(2,1)S(1)} collective-permute-done((bf16[1024,128]{1,0:T(8,128)(2,1)S(1)}, bf16[1024,128]{1,0:T(8,128)(2,1)S(1)}, u32[]{:S(2)}, u32[]{:S(2)}) %collective-permute-start.1) | collective-permute-done | bytes 262176 | tf_op jit(solution)/shard_map/ppermute | solution.py:31
  45.9 6.5 %collective-permute-done.6.refs_7_.refs_12_.refs_17_ = bf16[1040,128]{1,0:T(8,128)(2,1)S(1)} collective-permute-done((bf16[1040,128]{1,0:T(8,128)(2,1)S(1)}, bf16[1040,128]{1,0:T(8,128)(2,1)S(1)}, u32[]{:S(2)}, u32[]{:S(2)}) %collective-permute-start.6) | collective-permute-done | bytes 266272 | tf_op jit(solution)/shard_map/ppermute | solution.py:31
  54.3 3.9 %collective-permute-done.2.refs_7_.refs_12_ = bf16[1024,128]{1,0:T(8,128)(2,1)} collective-permute-done((bf16[1024,128]{1,0:T(8,128)(2,1)S(1)}, bf16[1024,128]{1,0:T(8,128)(2,1)}, u32[]{:S(2)}, u32[]{:S(2)}) %collective-permute-start.2) | collective-permute-done | bytes 262176 | tf_op jit(solution)/shard_map/ppermute | solution.py:31
  60.1 6.3 %collective-permute-done.7.refs_6_.refs_11_.refs_16_ = bf16[1040,128]{1,0:T(8,128)(2,1)S(1)} collective-permute-done((bf16[1040,128]{1,0:T(8,128)(2,1)S(1)}, bf16[1040,128]{1,0:T(8,128)(2,1)S(1)}, u32[]{:S(2)}, u32[]{:S(2)}) %collective-permute-start.7) | collective-permute-done | bytes 266272 | tf_op jit(solution)/shard_map/ppermute | solution.py:31
  67.1 10.1 %attend.2 = (bf16[128,4096]{1,0:T(8,128)(2,1)}, bf16[128,4096]{1,0:T(8,128)(2,1)}, bf16[128,1024]{1,0:T(8,128)(2,1)}, f32[128,1024]{1,0:T(8,128)}, f32[128,1024]...) custom-call(s32[1,128]{1,0:T(1,128)} %add_bitcast_fusion.refs_0_, s32[1,128]{1,0:T(1,128)} %bitcast.19, ...), custom_call_target="tpu_custom_call" | custom-call | flops 2013265920 | bytes 6029312 | tf_op jit(solution)/shard_map/attend/pallas_call | solution.py:195
  79.2 10.3 %attend.3 = (bf16[128,4096]{1,0:T(8,128)(2,1)}, bf16[128,4096]{1,0:T(8,128)(2,1)}, bf16[128,1024]{1,0:T(8,128)(2,1)}, f32[128,1024]{1,0:T(8,128)}, f32[128,1024]...) custom-call(s32[1,128]{1,0:T(1,128)} %add_bitcast_fusion.refs_0_, ...), custom_call_target="tpu_custom_call", output_to_operand_aliasing={{0}: (21, {}), {1}: (22, {}), {7}: (23, {})} | custom-call | flops 2013265920 | bytes 6029312 | tf_op jit(solution)/shard_map/attend/pallas_call | solution.py:195
  89.5 4.5 %collective-permute-done.13 = f32[128,128]{1,0:T(8,128)S(1)} collective-permute-done((f32[128,128]{1,0:T(8,128)}, f32[128,128]{1,0:T(8,128)S(1)}, u32[]{:S(2)}, u32[]{:S(2)}) %collective-permute-start.13) | collective-permute-done | bytes 65568 | tf_op jit(solution)/shard_map/ppermute | solution.py:320
  96.8 3.8 %collective-permute-done.14 = f32[128,128]{1,0:T(8,128)S(1)} collective-permute-done((f32[128,128]{1,0:T(8,128)S(1)}, f32[128,128]{1,0:T(8,128)S(1)}, u32[]{:S(2)}, u32[]{:S(2)}) %collective-permute-start.14) | collective-permute-done | bytes 65568 | tf_op jit(solution)/shard_map/ppermute | solution.py:320
  100.8 2.1 %collective-permute-start.9 = (bf16[128,1024]{1,0:T(8,128)(2,1)S(1)}, bf16[128,1024]{1,0:T(8,128)(2,1)S(1)}, u32[]{:S(2)}, u32[]{:S(2)}) collective-permute-start(bf16[128,1024]{1,0:T(8,128)(2,1)S(1)} %add_convert_fusion.5), channel_id=1, source_target_pairs={{1,0},{2,1},{3,2},{4,3},{5,4},{6,5},{7,6},{8,7},{9,8},{10,9},{11,1... | collective-permute-start | bytes 786440 | tf_op jit(solution)/shard_map/ppermute | solution.py:31
  104.6 8.3 %collective-permute-start.15 = (bf16[128,1024]{1,0:T(8,128)(2,1)S(1)}, bf16[128,1024]{1,0:T(8,128)(2,1)S(1)}, u32[]{:S(2)}, u32[]{:S(2)}) collective-permute-start(bf16[128,1024]{1,0:T(8,128)(2,1)S(1)} %add_convert_fusion.2), channel_id=1, source_target_pairs={{1,0},{2,1},{3,2},{4,3},{5,4},{6,5},{7,6},{8,7},{9,8},{10,9},{11,1... | collective-permute-start | bytes 786440 | tf_op jit(solution)/shard_map/ppermute | solution.py:31
  113.0 4.0 %collective-permute-start.19 = (f32[128,128]{1,0:T(8,128)S(1)}, f32[128,128]{1,0:T(8,128)S(1)}, u32[]{:S(2)}, u32[]{:S(2)}) collective-permute-start(f32[128,128]{1,0:T(8,128)S(1)} %add.85), channel_id=1, source_target_pairs={{0,128},{1,129},{2,130},{3,131},{4,132},{5,133},{6,134},{7,135},{8... | collective-permute-start | bytes 196616 | tf_op jit(solution)/shard_map/ppermute | solution.py:320
  117.1 6.5 %collective-permute-start.10 = (bf16[128,1024]{1,0:T(8,128)(2,1)S(1)}, bf16[128,1024]{1,0:T(8,128)(2,1)S(1)}, u32[]{:S(2)}, u32[]{:S(2)}) collective-permute-start(bf16[128,1024]{1,0:T(8,128)(2,1)S(1)} %add_convert_fusion.4), channel_id=1, source_target_pairs={{1,0},{2,1},{3,2},{4,3},{5,4},{6,5},{7,6},{8,7},{9,8},{10,9},{11,1... | collective-permute-start | bytes 786440 | tf_op jit(solution)/shard_map/ppermute | solution.py:31
  125.7 6.3 %collective-permute-done.20 = f32[128,128]{1,0:T(8,128)S(1)} collective-permute-done((f32[128,128]{1,0:T(8,128)S(1)}, f32[128,128]{1,0:T(8,128)S(1)}, u32[]{:S(2)}, u32[]{:S(2)}) %collective-permute-start.20) | collective-permute-done | bytes 65568 | tf_op jit(solution)/shard_map/ppermute | solution.py:320
  132.3 5.4 %collective-permute-done.22 = f32[128,128]{1,0:T(8,128)S(1)} collective-permute-done((f32[128,128]{1,0:T(8,128)S(1)}, f32[128,128]{1,0:T(8,128)S(1)}, u32[]{:S(2)}, u32[]{:S(2)}) %collective-permute-start.22) | collective-permute-done | bytes 65568 | tf_op jit(solution)/shard_map/ppermute | solution.py:320
  137.9 6.7 %collective-permute-start.21 = (bf16[128,1024]{1,0:T(8,128)(2,1)S(1)}, bf16[128,1024]{1,0:T(8,128)(2,1)S(1)}, u32[]{:S(2)}, u32[]{:S(2)}) collective-permute-start(bf16[128,1024]{1,0:T(8,128)(2,1)S(1)} %add_convert_fusion), channel_id=1, source_target_pairs={{1,0},{2,1},{3,2},{4,3},{5,4},{6,5},{7,6},{8,7},{9,8},{10,9},{11,1... | collective-permute-start | bytes 786440 | tf_op jit(solution)/shard_map/ppermute | solution.py:31
  144.5 3.3 %collective-permute-start.11 = (bf16[128,1024]{1,0:T(8,128)(2,1)S(1)}, bf16[128,1024]{1,0:T(8,128)(2,1)S(1)}, u32[]{:S(2)}, u32[]{:S(2)}) collective-permute-start(bf16[128,1024]{1,0:T(8,128)(2,1)S(1)} %add_convert_fusion.3), channel_id=1, source_target_pairs={{1,0},{2,1},{3,2},{4,3},{5,4},{6,5},{7,6},{8,7},{9,8},{10,9},{11,1... | collective-permute-start | bytes 786440 | tf_op jit(solution)/shard_map/ppermute | solution.py:31
  150.6 3.7 %collective-permute-done.11.refs_0_ = bf16[128,1024]{1,0:T(8,128)(2,1)S(1)} collective-permute-done((bf16[128,1024]{1,0:T(8,128)(2,1)S(1)}, bf16[128,1024]{1,0:T(8,128)(2,1)S(1)}, u32[]{:S(2)}, u32[]{:S(2)}) %collective-permute-start.11) | collective-permute-done | bytes 262176 | tf_op jit(solution)/shard_map/ppermute | solution.py:31
  155.1 2.7 %finish.1 = (bf16[128,1024]{1,0:T(8,128)(2,1)}, bf16[128,1024]{1,0:T(8,128)(2,1)}) custom-call(bf16[128,1024]{1,0:T(8,128)(2,1)} %copy-done.14, f32[128,1024]{1,0:T(8,128)} %get-tuple-element.41.refs_1_, bf16[128,1024]{1,0:T(8,128)(2,1)} %copy-done.13, f32[128,1024]{1,0:T(8,128)} %get-tuple-element.53.refs_3_, bf16[128,1024]{1,0:T(8,128)(2,1)} %refs_4_.1, ...), custom_call_target="tpu_custom_call" | custom-call | tf_op jit(solution)/shard_map/finish/pallas_call | solution.py:240
  (89 shorter events, 33.3 us)
Async XLA Ops:
  7.6 15.7 %collective-permute-start.4 = (bf16[1040,128]{1,0:T(8,128)(2,1)S(1)}, bf16[1040,128]{1,0:T(8,128)(2,1)S(1)}, u32[]{:S(2)}, u32[]{:S(2)}) collective-permute-start(bf16[1040,128]{1,0:T(8,128)(2,1)S(1)} %constant_dynamic-update-slice_fusion.8.refs_10_.refs_15_.refs_20_), channel_id=1, source_target_pairs={{0,1},{1,2},{2,3},{3,4},{4,5},{5,6},{6,7},{7,8},{8,9},{9,10},{10,1... | collective-permute-start | bytes 798728 | tf_op jit(solution)/shard_map/ppermute | solution.py:31
  11.5 17.5 %collective-permute-start = (bf16[1024,128]{1,0:T(8,128)(2,1)S(1)}, bf16[1024,128]{1,0:T(8,128)(2,1)S(1)}, u32[]{:S(2)}, u32[]{:S(2)}) collective-permute-start(bf16[1024,128]{1,0:T(8,128)(2,1)S(1)} %get-tuple-element.57.refs_10_.refs_15_), channel_id=1, source_target_pairs={{0,1},{1,2},{2,3},{3,4},{4,5},{5,6},{6,7},{7,8},{8,9},{9,10},{10,1... | collective-permute-start | bytes 786440 | tf_op jit(solution)/shard_map/ppermute | solution.py:31
  23.4 14.2 %collective-permute-start.5 = (bf16[1040,128]{1,0:T(8,128)(2,1)S(1)}, bf16[1040,128]{1,0:T(8,128)(2,1)S(1)}, u32[]{:S(2)}, u32[]{:S(2)}) collective-permute-start(bf16[1040,128]{1,0:T(8,128)(2,1)S(1)} %collective-permute-done.4.refs_9_.refs_14_.refs_19_), channel_id=1, source_target_pairs={{0,1},{1,2},{2,3},{3,4},{4,5},{5,6},{6,7},{7,8},{8,9},{9,10},{10,1... | collective-permute-start | bytes 798728 | tf_op jit(solution)/shard_map/ppermute | solution.py:31
  29.0 14.9 %collective-permute-start.1 = (bf16[1024,128]{1,0:T(8,128)(2,1)S(1)}, bf16[1024,128]{1,0:T(8,128)(2,1)S(1)}, u32[]{:S(2)}, u32[]{:S(2)}) collective-permute-start(bf16[1024,128]{1,0:T(8,128)(2,1)S(1)} %collective-permute-done.refs_9_.refs_14_), channel_id=1, source_target_pairs={{0,1},{1,2},{2,3},{3,4},{4,5},{5,6},{6,7},{7,8},{8,9},{9,10},{10,1... | collective-permute-start | bytes 786440 | tf_op jit(solution)/shard_map/ppermute | solution.py:31
  37.6 14.7 %collective-permute-start.6 = (bf16[1040,128]{1,0:T(8,128)(2,1)S(1)}, bf16[1040,128]{1,0:T(8,128)(2,1)S(1)}, u32[]{:S(2)}, u32[]{:S(2)}) collective-permute-start(bf16[1040,128]{1,0:T(8,128)(2,1)S(1)} %collective-permute-done.5.refs_8_.refs_13_.refs_18_), channel_id=1, source_target_pairs={{0,1},{1,2},{2,3},{3,4},{4,5},{5,6},{6,7},{7,8},{8,9},{9,10},{10,1... | collective-permute-start | bytes 798728 | tf_op jit(solution)/shard_map/ppermute | solution.py:31
  44.0 14.2 %collective-permute-start.2 = (bf16[1024,128]{1,0:T(8,128)(2,1)S(1)}, bf16[1024,128]{1,0:T(8,128)(2,1)}, u32[]{:S(2)}, u32[]{:S(2)}) collective-permute-start(bf16[1024,128]{1,0:T(8,128)(2,1)S(1)} %collective-permute-done.1.refs_8_.refs_13_), channel_id=1, source_target_pairs={{0,1},{1,2},{2,3},{3,4},{4,5},{5,6},{6,7},{7,8},{8,9},{9,10},{10,1... | collective-permute-start | bytes 786440 | tf_op jit(solution)/shard_map/ppermute | solution.py:31
  52.4 14.0 %collective-permute-start.7 = (bf16[1040,128]{1,0:T(8,128)(2,1)S(1)}, bf16[1040,128]{1,0:T(8,128)(2,1)S(1)}, u32[]{:S(2)}, u32[]{:S(2)}) collective-permute-start(bf16[1040,128]{1,0:T(8,128)(2,1)S(1)} %collective-permute-done.6.refs_7_.refs_12_.refs_17_), channel_id=1, source_target_pairs={{0,1},{1,2},{2,3},{3,4},{4,5},{5,6},{6,7},{7,8},{8,9},{9,10},{10,1... | collective-permute-start | bytes 798728 | tf_op jit(solution)/shard_map/ppermute | solution.py:31
  58.2 21.0 %collective-permute-start.3 = (bf16[1024,128]{1,0:T(8,128)(2,1)}, bf16[1024,128]{1,0:T(8,128)(2,1)}, u32[]{:S(2)}, u32[]{:S(2)}) collective-permute-start(bf16[1024,128]{1,0:T(8,128)(2,1)} %collective-permute-done.2.refs_7_.refs_12_), channel_id=1, source_target_pairs={{0,1},{1,2},{2,3},{3,4},{4,5},{5,6},{6,7},{7,8},{8,9},{9,10},{10,1... | collective-permute-start | bytes 786440 | tf_op jit(solution)/shard_map/ppermute | solution.py:31
  77.2 23.4 %collective-permute-start.8 = (bf16[128,1024]{1,0:T(8,128)(2,1)}, bf16[128,1024]{1,0:T(8,128)(2,1)S(1)}, u32[]{:S(2)}, u32[]{:S(2)}) collective-permute-start(bf16[128,1024]{1,0:T(8,128)(2,1)} %get-tuple-element.37), channel_id=1, source_target_pairs={{1,0},{2,1},{3,2},{4,3},{5,4},{6,5},{7,6},{8,7},{9,8},{10,9},{11,1... | collective-permute-start | bytes 786440 | tf_op jit(solution)/shard_map/ppermute | solution.py:31
  89.4 4.6 %collective-permute-start.13 = (f32[128,128]{1,0:T(8,128)}, f32[128,128]{1,0:T(8,128)S(1)}, u32[]{:S(2)}, u32[]{:S(2)}) collective-permute-start(f32[128,128]{1,0:T(8,128)} %get-tuple-element.44), channel_id=1, source_target_pairs={{0,8},{1,9},{2,10},{3,11},{4,12},{5,13},{6,14},{7,15},{8,0},{9,1},... | collective-permute-start | bytes 196616 | tf_op jit(solution)/shard_map/ppermute | solution.py:320
  94.9 5.8 %collective-permute-start.14 = (f32[128,128]{1,0:T(8,128)S(1)}, f32[128,128]{1,0:T(8,128)S(1)}, u32[]{:S(2)}, u32[]{:S(2)}) collective-permute-start(f32[128,128]{1,0:T(8,128)S(1)} %add.81), channel_id=1, source_target_pairs={{0,16},{1,17},{2,18},{3,19},{4,20},{5,21},{6,22},{7,23},{8,24},{9,... | collective-permute-start | bytes 196616 | tf_op jit(solution)/shard_map/ppermute | solution.py:320
  94.9 8.6 %collective-permute-start.12 = (bf16[128,1024]{1,0:T(8,128)(2,1)}, bf16[128,1024]{1,0:T(8,128)(2,1)S(1)}, u32[]{:S(2)}, u32[]{:S(2)}) collective-permute-start(bf16[128,1024]{1,0:T(8,128)(2,1)} %get-tuple-element.42), channel_id=1, source_target_pairs={{1,0},{2,1},{3,2},{4,3},{5,4},{6,5},{7,6},{8,7},{9,8},{10,9},{11,1... | collective-permute-start | bytes 786440 | tf_op jit(solution)/shard_map/ppermute | solution.py:31
  100.7 2.2 %collective-permute-start.16 = (f32[128,128]{1,0:T(8,128)S(1)}, f32[128,128]{1,0:T(8,128)S(1)}, u32[]{:S(2)}, u32[]{:S(2)}) collective-permute-start(f32[128,128]{1,0:T(8,128)S(1)} %add.82), channel_id=1, source_target_pairs={{0,32},{1,33},{2,34},{3,35},{4,36},{5,37},{6,38},{7,39},{8,40},{9,... | collective-permute-start | bytes 196616 | tf_op jit(solution)/shard_map/ppermute | solution.py:320
  100.8 12.1 %collective-permute-start.9 = (bf16[128,1024]{1,0:T(8,128)(2,1)S(1)}, bf16[128,1024]{1,0:T(8,128)(2,1)S(1)}, u32[]{:S(2)}, u32[]{:S(2)}) collective-permute-start(bf16[128,1024]{1,0:T(8,128)(2,1)S(1)} %add_convert_fusion.5), channel_id=1, source_target_pairs={{1,0},{2,1},{3,2},{4,3},{5,4},{6,5},{7,6},{8,7},{9,8},{10,9},{11,1... | collective-permute-start | bytes 786440 | tf_op jit(solution)/shard_map/ppermute | solution.py:31
  102.9 10.0 %collective-permute-start.17 = (f32[128,128]{1,0:T(8,128)S(1)}, f32[128,128]{1,0:T(8,128)S(1)}, u32[]{:S(2)}, u32[]{:S(2)}) collective-permute-start(f32[128,128]{1,0:T(8,128)S(1)} %add.84), channel_id=1, source_target_pairs={{0,64},{1,65},{2,66},{3,67},{4,68},{5,69},{6,70},{7,71},{8,72},{9,... | collective-permute-start | bytes 196616 | tf_op jit(solution)/shard_map/ppermute | solution.py:320
  104.6 19.1 %collective-permute-start.15 = (bf16[128,1024]{1,0:T(8,128)(2,1)S(1)}, bf16[128,1024]{1,0:T(8,128)(2,1)S(1)}, u32[]{:S(2)}, u32[]{:S(2)}) collective-permute-start(bf16[128,1024]{1,0:T(8,128)(2,1)S(1)} %add_convert_fusion.2), channel_id=1, source_target_pairs={{1,0},{2,1},{3,2},{4,3},{5,4},{6,5},{7,6},{8,7},{9,8},{10,9},{11,1... | collective-permute-start | bytes 786440 | tf_op jit(solution)/shard_map/ppermute | solution.py:31
  113.0 10.6 %collective-permute-start.19 = (f32[128,128]{1,0:T(8,128)S(1)}, f32[128,128]{1,0:T(8,128)S(1)}, u32[]{:S(2)}, u32[]{:S(2)}) collective-permute-start(f32[128,128]{1,0:T(8,128)S(1)} %add.85), channel_id=1, source_target_pairs={{0,128},{1,129},{2,130},{3,131},{4,132},{5,133},{6,134},{7,135},{8... | collective-permute-start | bytes 196616 | tf_op jit(solution)/shard_map/ppermute | solution.py:320
  117.1 15.1 %collective-permute-start.10 = (bf16[128,1024]{1,0:T(8,128)(2,1)S(1)}, bf16[128,1024]{1,0:T(8,128)(2,1)S(1)}, u32[]{:S(2)}, u32[]{:S(2)}) collective-permute-start(bf16[128,1024]{1,0:T(8,128)(2,1)S(1)} %add_convert_fusion.4), channel_id=1, source_target_pairs={{1,0},{2,1},{3,2},{4,3},{5,4},{6,5},{7,6},{8,7},{9,8},{10,9},{11,1... | collective-permute-start | bytes 786440 | tf_op jit(solution)/shard_map/ppermute | solution.py:31
  123.6 8.4 %collective-permute-start.20 = (f32[128,128]{1,0:T(8,128)S(1)}, f32[128,128]{1,0:T(8,128)S(1)}, u32[]{:S(2)}, u32[]{:S(2)}) collective-permute-start(f32[128,128]{1,0:T(8,128)S(1)} %add.87), channel_id=1, source_target_pairs={{0,4},{1,5},{2,6},{3,7},{4,0},{5,1},{6,2},{7,3},{8,12},{9,13},{10,... | collective-permute-start | bytes 196616 | tf_op jit(solution)/shard_map/ppermute | solution.py:320
  123.8 14.0 %collective-permute-start.18 = (bf16[128,1024]{1,0:T(8,128)(2,1)S(1)}, bf16[128,1024]{1,0:T(8,128)(2,1)S(1)}, u32[]{:S(2)}, u32[]{:S(2)}) collective-permute-start(bf16[128,1024]{1,0:T(8,128)(2,1)S(1)} %add_convert_fusion.1), channel_id=1, source_target_pairs={{1,0},{2,1},{3,2},{4,3},{5,4},{6,5},{7,6},{8,7},{9,8},{10,9},{11,1... | collective-permute-start | bytes 786440 | tf_op jit(solution)/shard_map/ppermute | solution.py:31
  132.2 5.5 %collective-permute-start.22 = (f32[128,128]{1,0:T(8,128)S(1)}, f32[128,128]{1,0:T(8,128)S(1)}, u32[]{:S(2)}, u32[]{:S(2)}) collective-permute-start(f32[128,128]{1,0:T(8,128)S(1)} %add.88), channel_id=1, source_target_pairs={{0,2},{1,3},{2,0},{3,1},{4,6},{5,7},{6,4},{7,5},{8,10},{9,11},{10,... | collective-permute-start | bytes 196616 | tf_op jit(solution)/shard_map/ppermute | solution.py:320
  137.7 10.2 %collective-permute-start.23 = (f32[128,128]{1,0:T(8,128)S(1)}, f32[128,128]{1,0:T(8,128)S(1)}, u32[]{:S(2)}, u32[]{:S(2)}) collective-permute-start(f32[128,128]{1,0:T(8,128)S(1)} %add.89), channel_id=1, source_target_pairs={{0,1},{1,0},{2,3},{3,2},{4,5},{5,4},{6,7},{7,6},{8,9},{9,8},{10,11... | collective-permute-start | bytes 196616 | tf_op jit(solution)/shard_map/ppermute | solution.py:320
  137.9 12.7 %collective-permute-start.21 = (bf16[128,1024]{1,0:T(8,128)(2,1)S(1)}, bf16[128,1024]{1,0:T(8,128)(2,1)S(1)}, u32[]{:S(2)}, u32[]{:S(2)}) collective-permute-start(bf16[128,1024]{1,0:T(8,128)(2,1)S(1)} %add_convert_fusion), channel_id=1, source_target_pairs={{1,0},{2,1},{3,2},{4,3},{5,4},{6,5},{7,6},{8,7},{9,8},{10,9},{11,1... | collective-permute-start | bytes 786440 | tf_op jit(solution)/shard_map/ppermute | solution.py:31
  144.5 9.8 %collective-permute-start.11 = (bf16[128,1024]{1,0:T(8,128)(2,1)S(1)}, bf16[128,1024]{1,0:T(8,128)(2,1)S(1)}, u32[]{:S(2)}, u32[]{:S(2)}) collective-permute-start(bf16[128,1024]{1,0:T(8,128)(2,1)S(1)} %add_convert_fusion.3), channel_id=1, source_target_pairs={{1,0},{2,1},{3,2},{4,3},{5,4},{6,5},{7,6},{8,7},{9,8},{10,9},{11,1... | collective-permute-start | bytes 786440 | tf_op jit(solution)/shard_map/ppermute | solution.py:31
  (15 other events, 434.3 us)
